TPU v7x, 512 devices: a whole 4x8x8 slice. The times are simulated.
512 devices in a mesh: space: 32 (over z_hi, y, core), angle: 16 (over z_lo, x).
Axes of the slice: x: 4, y: 8, z: 8 (z_hi: 2, z_lo: 4; z = z_hi * 4 + z_lo), core: 2. Of those that a mesh axis runs over, the one named last changes fastest.
Arguments:
- phase_delay: float32 [2, 1024, 2048], P(None, 'space'), may hold values from -6 to 6
- measured: float32 [16, 2, 1024, 2048], P('angle', None, 'space'), may hold values from -6 to 6
- tilts: float32 [16, 2], P('angle'), may hold values from -0.4 to 0.4
- fresnel_taps: float32 [2, 2, 33], replicated, may hold values from -0.75 to 0.75
Outputs:
- gradient: float32 [2, 1024, 2048], P(None, 'space', 'angle')
All inputs are finite; a program needn't handle non-finite values.
Results may differ from a plain program's by a relative error of at most 0.0003.
Values sent between devices are 32-bit elements; how exact they have to be, the bound alone decides.
No kernel may reach another device: no remote copies, remote signals or barrier semaphores. Data moves between devices by JAX's collectives and lax.ppermute only.
A program may use at most 64 MiB of HBM per device.

v0:
```python
import jax
import jax.numpy as jnp
from jax import lax
from jax.sharding import PartitionSpec as P

tile_width = 128
highest = lax.Precision.HIGHEST


def padded_2(block, sides, width):
    for axis, dim in sides:
        count = lax.axis_size(axis)
        forward = [(i, i + 1) for i in range(count - 1)]
        backward = [(target, source) for source, target in forward]
        low = lax.ppermute(
            lax.slice_in_dim(block, block.shape[dim] - width, None, axis=dim), axis, forward
        )
        high = lax.ppermute(lax.slice_in_dim(block, 0, width, axis=dim), axis, backward)
        block = jnp.concatenate([low, block, high], axis=dim)
    return block


def adjoint_kernel(kernel):
    return jnp.stack([kernel[0, ::-1], -kernel[1, ::-1]])


def tap_table(kernel, offsets):
    tap_count = kernel.shape[1]
    onehot = (offsets[None] == jnp.arange(tap_count, dtype=jnp.int32)[:, None, None]).astype(
        jnp.float32
    )
    return jnp.einsum("ck,kij->cij", kernel, onehot, precision=highest)


def band_blocks(kernel):
    reach = (kernel.shape[1] - 1) // 2
    source = lax.broadcasted_iota(jnp.int32, (tile_width, tile_width), 0)
    target = lax.broadcasted_iota(jnp.int32, (tile_width, tile_width), 1)
    stacked = []
    for block_shift in (-1, 0, 1):
        table = tap_table(kernel, target - source - tile_width * block_shift + reach)
        real_row = jnp.stack([table[0], table[1]], axis=1)
        imag_row = jnp.stack([-table[1], table[0]], axis=1)
        stacked.append(jnp.stack([real_row, imag_row]))
    return jnp.stack(stacked)


def row_matrix(kernel, out_rows):
    reach = (kernel.shape[1] - 1) // 2
    out_index = lax.broadcasted_iota(jnp.int32, (out_rows, out_rows + 2 * reach), 0)
    in_index = lax.broadcasted_iota(jnp.int32, (out_rows, out_rows + 2 * reach), 1)
    return tap_table(kernel, out_index + 2 * reach - in_index)


def complex_rows(padded, matrix):
    real_in = padded[..., 0, :, :]
    imag_in = padded[..., 1, :, :]
    real_out = jnp.einsum("xj,...jy->...xy", matrix[0], real_in, precision=highest) - jnp.einsum(
        "xj,...jy->...xy", matrix[1], imag_in, precision=highest
    )
    imag_out = jnp.einsum("xj,...jy->...xy", matrix[0], imag_in, precision=highest) + jnp.einsum(
        "xj,...jy->...xy", matrix[1], real_in, precision=highest
    )
    return jnp.stack([real_out, imag_out], axis=-3)


def complex_columns(wave_field, blocks):
    shape = wave_field.shape
    tile_count = shape[-1] // tile_width
    tiles = wave_field.reshape(shape[:-1] + (tile_count, tile_width))
    padding = [(0, 0)] * (tiles.ndim - 2) + [(1, 1), (0, 0)]
    tiles = jnp.pad(tiles, padding)
    total = None
    for position, block_shift in enumerate((-1, 0, 1)):
        source_tiles = tiles[..., 1 + block_shift : 1 + block_shift + tile_count, :]
        term = jnp.einsum(
            "...cxtk,ckdj->...dxtj", source_tiles, blocks[position], precision=highest
        )
        total = term if total is None else total + term
    return total.reshape(shape)


def transmit(wave_field, cosine, sine):
    real_in = wave_field[:, 0]
    imag_in = wave_field[:, 1]
    return jnp.stack([cosine * real_in - sine * imag_in, cosine * imag_in + sine * real_in], axis=1)


def release(wave_field, cosine, sine):
    real_in = wave_field[:, 0]
    imag_in = wave_field[:, 1]
    return jnp.stack([cosine * real_in + sine * imag_in, cosine * imag_in - sine * real_in], axis=1)


def incident(tilts, first_row, length, column_count):
    positions = (first_row + jnp.arange(length, dtype=jnp.int32)).astype(jnp.float32)
    columns_float = jnp.arange(column_count, dtype=jnp.float32)
    ramp = (
        tilts[:, 0, None, None] * positions[None, :, None]
        + tilts[:, 1, None, None] * columns_float[None, None, :]
    )
    return jnp.stack([jnp.cos(ramp), jnp.sin(ramp)], axis=1)


def body(phase_delay, measured, tilts, fresnel_taps):
    slice_count, strip_rows, column_count = phase_delay.shape
    reach = (fresnel_taps.shape[2] - 1) // 2
    first_row = lax.axis_index("space") * strip_rows
    column_blocks = band_blocks(fresnel_taps[1])
    column_back = band_blocks(adjoint_kernel(fresnel_taps[1]))
    cosines = jnp.cos(phase_delay)
    sines = jnp.sin(phase_delay)
    stored = []
    wave_field = incident(tilts, first_row, strip_rows, column_count)
    row_forward = row_matrix(fresnel_taps[0], strip_rows)
    for layer in range(slice_count):
        transmitted = transmit(wave_field, cosines[layer], sines[layer])
        stored.append(transmitted)
        padded = padded_2(transmitted, (("space", 2),), reach)
        wave_field = complex_columns(complex_rows(padded, row_forward), column_blocks)
    row_backward = row_matrix(adjoint_kernel(fresnel_taps[0]), strip_rows)
    backward = wave_field - measured
    terms = [None] * slice_count
    for layer in reversed(range(slice_count)):
        spread_field = complex_columns(backward, column_back)
        padded = padded_2(spread_field, (("space", 2),), reach)
        sensitivity = complex_rows(padded, row_backward)
        transmitted = stored[layer]
        terms[layer] = jnp.sum(
            transmitted[:, 0] * sensitivity[:, 1] - transmitted[:, 1] * sensitivity[:, 0], axis=0
        )
        if layer > 0:
            backward = release(sensitivity, cosines[layer], sines[layer])
    return lax.psum_scatter(jnp.stack(terms), "angle", scatter_dimension=2, tiled=True)


def solution(mesh):
    return jax.shard_map(
        body,
        mesh=mesh,
        in_specs=(P(None, "space", None), P("angle", None, "space", None), P("angle", None), P()),
        out_specs=P(None, "space", "angle"),
        check_vma=False,
    )
```

profile of v0, /device:TPU:8, one launch (start us, length us, event | category | flops | bytes accessed | tf_op | source)
XLA Modules:
  0.0 210.4 jit_solution(607793131118652631)
XLA Ops:
  6.5 2.8 %fusion.135 = (f32[2,32,2048]{2,1,0:T(8,128)S(1)}, f32[2,32,2048]{2,1,0:T(8,128)S(1)}) fusion(f32[2,32,2048]{2,1,0:T(8,128)} %param.4), kind=kLoop, calls=%fused_computation.226 | loop fusion | bytes 1572864 | tf_op jit(solution)/shard_map/cos | solution.py:111
  11.2 1.2 fusion.129
  13.1 1.9 collective-permute-start
  15.0 3.6 %collective-permute-start.1 = (f32[1,2,16,2048]{3,2,1,0:T(8,128)S(1)}, f32[1,2,16,2048]{3,2,1,0:T(8,128)}, u32[]{:S(2)}, u32[]{:S(2)}) collective-permute-start(f32[1,2,16,2048]{3,2,1,0:T(8,128)S(1)} %get-tuple-element.25), channel_id=1, source_target_pairs={{16,0},{32,16},{48,32},{64,48},{80,64},{96,80},{112,96},{128,112},... | collective-permute-start | bytes 786440 | tf_op jit(solution)/shard_map/ppermute | solution.py:18
  18.8 1.0 fusion.36
  19.7 1.0 fusion.37
  22.7 1.0 fusion.35
  25.9 1.1 pad_maximum_fusion
  32.1 1.9 collective-permute-start.2
  34.1 6.4 %collective-permute-start.3 = (f32[1,2,16,2048]{3,2,1,0:T(8,128)S(1)}, f32[1,2,16,2048]{3,2,1,0:T(8,128)}, u32[]{:S(2)}, u32[]{:S(2)}) collective-permute-start(f32[1,2,16,2048]{3,2,1,0:T(8,128)S(1)} %get-tuple-element.21), channel_id=1, source_target_pairs={{16,0},{32,16},{48,32},{64,48},{80,64},{96,80},{112,96},{128,112},... | collective-permute-start | bytes 786440 | tf_op jit(solution)/shard_map/ppermute | solution.py:18
  40.7 2.0 collective-permute-done.2
  42.7 1.4 collective-permute-done.3
  44.1 1.1 pad_maximum_fusion.1
  53.3 1.9 collective-permute-start.4
  55.2 4.1 %collective-permute-start.5 = (f32[1,2,16,2048]{3,0,2,1:T(1,128)S(1)}, f32[1,2,16,2048]{3,0,2,1:T(1,128)S(1)}, u32[]{:S(2)}, u32[]{:S(2)}) collective-permute-start(f32[1,2,16,2048]{3,0,2,1:T(1,128)S(1)} %get-tuple-element.19), channel_id=1, source_target_pairs={{16,0},{32,16},{48,32},{64,48},{80,64},{96,80},{112,96},{128,112},... | collective-permute-start | bytes 786440 | tf_op jit(solution)/shard_map/ppermute | solution.py:18
  59.7 1.5 collective-permute-done.4
  61.3 1.8 collective-permute-done.5
  68.9 1.9 collective-permute-start.6
  70.8 3.8 %collective-permute-start.7 = (f32[1,2,16,2048]{3,0,2,1:T(1,128)S(1)}, f32[1,2,16,2048]{3,0,2,1:T(1,128)S(1)}, u32[]{:S(2)}, u32[]{:S(2)}) collective-permute-start(f32[1,2,16,2048]{3,0,2,1:T(1,128)S(1)} %get-tuple-element.16), channel_id=1, source_target_pairs={{16,0},{32,16},{48,32},{64,48},{80,64},{96,80},{112,96},{128,112},... | collective-permute-start | bytes 786440 | tf_op jit(solution)/shard_map/ppermute | solution.py:18
  74.7 2.1 %collective-permute-done.6 = f32[1,2,16,2048]{3,0,2,1:T(1,128)S(1)} collective-permute-done((f32[1,2,16,2048]{3,0,2,1:T(1,128)S(1)}, f32[1,2,16,2048]{3,0,2,1:T(1,128)S(1)}, u32[]{:S(2)}, u32[]{:S(2)}) %collective-permute-start.6) | collective-permute-done | bytes 262176 | tf_op jit(solution)/shard_map/ppermute | solution.py:15
  76.8 1.8 collective-permute-done.7
  80.7 1.5 fusion.12
  82.2 1.5 fusion.11
  84.5 119.1 %reduce-scatter.2.cloned.1.call-done = f32[2,32,128]{2,1,0:T(8,128)} async-done(((f32[2,32,2048]{2,1,0:T(8,128)}), f32[2,32,128]{2,1,0:T(8,128)}) %reduce-scatter.2.cloned.1.call-update) | async-done | bytes 32784 | tf_op jit(solution)/shard_map/reduce_scatter | solution.py:134
  (105 shorter events, 29.0 us)
Async XLA Ops:
  6.5 2.8 %copy-start.2 = (f32[1,2]{1,0:T(1,128)S(1)}, f32[1,2]{1,0:T(1,128)}, u32[]{:S(2)}) copy-start(f32[1,2]{1,0:T(1,128)} %param.6) | copy-start | bytes 28
  6.5 197.1 %reduce-scatter.2.cloned.1.call-start = ((), (), s32[]{:S(2)}) async-start(), calls=%async_computation.1 | async-start | bytes 557056 | tf_op jit(solution)/shard_map/reduce_scatter | solution.py:134
  11.2 7.6 %copy-start.1 = (f32[2,2,33]{2,1,0:T(2,128)S(1)}, f32[2,2,33]{2,1,0:T(2,128)}, u32[]{:S(2)}) copy-start(f32[2,2,33]{2,1,0:T(2,128)} %param.7) | copy-start | bytes 1588
  13.1 12.8 %collective-permute-start = (f32[1,2,16,2048]{3,2,1,0:T(8,128)}, f32[1,2,16,2048]{3,2,1,0:T(8,128)}, u32[]{:S(2)}, u32[]{:S(2)}) collective-permute-start(f32[1,2,16,2048]{3,2,1,0:T(8,128)} %get-tuple-element.24), channel_id=1, source_target_pairs={{0,16},{16,32},{32,48},{48,64},{64,80},{80,96},{96,112},{112,128},... | collective-permute-start | bytes 786440 | tf_op jit(solution)/shard_map/ppermute | solution.py:15
  15.0 10.9 %collective-permute-start.1 = (f32[1,2,16,2048]{3,2,1,0:T(8,128)S(1)}, f32[1,2,16,2048]{3,2,1,0:T(8,128)}, u32[]{:S(2)}, u32[]{:S(2)}) collective-permute-start(f32[1,2,16,2048]{3,2,1,0:T(8,128)S(1)} %get-tuple-element.25), channel_id=1, source_target_pairs={{16,0},{32,16},{48,32},{64,48},{80,64},{96,80},{112,96},{128,112},... | collective-permute-start | bytes 786440 | tf_op jit(solution)/shard_map/ppermute | solution.py:18
  32.1 10.5 %collective-permute-start.2 = (f32[1,2,16,2048]{3,2,1,0:T(8,128)}, f32[1,2,16,2048]{3,2,1,0:T(8,128)}, u32[]{:S(2)}, u32[]{:S(2)}) collective-permute-start(f32[1,2,16,2048]{3,2,1,0:T(8,128)} %get-tuple-element.20), channel_id=1, source_target_pairs={{0,16},{16,32},{32,48},{48,64},{64,80},{80,96},{96,112},{112,128},... | collective-permute-start | bytes 786440 | tf_op jit(solution)/shard_map/ppermute | solution.py:15
  34.1 10.1 %collective-permute-start.3 = (f32[1,2,16,2048]{3,2,1,0:T(8,128)S(1)}, f32[1,2,16,2048]{3,2,1,0:T(8,128)}, u32[]{:S(2)}, u32[]{:S(2)}) collective-permute-start(f32[1,2,16,2048]{3,2,1,0:T(8,128)S(1)} %get-tuple-element.21), channel_id=1, source_target_pairs={{16,0},{32,16},{48,32},{64,48},{80,64},{96,80},{112,96},{128,112},... | collective-permute-start | bytes 786440 | tf_op jit(solution)/shard_map/ppermute | solution.py:18
  49.1 1.0 copy-start
  53.3 8.0 %collective-permute-start.4 = (f32[1,2,16,2048]{3,0,2,1:T(1,128)S(1)}, f32[1,2,16,2048]{3,0,2,1:T(1,128)S(1)}, u32[]{:S(2)}, u32[]{:S(2)}) collective-permute-start(f32[1,2,16,2048]{3,0,2,1:T(1,128)S(1)} %get-tuple-element.18), channel_id=1, source_target_pairs={{0,16},{16,32},{32,48},{48,64},{64,80},{80,96},{96,112},{112,128},... | collective-permute-start | bytes 786440 | tf_op jit(solution)/shard_map/ppermute | solution.py:15
  55.2 7.8 %collective-permute-start.5 = (f32[1,2,16,2048]{3,0,2,1:T(1,128)S(1)}, f32[1,2,16,2048]{3,0,2,1:T(1,128)S(1)}, u32[]{:S(2)}, u32[]{:S(2)}) collective-permute-start(f32[1,2,16,2048]{3,0,2,1:T(1,128)S(1)} %get-tuple-element.19), channel_id=1, source_target_pairs={{16,0},{32,16},{48,32},{64,48},{80,64},{96,80},{112,96},{128,112},... | collective-permute-start | bytes 786440 | tf_op jit(solution)/shard_map/ppermute | solution.py:18
  68.9 7.9 %collective-permute-start.6 = (f32[1,2,16,2048]{3,0,2,1:T(1,128)S(1)}, f32[1,2,16,2048]{3,0,2,1:T(1,128)S(1)}, u32[]{:S(2)}, u32[]{:S(2)}) collective-permute-start(f32[1,2,16,2048]{3,0,2,1:T(1,128)S(1)} %get-tuple-element.15), channel_id=1, source_target_pairs={{0,16},{16,32},{32,48},{48,64},{64,80},{80,96},{96,112},{112,128},... | collective-permute-start | bytes 786440 | tf_op jit(solution)/shard_map/ppermute | solution.py:15
  70.8 7.7 %collective-permute-start.7 = (f32[1,2,16,2048]{3,0,2,1:T(1,128)S(1)}, f32[1,2,16,2048]{3,0,2,1:T(1,128)S(1)}, u32[]{:S(2)}, u32[]{:S(2)}) collective-permute-start(f32[1,2,16,2048]{3,0,2,1:T(1,128)S(1)} %get-tuple-element.16), channel_id=1, source_target_pairs={{16,0},{32,16},{48,32},{64,48},{80,64},{96,80},{112,96},{128,112},... | collective-permute-start | bytes 786440 | tf_op jit(solution)/shard_map/ppermute | solution.py:18
Sparse Core Ops, SparseCore 0:
  84.6 118.9 reduce-scatter.1
where the time goes:
time: 211 us; the launch traced here: 210 us
  waiting for transfers between devices  130 us (62%)
  starting transfers between devices  25.6 us (12%)
  matrix products  23.4 us (11%)
  between operations  14.1 us (7%)
  other arithmetic  9.96 us (5%)
  local copies, waits for them, and re-layouts  7.62 us (4%)
    reduce_scatter x1, waiting for transfers between devices, body(): lax.psum_scatter(jnp.stack(terms), 'angle', scatter_dimension=2, tiled=True)  119 us
    ppermute x4, starting transfers between devices, padded_2(): lax.ppermute(lax.slice_in_dim(block, 0, width, axis=dim), axis, backward)  18 us
    ppermute x4, starting transfers between devices, padded_2(): lax.ppermute(lax.slice_in_dim(block, block.shape[dim] - width, None, axis...  7.66 us
    dot_general x12, matrix products, complex_columns(): jnp.einsum('...cxtk,ckdj->...dxtj', source_tiles, blocks[position], preci...  7.3 us
    dot_general x8, matrix products, tap_table(): return jnp.einsum('ck,kij->cij', kernel, onehot, precision=highest)  6.31 us
    ppermute x4, waiting for transfers between devices, padded_2(): lax.ppermute(lax.slice_in_dim(block, block.shape[dim] - width, None, axis...  5.63 us
    ppermute x4, waiting for transfers between devices, padded_2(): lax.ppermute(lax.slice_in_dim(block, 0, width, axis=dim), axis, backward)  4.95 us
  transfers between devices with their start and end apart: 9, of which 7 were waited for; matrix products, arithmetic and copies ran while one was open for 4% of the time, Pallas kernels for 0%

commit v1 on v0

--- a/solution.py
+++ b/solution.py
@@ -131,7 +131,10 @@
         )
         if layer > 0:
             backward = release(sensitivity, cosines[layer], sines[layer])
-    return lax.psum_scatter(jnp.stack(terms), "angle", scatter_dimension=2, tiled=True)
+    parts = lax.axis_size("angle")
+    blocks = jnp.stack(terms).reshape(slice_count, strip_rows, parts, column_count // parts)
+    blocks = lax.all_to_all(blocks.transpose(2, 0, 1, 3), "angle", 0, 0)
+    return jnp.sum(blocks, axis=0)
 
 
 def solution(mesh):

time: 211 us -> 132 us (0.63)
  the two profiles are of different devices: /device:TPU:8 before, /device:TPU:57 now
where the time goes in v1:
time: 132 us
  waiting for transfers between devices  48.3 us (37%)
  starting transfers between devices  25.7 us (19%)
  matrix products  23.4 us (18%)
  blocking collectives  15.8 us (12%)
  other arithmetic  9.9 us (8%)
  local copies, waits for them, and re-layouts  7.76 us (6%)
    ppermute x4, waiting for transfers between devices, padded_2(): lax.ppermute(lax.slice_in_dim(block, 0, width, axis=dim), axis, backward)  46 us
    ppermute x4, starting transfers between devices, padded_2(): lax.ppermute(lax.slice_in_dim(block, block.shape[dim] - width, None, axis...  16.4 us
    all_to_all x1, blocking collectives, body(): blocks = lax.all_to_all(blocks.transpose(2, 0, 1, 3), 'angle', 0, 0)  15.8 us
    ppermute x4, starting transfers between devices, padded_2(): lax.ppermute(lax.slice_in_dim(block, 0, width, axis=dim), axis, backward)  9.24 us
    dot_general x12, matrix products, complex_columns(): jnp.einsum('...cxtk,ckdj->...dxtj', source_tiles, blocks[position], preci...  7.3 us
    dot_general x8, matrix products, tap_table(): return jnp.einsum('ck,kij->cij', kernel, onehot, precision=highest)  6.31 us
    concatenate x4, other arithmetic, padded_2(): block = jnp.concatenate([low, block, high], axis=dim)  4.06 us
    dot_general x4, matrix products, complex_rows(): jnp.einsum('xj,...jy->...xy', matrix[1], imag_in, precision=highest)  2.96 us
  transfers between devices with their start and end apart: 8, of which 7 were waited for; matrix products, arithmetic and copies ran while one was open for 6% of the time, Pallas kernels for 0%

profile of v1, /device:TPU:57, one launch (start us, length us, event | category | flops | bytes accessed | tf_op | source)
XLA Modules:
  0.0 131.5 jit_solution(11919361675059841634)
XLA Ops:
  0.0 2.8 %fusion.136 = (f32[2,32,2048]{2,1,0:T(8,128)S(1)}, f32[2,32,2048]{2,1,0:T(8,128)S(1)}) fusion(f32[2,32,2048]{2,1,0:T(8,128)} %param.4), kind=kLoop, calls=%fused_computation.229 | loop fusion | bytes 1572864 | tf_op jit(solution)/shard_map/cos | solution.py:111
  4.8 1.2 fusion.130
  6.7 10.4 %collective-permute-start = (f32[1,2,16,2048]{3,2,1,0:T(8,128)}, f32[1,2,16,2048]{3,2,1,0:T(8,128)}, u32[]{:S(2)}, u32[]{:S(2)}) collective-permute-start(f32[1,2,16,2048]{3,2,1,0:T(8,128)} %get-tuple-element.24), channel_id=1, source_target_pairs={{0,16},{16,32},{32,48},{48,64},{64,80},{80,96},{96,112},{112,128},... | collective-permute-start | bytes 786440 | tf_op jit(solution)/shard_map/ppermute | solution.py:15
  17.1 1.9 %collective-permute-start.1 = (f32[1,2,16,2048]{3,2,1,0:T(8,128)S(1)}, f32[1,2,16,2048]{3,2,1,0:T(8,128)}, u32[]{:S(2)}, u32[]{:S(2)}) collective-permute-start(f32[1,2,16,2048]{3,2,1,0:T(8,128)S(1)} %get-tuple-element.25), channel_id=1, source_target_pairs={{16,0},{32,16},{48,32},{64,48},{80,64},{96,80},{112,96},{128,112},... | collective-permute-start | bytes 786440 | tf_op jit(solution)/shard_map/ppermute | solution.py:18
  19.1 1.0 fusion.37
  20.1 1.0 fusion.38
  23.1 1.0 fusion.36
  26.3 7.5 %collective-permute-done.1 = f32[1,2,16,2048]{3,2,1,0:T(8,128)} collective-permute-done((f32[1,2,16,2048]{3,2,1,0:T(8,128)S(1)}, f32[1,2,16,2048]{3,2,1,0:T(8,128)}, u32[]{:S(2)}, u32[]{:S(2)}) %collective-permute-start.1) | collective-permute-done | bytes 262176 | tf_op jit(solution)/shard_map/ppermute | solution.py:18
  33.8 1.1 pad_maximum_fusion
  40.0 2.2 %collective-permute-start.2 = (f32[1,2,16,2048]{3,2,1,0:T(8,128)}, f32[1,2,16,2048]{3,2,1,0:T(8,128)}, u32[]{:S(2)}, u32[]{:S(2)}) collective-permute-start(f32[1,2,16,2048]{3,2,1,0:T(8,128)} %get-tuple-element.20), channel_id=1, source_target_pairs={{0,16},{16,32},{32,48},{48,64},{64,80},{80,96},{96,112},{112,128},... | collective-permute-start | bytes 786440 | tf_op jit(solution)/shard_map/ppermute | solution.py:15
  42.2 2.3 %collective-permute-start.3 = (f32[1,2,16,2048]{3,2,1,0:T(8,128)S(1)}, f32[1,2,16,2048]{3,2,1,0:T(8,128)}, u32[]{:S(2)}, u32[]{:S(2)}) collective-permute-start(f32[1,2,16,2048]{3,2,1,0:T(8,128)S(1)} %get-tuple-element.21), channel_id=1, source_target_pairs={{16,0},{32,16},{48,32},{64,48},{80,64},{96,80},{112,96},{128,112},... | collective-permute-start | bytes 786440 | tf_op jit(solution)/shard_map/ppermute | solution.py:18
  44.8 1.0 collective-permute-done.2
  45.8 13.0 %collective-permute-done.3 = f32[1,2,16,2048]{3,2,1,0:T(8,128)} collective-permute-done((f32[1,2,16,2048]{3,2,1,0:T(8,128)S(1)}, f32[1,2,16,2048]{3,2,1,0:T(8,128)}, u32[]{:S(2)}, u32[]{:S(2)}) %collective-permute-start.3) | collective-permute-done | bytes 262176 | tf_op jit(solution)/shard_map/ppermute | solution.py:18
  58.8 1.1 pad_maximum_fusion.1
  68.0 1.9 %collective-permute-start.4 = (f32[1,2,16,2048]{3,0,2,1:T(1,128)S(1)}, f32[1,2,16,2048]{3,0,2,1:T(1,128)S(1)}, u32[]{:S(2)}, u32[]{:S(2)}) collective-permute-start(f32[1,2,16,2048]{3,0,2,1:T(1,128)S(1)} %get-tuple-element.18), channel_id=1, source_target_pairs={{0,16},{16,32},{32,48},{48,64},{64,80},{80,96},{96,112},{112,128},... | collective-permute-start | bytes 786440 | tf_op jit(solution)/shard_map/ppermute | solution.py:15
  69.9 2.6 %collective-permute-start.5 = (f32[1,2,16,2048]{3,0,2,1:T(1,128)S(1)}, f32[1,2,16,2048]{3,0,2,1:T(1,128)S(1)}, u32[]{:S(2)}, u32[]{:S(2)}) collective-permute-start(f32[1,2,16,2048]{3,0,2,1:T(1,128)S(1)} %get-tuple-element.19), channel_id=1, source_target_pairs={{16,0},{32,16},{48,32},{64,48},{80,64},{96,80},{112,96},{128,112},... | collective-permute-start | bytes 786440 | tf_op jit(solution)/shard_map/ppermute | solution.py:18
  73.2 12.9 %collective-permute-done.5 = f32[1,2,16,2048]{3,0,2,1:T(1,128)S(1)} collective-permute-done((f32[1,2,16,2048]{3,0,2,1:T(1,128)S(1)}, f32[1,2,16,2048]{3,0,2,1:T(1,128)S(1)}, u32[]{:S(2)}, u32[]{:S(2)}) %collective-permute-start.5) | collective-permute-done | bytes 262176 | tf_op jit(solution)/shard_map/ppermute | solution.py:18
  86.2 0.9 pad_maximum_fusion.2
  92.0 1.9 %collective-permute-start.6 = (f32[1,2,16,2048]{3,0,2,1:T(1,128)S(1)}, f32[1,2,16,2048]{3,0,2,1:T(1,128)S(1)}, u32[]{:S(2)}, u32[]{:S(2)}) collective-permute-start(f32[1,2,16,2048]{3,0,2,1:T(1,128)S(1)} %get-tuple-element.15), channel_id=1, source_target_pairs={{0,16},{16,32},{32,48},{48,64},{64,80},{80,96},{96,112},{112,128},... | collective-permute-start | bytes 786440 | tf_op jit(solution)/shard_map/ppermute | solution.py:15
  94.0 2.4 %collective-permute-start.7 = (f32[1,2,16,2048]{3,0,2,1:T(1,128)S(1)}, f32[1,2,16,2048]{3,0,2,1:T(1,128)S(1)}, u32[]{:S(2)}, u32[]{:S(2)}) collective-permute-start(f32[1,2,16,2048]{3,0,2,1:T(1,128)S(1)} %get-tuple-element.16), channel_id=1, source_target_pairs={{16,0},{32,16},{48,32},{64,48},{80,64},{96,80},{112,96},{128,112},... | collective-permute-start | bytes 786440 | tf_op jit(solution)/shard_map/ppermute | solution.py:18
  97.3 12.6 %collective-permute-done.7 = f32[1,2,16,2048]{3,0,2,1:T(1,128)S(1)} collective-permute-done((f32[1,2,16,2048]{3,0,2,1:T(1,128)S(1)}, f32[1,2,16,2048]{3,0,2,1:T(1,128)S(1)}, u32[]{:S(2)}, u32[]{:S(2)}) %collective-permute-start.7) | collective-permute-done | bytes 262176 | tf_op jit(solution)/shard_map/ppermute | solution.py:18
  112.0 1.5 %fusion.12 = f32[1,32,2048]{2,1,0:T(8,128)S(1)} fusion(f32[2048,32]{0,1:T(8,128)S(1)} %fusion.56, f32[32,64]{1,0:T(8,128)S(1)} %bitcast.459, f32[1,1,64,2048]{3,0,2,1:T(1,128)S(1)} %get-tuple-element.11, f32[2,32,2048]{2,1,0:T(8,128)S(1)} %get-tuple-element.27, f32[2048]{0:T(1024)S(1)} %iota_multiply_fusion, f32[32]{0:T(128)S(1)} %convert_multiply_fusion, ...), kind=kOutput, calls=%fused_computation.23 | convolution fusion | flops 50724864 | bytes 1589376 | tf_op jit(solution)/shard_map/xj,...jy->...xy/dot_general | solution.py:58
  113.5 1.5 %fusion.35 = f32[1,4,16,8,128]{4,3,2,1,0:T(8,128)S(1)} fusion(f32[1,32,2048]{2,1,0:T(8,128)S(1)} %fusion.12, f32[2048,32]{0,1:T(8,128)S(1)} %fusion.60, f32[32,64]{1,0:T(8,128)S(1)} %bitcast.460, f32[1,1,64,2048]{3,0,2,1:T(1,128)S(1)} %get-tuple-element.12, f32[2,32,2048]{2,1,0:T(8,128)S(1)} %get-tuple-element.27, f32[2048]{0:T(1024)S(1)} %iota_multiply_fusion, ...), kind=kOutput, calls=%fused_computation.58 | convolution fusion | flops 50790400 | bytes 1851520 | tf_op jit(solution)/shard_map/xj,...jy->...xy/dot_general | solution.py:61
  115.1 15.8 %all_to_all.5 = f32[16,2,32,128]{3,2,1,0:T(8,128)S(1)} all-to-all(f32[16,2,32,128]{3,2,1,0:T(8,128)S(1)} %maximum_bitcast_fusion), channel_id=1, replica_groups=mesh['space'=32,'angle'=16] {'angle'}, dimensions={0} | all-to-all | bytes 1048576 | tf_op jit(solution)/shard_map/all_to_all | solution.py:136
  (105 shorter events, 29.3 us)
Async XLA Ops:
  0.0 2.8 %copy-start.2 = (f32[1,2]{1,0:T(1,128)S(1)}, f32[1,2]{1,0:T(1,128)}, u32[]{:S(2)}) copy-start(f32[1,2]{1,0:T(1,128)} %param.6) | copy-start | bytes 28
  4.8 14.3 %copy-start.1 = (f32[2,2,33]{2,1,0:T(2,128)S(1)}, f32[2,2,33]{2,1,0:T(2,128)}, u32[]{:S(2)}) copy-start(f32[2,2,33]{2,1,0:T(2,128)} %param.7) | copy-start | bytes 1588
  6.7 19.6 %collective-permute-start = (f32[1,2,16,2048]{3,2,1,0:T(8,128)}, f32[1,2,16,2048]{3,2,1,0:T(8,128)}, u32[]{:S(2)}, u32[]{:S(2)}) collective-permute-start(f32[1,2,16,2048]{3,2,1,0:T(8,128)} %get-tuple-element.24), channel_id=1, source_target_pairs={{0,16},{16,32},{32,48},{48,64},{64,80},{80,96},{96,112},{112,128},... | collective-permute-start | bytes 786440 | tf_op jit(solution)/shard_map/ppermute | solution.py:15
  17.1 16.6 %collective-permute-start.1 = (f32[1,2,16,2048]{3,2,1,0:T(8,128)S(1)}, f32[1,2,16,2048]{3,2,1,0:T(8,128)}, u32[]{:S(2)}, u32[]{:S(2)}) collective-permute-start(f32[1,2,16,2048]{3,2,1,0:T(8,128)S(1)} %get-tuple-element.25), channel_id=1, source_target_pairs={{16,0},{32,16},{48,32},{64,48},{80,64},{96,80},{112,96},{128,112},... | collective-permute-start | bytes 786440 | tf_op jit(solution)/shard_map/ppermute | solution.py:18
  40.0 5.8 %collective-permute-start.2 = (f32[1,2,16,2048]{3,2,1,0:T(8,128)}, f32[1,2,16,2048]{3,2,1,0:T(8,128)}, u32[]{:S(2)}, u32[]{:S(2)}) collective-permute-start(f32[1,2,16,2048]{3,2,1,0:T(8,128)} %get-tuple-element.20), channel_id=1, source_target_pairs={{0,16},{16,32},{32,48},{48,64},{64,80},{80,96},{96,112},{112,128},... | collective-permute-start | bytes 786440 | tf_op jit(solution)/shard_map/ppermute | solution.py:15
  42.2 16.6 %collective-permute-start.3 = (f32[1,2,16,2048]{3,2,1,0:T(8,128)S(1)}, f32[1,2,16,2048]{3,2,1,0:T(8,128)}, u32[]{:S(2)}, u32[]{:S(2)}) collective-permute-start(f32[1,2,16,2048]{3,2,1,0:T(8,128)S(1)} %get-tuple-element.21), channel_id=1, source_target_pairs={{16,0},{32,16},{48,32},{64,48},{80,64},{96,80},{112,96},{128,112},... | collective-permute-start | bytes 786440 | tf_op jit(solution)/shard_map/ppermute | solution.py:18
  63.8 1.0 copy-start
  68.0 5.2 %collective-permute-start.4 = (f32[1,2,16,2048]{3,0,2,1:T(1,128)S(1)}, f32[1,2,16,2048]{3,0,2,1:T(1,128)S(1)}, u32[]{:S(2)}, u32[]{:S(2)}) collective-permute-start(f32[1,2,16,2048]{3,0,2,1:T(1,128)S(1)} %get-tuple-element.18), channel_id=1, source_target_pairs={{0,16},{16,32},{32,48},{48,64},{64,80},{80,96},{96,112},{112,128},... | collective-permute-start | bytes 786440 | tf_op jit(solution)/shard_map/ppermute | solution.py:15
  69.9 16.2 %collective-permute-start.5 = (f32[1,2,16,2048]{3,0,2,1:T(1,128)S(1)}, f32[1,2,16,2048]{3,0,2,1:T(1,128)S(1)}, u32[]{:S(2)}, u32[]{:S(2)}) collective-permute-start(f32[1,2,16,2048]{3,0,2,1:T(1,128)S(1)} %get-tuple-element.19), channel_id=1, source_target_pairs={{16,0},{32,16},{48,32},{64,48},{80,64},{96,80},{112,96},{128,112},... | collective-permute-start | bytes 786440 | tf_op jit(solution)/shard_map/ppermute | solution.py:18
  92.0 5.2 %collective-permute-start.6 = (f32[1,2,16,2048]{3,0,2,1:T(1,128)S(1)}, f32[1,2,16,2048]{3,0,2,1:T(1,128)S(1)}, u32[]{:S(2)}, u32[]{:S(2)}) collective-permute-start(f32[1,2,16,2048]{3,0,2,1:T(1,128)S(1)} %get-tuple-element.15), channel_id=1, source_target_pairs={{0,16},{16,32},{32,48},{48,64},{64,80},{80,96},{96,112},{112,128},... | collective-permute-start | bytes 786440 | tf_op jit(solution)/shard_map/ppermute | solution.py:15
  94.0 15.9 %collective-permute-start.7 = (f32[1,2,16,2048]{3,0,2,1:T(1,128)S(1)}, f32[1,2,16,2048]{3,0,2,1:T(1,128)S(1)}, u32[]{:S(2)}, u32[]{:S(2)}) collective-permute-start(f32[1,2,16,2048]{3,0,2,1:T(1,128)S(1)} %get-tuple-element.16), channel_id=1, source_target_pairs={{16,0},{32,16},{48,32},{64,48},{80,64},{96,80},{112,96},{128,112},... | collective-permute-start | bytes 786440 | tf_op jit(solution)/shard_map/ppermute | solution.py:18

commit v2 on v0

v2 whole, which is shorter than its diff:
```python
import functools

import jax
import jax.numpy as jnp
from jax import lax
from jax.experimental import pallas as pl
from jax.experimental.pallas import tpu as pltpu
from jax.sharding import PartitionSpec as P

TILE = 128
REACH = 16
TAPS = 2 * REACH + 1
ROWS = 32
WIDE = ROWS + 2 * REACH
WIDEST = ROWS + 4 * REACH
F32 = jnp.float32
BF16 = jnp.bfloat16
VMEM_LIMIT = 48 * 1024 * 1024


def split(x):
    high = x.astype(BF16)
    return high, (x - high.astype(F32)).astype(BF16)


def matmul(a, b):
    return jnp.dot(a, b, preferred_element_type=F32)


def tap_matrices(taps_ref, rows1_ref, rows2_ref, band_ref):
    lane = lax.broadcasted_iota(jnp.int32, (8, 256), 1)

    def laid(direction, part, start, step):
        out = jnp.zeros((8, 256), F32)
        for tap in range(TAPS):
            out = jnp.where(lane == start + step * tap, taps_ref[direction, part, tap], out)
        return out

    def toeplitz(vector, rows):
        full = jnp.broadcast_to(vector[:1], (rows, 256))
        return pltpu.roll(full, 0, 1, stride=1, stride_axis=0)

    def put(ref, index, value):
        high, low = split(value)
        ref[index, 0] = high
        ref[index, 1] = low

    for index, sign in ((0, 1.0), (1, -1.0)):
        for ref, out_rows, in_rows in ((rows1_ref, WIDE, WIDEST), (rows2_ref, ROWS, WIDE)):
            halves = []
            for offset in (0, in_rows):
                start, step = (offset + TAPS - 1, -1) if index == 0 else (offset, 1)
                halves.append((laid(0, 0, start, step), laid(0, 1, start, step) * sign))
            top = toeplitz(halves[0][0] - halves[1][1], out_rows)
            bottom = toeplitz(halves[0][1] + halves[1][0], out_rows)
            put(ref, index, jnp.concatenate([top, bottom], axis=0)[:, : 2 * in_rows])
        first = 256 - TILE // 2 - REACH
        start, step = (first, 1) if index == 0 else (first + TAPS - 1, -1)
        real = toeplitz(laid(1, 0, start, step), 256)[:, :TILE]
        imag = toeplitz(laid(1, 1, start, step) * sign, 256)[:, :TILE]
        put(
            band_ref,
            index,
            jnp.concatenate(
                [
                    jnp.concatenate([real, imag], axis=1),
                    jnp.concatenate([-imag, real], axis=1),
                ],
                axis=0,
            ),
        )


def row_pass(real, imag, matrix_ref, index):
    high, low = split(jnp.concatenate([real, imag], axis=0))
    matrix_high = matrix_ref[index, 0]
    both = jnp.concatenate([matrix_high, matrix_ref[index, 1]], axis=0)
    count = matrix_high.shape[0]
    product = matmul(both, high)
    total = product[:count] + (product[count:] + matmul(matrix_high, low))
    return total[: count // 2], total[count // 2 :]


def column_pass(real, imag, band_ref, index, tiles, first):
    rows = real.shape[0]
    have = real.shape[1] // TILE
    blank = jnp.zeros((rows, TILE), BF16)
    parts = [split(real), split(imag)]

    def stacked(level):
        def tile(part, j):
            if 0 <= j < have:
                return parts[part][level][:, j * TILE : (j + 1) * TILE]
            return blank

        return jnp.concatenate(
            [
                jnp.concatenate(
                    [tile(0, first + j), tile(0, first + j + 1), tile(1, first + j), tile(1, first + j + 1)],
                    axis=1,
                )
                for j in range(tiles)
            ],
            axis=0,
        )

    high, low = stacked(0), stacked(1)
    band_high = band_ref[index, 0]
    out = matmul(high, band_high) + (matmul(low, band_high) + matmul(high, band_ref[index, 1]))
    pieces = [out[j * rows : (j + 1) * rows] for j in range(tiles)]
    return (
        jnp.concatenate([p[:, :TILE] for p in pieces], axis=1),
        jnp.concatenate([p[:, TILE:] for p in pieces], axis=1),
    )


def neighbours(even, across, beside):
    return jnp.where(even, across, beside), jnp.where(even, beside, across)


def forward(
    where_ref, tilts_ref, own_ref, across_ref, beside_ref, measured_ref, rows1_ref, rows2_ref, band_ref,
    spread_ref, wave0_ref, wave1_ref, turn1_ref, *, total_rows, total_columns,
):
    first_row = where_ref[0]
    even = where_ref[1] == 0
    below, above = neighbours(even, across_ref[...], beside_ref[...])
    width = own_ref.shape[2]
    tiles = width // TILE

    def row_numbers(count, start):
        return first_row - start + lax.broadcasted_iota(jnp.int32, (count, 1), 0)

    def turn(phase, start):
        row = row_numbers(phase.shape[0], start)
        inside = (row >= 0) & (row < total_rows)
        return jnp.where(inside, jnp.cos(phase), 0.0), jnp.where(inside, jnp.sin(phase), 0.0)

    cos0, sin0 = turn(jnp.concatenate([below[:ROWS], own_ref[0], above[:ROWS]], axis=0), 2 * REACH)
    phase1 = jnp.concatenate([below[ROWS:], own_ref[1], above[ROWS:]], axis=0)
    cos1, sin1 = turn(phase1, REACH)
    half = jnp.zeros((WIDE, TILE // 2), F32)
    cos1 = jnp.concatenate([half, cos1, half], axis=1)
    sin1 = jnp.concatenate([half, sin1, half], axis=1)
    turn1_ref[0] = cos1
    turn1_ref[1] = sin1
    row = row_numbers(WIDEST, 2 * REACH).astype(F32)
    column = lax.broadcasted_iota(jnp.int32, (1, width), 1).astype(F32)
    for angle in range(measured_ref.shape[0]):
        along, over = tilts_ref[angle, 0] * row, tilts_ref[angle, 1] * column
        cos_r, sin_r, cos_c, sin_c = jnp.cos(along), jnp.sin(along), jnp.cos(over), jnp.sin(over)
        left_r, left_i = cos0 * cos_r - sin0 * sin_r, sin0 * cos_r + cos0 * sin_r
        real, imag = left_r * cos_c - left_i * sin_c, left_r * sin_c + left_i * cos_c
        wave0_ref[angle, 0] = real[2 * REACH : 2 * REACH + ROWS]
        wave0_ref[angle, 1] = imag[2 * REACH : 2 * REACH + ROWS]
        real, imag = row_pass(real, imag, rows1_ref, 0)
        real, imag = column_pass(real, imag, band_ref, 0, tiles + 1, -1)
        real, imag = cos1 * real - sin1 * imag, cos1 * imag + sin1 * real
        wave1_ref[angle, 0] = real[REACH : REACH + ROWS]
        wave1_ref[angle, 1] = imag[REACH : REACH + ROWS]
        real, imag = row_pass(real, imag, rows2_ref, 0)
        real, imag = column_pass(real, imag, band_ref, 0, tiles, 0)
        real, imag = real - measured_ref[angle, 0], imag - measured_ref[angle, 1]
        real, imag = column_pass(real, imag, band_ref, 1, tiles + 1, -1)
        spread_ref[angle, 0] = real
        spread_ref[angle, 1] = imag


def backward(
    where_ref, own_ref, across_ref, beside_ref, wave0_ref, wave1_ref, turn1_ref, rows1_ref, rows2_ref, band_ref,
    out_ref,
):
    even = where_ref[1] == 0
    tiles = wave0_ref.shape[3] // TILE
    for angle in range(own_ref.shape[0]):
        window = []
        for part in range(2):
            below, above = neighbours(even, across_ref[angle, part], beside_ref[angle, part])
            window.append(jnp.concatenate([below, own_ref[angle, part], above], axis=0))
        real, imag = row_pass(window[0], window[1], rows1_ref, 1)
        keep = slice(REACH, REACH + ROWS)
        term1 = wave1_ref[angle, 0] * imag[keep] - wave1_ref[angle, 1] * real[keep]
        cos1, sin1 = turn1_ref[0], turn1_ref[1]
        real, imag = cos1 * real + sin1 * imag, cos1 * imag - sin1 * real
        real, imag = column_pass(real, imag, band_ref, 1, tiles, 0)
        real, imag = row_pass(real, imag, rows2_ref, 1)
        term0 = wave0_ref[angle, 0] * imag - wave0_ref[angle, 1] * real
        total0 = term0 if angle == 0 else total0 + term0
        total1 = term1 if angle == 0 else total1 + term1
    total1 = total1[:, TILE // 2 : TILE // 2 + tiles * TILE]
    for j in range(tiles):
        out_ref[j, 0] = total0[:, j * TILE : (j + 1) * TILE]
        out_ref[j, 1] = total1[:, j * TILE : (j + 1) * TILE]


def call(kernel, shapes, scalars, arrays, flops):
    moved = sum(a.size * a.dtype.itemsize for a in arrays)
    moved += sum(int(s.size) * s.dtype.itemsize for s in shapes)
    return pl.pallas_call(
        kernel,
        out_shape=shapes,
        in_specs=[pl.BlockSpec(memory_space=pltpu.SMEM)] * len(scalars)
        + [pl.BlockSpec(memory_space=pltpu.VMEM)] * len(arrays),
        out_specs=[pl.BlockSpec(memory_space=pltpu.VMEM)] * len(shapes),
        compiler_params=pltpu.CompilerParams(vmem_limit_bytes=VMEM_LIMIT),
        cost_estimate=pl.CostEstimate(flops=flops, bytes_accessed=moved, transcendentals=0),
    )(*scalars, *arrays)


def swaps(pairs):
    return pairs + [(b, a) for a, b in pairs]


def body(total_rows, phase_delay, measured, tilts, fresnel_taps):
    angles, columns = measured.shape[0], phase_delay.shape[2]
    strips = lax.axis_size("space")
    strip = lax.axis_index("space")
    parity = strip % 2
    where = jnp.stack([strip * ROWS, parity]).astype(jnp.int32)
    over_border = swaps([(i, i + 1) for i in range(1, strips - 1, 2)])
    in_chip = swaps([(i, i + 1) for i in range(0, strips, 2)])
    low, high = phase_delay[1, :REACH], phase_delay[1, ROWS - REACH :]
    to_border = jnp.concatenate([phase_delay[0], jnp.where(parity == 0, low, high)], axis=0)
    to_core = jnp.concatenate([phase_delay[0], jnp.where(parity == 0, high, low)], axis=0)
    across = lax.ppermute(to_border, "space", over_border)
    beside = lax.ppermute(to_core, "space", in_chip)
    struct = jax.ShapeDtypeStruct
    rows1, rows2, band = call(
        tap_matrices,
        [
            struct((2, 2, 2 * WIDE, 2 * WIDEST), BF16),
            struct((2, 2, 2 * ROWS, 2 * WIDE), BF16),
            struct((2, 2, 512, 256), BF16),
        ],
        [fresnel_taps],
        [],
        10_000_000,
    )
    spread, wave0, wave1, turn1 = call(
        functools.partial(forward, total_rows=total_rows, total_columns=columns),
        [
            struct((angles, 2, ROWS, columns + TILE), F32),
            struct((angles, 2, ROWS, columns), F32),
            struct((angles, 2, ROWS, columns + TILE), F32),
            struct((2, WIDE, columns + TILE), F32),
        ],
        [where, tilts],
        [phase_delay, across, beside, measured, rows1, rows2, band],
        4_000_000_000,
    )
    across = lax.ppermute(spread, "space", over_border)
    beside = lax.ppermute(spread, "space", in_chip)
    (tiles,) = call(
        backward,
        [struct((columns // TILE, 2, ROWS, TILE), F32)],
        [where],
        [spread, across, beside, wave0, wave1, turn1, rows1, rows2, band],
        3_000_000_000,
    )
    return jnp.sum(lax.all_to_all(tiles, "angle", 0, 0), axis=0)


def solution(mesh):
    def step(phase_delay, measured, tilts, fresnel_taps):
        return jax.shard_map(
            functools.partial(body, phase_delay.shape[1]),
            mesh=mesh,
            in_specs=(P(None, "space", None), P("angle", None, "space", None), P("angle", None), P()),
            out_specs=P(None, "space", "angle"),
            check_vma=False,
        )(phase_delay, measured, tilts, fresnel_taps)

    return step
```

time: 211 us -> 80 us (0.38)
  the two profiles are of different devices: /device:TPU:8 before, /device:TPU:57 now
where the time goes in v2:
time: 80 us; the launch traced here: 79 us
  starting transfers between devices  25.3 us (32%)
  waiting for transfers between devices  20.4 us (25%)
  blocking collectives  16.9 us (21%)
  Pallas kernels  13.5 us (17%)
  other arithmetic  1.78 us (2%)
  local copies, waits for them, and re-layouts  1.07 us (1%)
    all_to_all x1, blocking collectives, body(): return jnp.sum(lax.all_to_all(tiles, 'angle', 0, 0), axis=0)  16.9 us
    pallas_call x3, Pallas kernels, call(): pl.pallas_call(kernel, out_shape=shapes, in_specs=[pl.BlockSpec(memory_sp...  13.5 us
    ppermute x1, waiting for transfers between devices, body(): across = lax.ppermute(spread, 'space', over_border)  13.2 us
    ppermute x1, starting transfers between devices, body(): across = lax.ppermute(spread, 'space', over_border)  11.1 us
    ppermute x1, starting transfers between devices, body(): across = lax.ppermute(to_border, 'space', over_border)  9.74 us
    ppermute x1, waiting for transfers between devices, body(): across = lax.ppermute(to_border, 'space', over_border)  7.14 us
    ppermute x1, starting transfers between devices, body(): beside = lax.ppermute(to_core, 'space', in_chip)  2.58 us
    ppermute x1, starting transfers between devices, body(): beside = lax.ppermute(spread, 'space', in_chip)  1.92 us
  transfers between devices with their start and end apart: 4, of which 2 were waited for; matrix products, arithmetic and copies ran while one was open for 0% of the time, Pallas kernels for 1%

profile of v2, /device:TPU:57, one launch (start us, length us, event | category | flops | bytes accessed | tf_op | source)
XLA Modules:
  0.0 79.0 jit_solution(9430586183785232427)
XLA Ops:
  0.0 0.0 copy-start.2
  0.0 0.0 copy-start
  0.0 0.0 copy-start.3
  0.0 1.1 %slice_bitcast_fusion = f32[32,2048]{1,0:T(8,128)S(1)} fusion(f32[2,32,2048]{2,1,0:T(8,128)} %own_ref.1), kind=kLoop, calls=%fused_computation.2 | loop fusion | bytes 524288 | tf_op jit(solution)/shard_map/squeeze | solution.py:223
  1.1 1.0 %select_bitcast_fusion = (f32[16,2048]{1,0:T(8,128)S(1)}, f32[16,2048]{1,0:T(8,128)S(1)}) fusion(f32[2,32,2048]{2,1,0:T(8,128)} %own_ref.1, pred[]{:T(512)S(6)} %eq.6), kind=kLoop, calls=%fused_computation.3 | loop fusion | flops 65536 | bytes 524289 | tf_op jit(solution)/shard_map/jit(_where)/select_n | solution.py:224
  2.1 0.1 pad_maximum_fusion
  2.2 2.6 %collective-permute-start.1 = (f32[48,2048]{1,0:T(8,128)S(1)}, f32[48,2048]{1,0:T(8,128)S(1)}, u32[]{:S(2)}, u32[]{:S(2)}) collective-permute-start(f32[48,2048]{1,0:T(8,128)S(1)} %get-tuple-element.21), channel_id=1, source_target_pairs={{0,16},{32,48},{64,80},{96,112},{128,144},{160,176},{192,208},{224... | collective-permute-start | bytes 1179656 | tf_op jit(solution)/shard_map/ppermute | solution.py:226
  4.7 9.7 %collective-permute-start = (f32[48,2048]{1,0:T(8,128)S(1)}, f32[48,2048]{1,0:T(8,128)S(1)}, u32[]{:S(2)}, u32[]{:S(2)}) collective-permute-start(f32[48,2048]{1,0:T(8,128)S(1)} %get-tuple-element.22), channel_id=1, source_target_pairs={{16,32},{48,64},{80,96},{112,128},{144,160},{176,192},{208,224},{2... | collective-permute-start | bytes 1179656 | tf_op jit(solution)/shard_map/ppermute | solution.py:225
  14.5 0.0 copy-done.2
  14.5 1.0 %shard_map.46 = (bf16[2,2,128,192]{3,2,1,0:T(8,128)(2,1)S(1)}, bf16[2,2,64,128]{3,2,1,0:T(8,128)(2,1)S(1)}, bf16[2,2,512,256]{3,2,1,0:T(8,128)(2,1)S(1)}) custom-call(f32[2,2,33]{2,1,0:T(2,128)S(1)} %copy-done.2), custom_call_target="tpu_custom_call" | custom-call | flops 10000000 | bytes 1310720 | tf_op jit(solution)/shard_map/pallas_call | solution.py:199
  15.5 0.1 pad_add_fusion.where_ref
  15.6 0.0 collective-permute-done.1.beside_ref
  15.6 7.1 %collective-permute-done.across_ref = f32[48,2048]{1,0:T(8,128)S(1)} collective-permute-done((f32[48,2048]{1,0:T(8,128)S(1)}, f32[48,2048]{1,0:T(8,128)S(1)}, u32[]{:S(2)}, u32[]{:S(2)}) %collective-permute-start) | collective-permute-done | bytes 393248 | tf_op jit(solution)/shard_map/ppermute | solution.py:225
  22.7 0.0 copy-done
  22.7 0.0 copy-done.1
  22.7 0.0 copy-done.3
  22.7 9.8 %shard_map.47 = (f32[1,2,32,2176]{3,2,1,0:T(8,128)S(1)}, f32[1,2,32,2048]{3,2,1,0:T(8,128)S(1)}, f32[1,2,32,2176]{3,2,1,0:T(8,128)S(1)}, f32[2,64,2176]{2,1,0:T(8,128)S(1)}) custom-call(s32[2]{0:T(128)S(1)} %pad_add_fusion.where_ref, f32[1,2]{1,0:T(1,128)S(1)} %copy-done.3, f32[2,32,2048]{2,1,0:T(8,128)S(1)} %copy-done, ...), custom_call_target="tpu_custom_call" | custom-call | flops 4000000000 | bytes 5898240 | tf_op jit(solution)/shard_map/pallas_call | solution.py:199
  32.5 1.9 %collective-permute-start.3 = (f32[1,2,32,2176]{3,2,1,0:T(8,128)S(1)}, f32[1,2,32,2176]{3,2,1,0:T(8,128)S(1)}, u32[]{:S(2)}, u32[]{:S(2)}) collective-permute-start(f32[1,2,32,2176]{3,2,1,0:T(8,128)S(1)} %get-tuple-element.15.own_ref), channel_id=1, source_target_pairs={{0,16},{32,48},{64,80},{96,112},{128,144},{160,176},{192,208},{224... | collective-permute-start | bytes 1671176 | tf_op jit(solution)/shard_map/ppermute | solution.py:252
  34.4 11.1 %collective-permute-start.2 = (f32[1,2,32,2176]{3,2,1,0:T(8,128)S(1)}, f32[1,2,32,2176]{3,2,1,0:T(8,128)S(1)}, u32[]{:S(2)}, u32[]{:S(2)}) collective-permute-start(f32[1,2,32,2176]{3,2,1,0:T(8,128)S(1)} %get-tuple-element.15.own_ref), channel_id=1, source_target_pairs={{16,32},{48,64},{80,96},{112,128},{144,160},{176,192},{208,224},{2... | collective-permute-start | bytes 1671176 | tf_op jit(solution)/shard_map/ppermute | solution.py:251
  45.5 0.0 collective-permute-done.3.beside_ref
  45.5 13.2 %collective-permute-done.2.across_ref = f32[1,2,32,2176]{3,2,1,0:T(8,128)S(1)} collective-permute-done((f32[1,2,32,2176]{3,2,1,0:T(8,128)S(1)}, f32[1,2,32,2176]{3,2,1,0:T(8,128)S(1)}, u32[]{:S(2)}, u32[]{:S(2)}) %collective-permute-start.2) | collective-permute-done | bytes 557088 | tf_op jit(solution)/shard_map/ppermute | solution.py:251
  58.8 2.7 %shard_map.48 = f32[16,2,32,128]{3,2,1,0:T(8,128)S(1)} custom-call(s32[2]{0:T(128)S(1)} %pad_add_fusion.where_ref, f32[1,2,32,2176]{3,2,1,0:T(8,128)S(1)} %get-tuple-element.15.own_ref, f32[1,2,32,2176]{3,2,1,0:T(8,128)S(1)} %collective-permute-done.2.across_ref, f32[1,2,32,2176]{3,2,1,0:T(8,128)S(1)} %collective-permute-done.3.beside_ref, ...), custom_call_target="tpu_custom_call" | custom-call | flops 3000000000 | bytes 5701632 | tf_op jit(solution)/shard_map/pallas_call | solution.py:199
  61.5 16.9 %all_to_all.5 = f32[16,2,32,128]{3,2,1,0:T(8,128)S(1)} all-to-all(f32[16,2,32,128]{3,2,1,0:T(8,128)S(1)} %shard_map.48), channel_id=1, replica_groups=mesh['space'=32,'angle'=16] {'angle'}, dimensions={0} | all-to-all | bytes 1048576 | tf_op jit(solution)/shard_map/all_to_all | solution.py:260
  78.4 0.6 reduce_sum.9
  (1 shorter events, 0.0 us)
Async XLA Ops:
  0.0 14.5 %copy-start.2 = (f32[2,2,33]{2,1,0:T(2,128)S(1)}, f32[2,2,33]{2,1,0:T(2,128)}, u32[]{:S(2)}) copy-start(f32[2,2,33]{2,1,0:T(2,128)} %taps_ref.1) | copy-start | bytes 1588
  0.0 22.7 %copy-start = (f32[2,32,2048]{2,1,0:T(8,128)S(1)}, f32[2,32,2048]{2,1,0:T(8,128)}, u32[]{:S(2)}) copy-start(f32[2,32,2048]{2,1,0:T(8,128)} %own_ref.1) | copy-start | bytes 1572868
  0.0 22.7 %copy-start.1 = (f32[1,2,32,2048]{3,2,1,0:T(8,128)S(1)}, f32[1,2,32,2048]{3,2,1,0:T(8,128)}, u32[]{:S(2)}) copy-start(f32[1,2,32,2048]{3,2,1,0:T(8,128)} %measured_ref.1) | copy-start | bytes 1572868
  0.0 22.7 %copy-start.3 = (f32[1,2]{1,0:T(1,128)S(1)}, f32[1,2]{1,0:T(1,128)}, u32[]{:S(2)}) copy-start(f32[1,2]{1,0:T(1,128)} %tilts_ref.1) | copy-start | bytes 28
  2.2 13.4 %collective-permute-start.1 = (f32[48,2048]{1,0:T(8,128)S(1)}, f32[48,2048]{1,0:T(8,128)S(1)}, u32[]{:S(2)}, u32[]{:S(2)}) collective-permute-start(f32[48,2048]{1,0:T(8,128)S(1)} %get-tuple-element.21), channel_id=1, source_target_pairs={{0,16},{32,48},{64,80},{96,112},{128,144},{160,176},{192,208},{224... | collective-permute-start | bytes 1179656 | tf_op jit(solution)/shard_map/ppermute | solution.py:226
  4.7 18.0 %collective-permute-start = (f32[48,2048]{1,0:T(8,128)S(1)}, f32[48,2048]{1,0:T(8,128)S(1)}, u32[]{:S(2)}, u32[]{:S(2)}) collective-permute-start(f32[48,2048]{1,0:T(8,128)S(1)} %get-tuple-element.22), channel_id=1, source_target_pairs={{16,32},{48,64},{80,96},{112,128},{144,160},{176,192},{208,224},{2... | collective-permute-start | bytes 1179656 | tf_op jit(solution)/shard_map/ppermute | solution.py:225
  32.5 13.0 %collective-permute-start.3 = (f32[1,2,32,2176]{3,2,1,0:T(8,128)S(1)}, f32[1,2,32,2176]{3,2,1,0:T(8,128)S(1)}, u32[]{:S(2)}, u32[]{:S(2)}) collective-permute-start(f32[1,2,32,2176]{3,2,1,0:T(8,128)S(1)} %get-tuple-element.15.own_ref), channel_id=1, source_target_pairs={{0,16},{32,48},{64,80},{96,112},{128,144},{160,176},{192,208},{224... | collective-permute-start | bytes 1671176 | tf_op jit(solution)/shard_map/ppermute | solution.py:252
  34.4 24.3 %collective-permute-start.2 = (f32[1,2,32,2176]{3,2,1,0:T(8,128)S(1)}, f32[1,2,32,2176]{3,2,1,0:T(8,128)S(1)}, u32[]{:S(2)}, u32[]{:S(2)}) collective-permute-start(f32[1,2,32,2176]{3,2,1,0:T(8,128)S(1)} %get-tuple-element.15.own_ref), channel_id=1, source_target_pairs={{16,32},{48,64},{80,96},{112,128},{144,160},{176,192},{208,224},{2... | collective-permute-start | bytes 1671176 | tf_op jit(solution)/shard_map/ppermute | solution.py:251

commit v3 on v2

--- a/solution.py
+++ b/solution.py
@@ -21,6 +21,25 @@
 def split(x):
     high = x.astype(BF16)
     return high, (x - high.astype(F32)).astype(BF16)
+
+
+def cos_sin(x):
+    turns = jnp.round(x * 0.6366197723675814)
+    rest = ((x - turns * 1.5703125) - turns * 4.837512969970703125e-4) - turns * 7.54978995489188216e-8
+    square = rest * rest
+    sine = rest + rest * square * (
+        -1.6666654611e-1 + square * (8.3321608736e-3 + square * -1.9515295891e-4)
+    )
+    cosine = (1.0 - 0.5 * square) + square * square * (
+        4.166664568298827e-2 + square * (-1.388731625493765e-3 + square * 2.443315711809948e-5)
+    )
+    quarter = turns.astype(jnp.int32)
+    odd = (quarter & 1) == 1
+    cos_part, sin_part = jnp.where(odd, sine, cosine), jnp.where(odd, cosine, sine)
+    return (
+        jnp.where(((quarter + 1) & 2) == 2, -cos_part, cos_part),
+        jnp.where((quarter & 2) == 2, -sin_part, sin_part),
+    )
 
 
 def matmul(a, b):
@@ -118,37 +137,59 @@
     return jnp.where(even, across, beside), jnp.where(even, beside, across)
 
 
+def pack(where_ref, phase_ref, border_ref, core_ref):
+    even = where_ref[1] == 0
+    low, high = phase_ref[1, :REACH], phase_ref[1, ROWS - REACH :]
+    for ref, nearest in ((border_ref, jnp.where(even, low, high)), (core_ref, jnp.where(even, high, low))):
+        ref[:ROWS] = phase_ref[0]
+        ref[ROWS:] = nearest
+
+
+def half_tile(x):
+    blank = jnp.zeros((x.shape[0], TILE // 2), x.dtype)
+    return jnp.concatenate([blank, x, blank], axis=1)
+
+
+def prepare(
+    where_ref, tilts_ref, taps_ref, phase_ref,
+    turn0_ref, turn1_ref, along_ref, over_ref, rows1_ref, rows2_ref, band_ref,
+):
+    tap_matrices(taps_ref, rows1_ref, rows2_ref, band_ref)
+    turn0_ref[0], turn0_ref[1] = cos_sin(phase_ref[0])
+    cosine, sine = cos_sin(phase_ref[1])
+    turn1_ref[0], turn1_ref[1] = half_tile(cosine), half_tile(sine)
+    row = (where_ref[0] - 2 * REACH + lax.broadcasted_iota(jnp.int32, (WIDEST, TILE), 0)).astype(F32)
+    column = lax.broadcasted_iota(jnp.int32, (8, phase_ref.shape[2]), 1).astype(F32)
+    for angle in range(along_ref.shape[0]):
+        along_ref[angle, 0], along_ref[angle, 1] = cos_sin(tilts_ref[angle, 0] * row)
+        over_ref[angle, 0], over_ref[angle, 1] = cos_sin(tilts_ref[angle, 1] * column)
+
+
 def forward(
-    where_ref, tilts_ref, own_ref, across_ref, beside_ref, measured_ref, rows1_ref, rows2_ref, band_ref,
-    spread_ref, wave0_ref, wave1_ref, turn1_ref, *, total_rows, total_columns,
+    where_ref, across_ref, beside_ref, own0_ref, own1_ref, along_ref, over_ref, measured_ref,
+    rows1_ref, rows2_ref, band_ref, spread_ref, wave0_ref, wave1_ref, turn1_ref, *, total_rows,
 ):
     first_row = where_ref[0]
     even = where_ref[1] == 0
     below, above = neighbours(even, across_ref[...], beside_ref[...])
-    width = own_ref.shape[2]
-    tiles = width // TILE
-
-    def row_numbers(count, start):
-        return first_row - start + lax.broadcasted_iota(jnp.int32, (count, 1), 0)
-
-    def turn(phase, start):
-        row = row_numbers(phase.shape[0], start)
-        inside = (row >= 0) & (row < total_rows)
-        return jnp.where(inside, jnp.cos(phase), 0.0), jnp.where(inside, jnp.sin(phase), 0.0)
-
-    cos0, sin0 = turn(jnp.concatenate([below[:ROWS], own_ref[0], above[:ROWS]], axis=0), 2 * REACH)
-    phase1 = jnp.concatenate([below[ROWS:], own_ref[1], above[ROWS:]], axis=0)
-    cos1, sin1 = turn(phase1, REACH)
-    half = jnp.zeros((WIDE, TILE // 2), F32)
-    cos1 = jnp.concatenate([half, cos1, half], axis=1)
-    sin1 = jnp.concatenate([half, sin1, half], axis=1)
+    tiles = own0_ref.shape[2] // TILE
+    below_there, above_there = first_row > 0, first_row + ROWS < total_rows
+
+    def turn(phase, there):
+        cosine, sine = cos_sin(phase)
+        return jnp.where(there, cosine, 0.0), jnp.where(there, sine, 0.0)
+
+    cos_b, sin_b = turn(below, below_there)
+    cos_a, sin_a = turn(above, above_there)
+    cos0 = jnp.concatenate([cos_b[:ROWS], own0_ref[0], cos_a[:ROWS]], axis=0)
+    sin0 = jnp.concatenate([sin_b[:ROWS], own0_ref[1], sin_a[:ROWS]], axis=0)
+    cos1 = jnp.concatenate([half_tile(cos_b[ROWS:]), own1_ref[0], half_tile(cos_a[ROWS:])], axis=0)
+    sin1 = jnp.concatenate([half_tile(sin_b[ROWS:]), own1_ref[1], half_tile(sin_a[ROWS:])], axis=0)
     turn1_ref[0] = cos1
     turn1_ref[1] = sin1
-    row = row_numbers(WIDEST, 2 * REACH).astype(F32)
-    column = lax.broadcasted_iota(jnp.int32, (1, width), 1).astype(F32)
     for angle in range(measured_ref.shape[0]):
-        along, over = tilts_ref[angle, 0] * row, tilts_ref[angle, 1] * column
-        cos_r, sin_r, cos_c, sin_c = jnp.cos(along), jnp.sin(along), jnp.cos(over), jnp.sin(over)
+        cos_r, sin_r = along_ref[angle, 0, :, :1], along_ref[angle, 1, :, :1]
+        cos_c, sin_c = over_ref[angle, 0, :1], over_ref[angle, 1, :1]
         left_r, left_i = cos0 * cos_r - sin0 * sin_r, sin0 * cos_r + cos0 * sin_r
         real, imag = left_r * cos_c - left_i * sin_c, left_r * sin_c + left_i * cos_c
         wave0_ref[angle, 0] = real[2 * REACH : 2 * REACH + ROWS]
@@ -219,37 +260,41 @@
     where = jnp.stack([strip * ROWS, parity]).astype(jnp.int32)
     over_border = swaps([(i, i + 1) for i in range(1, strips - 1, 2)])
     in_chip = swaps([(i, i + 1) for i in range(0, strips, 2)])
-    low, high = phase_delay[1, :REACH], phase_delay[1, ROWS - REACH :]
-    to_border = jnp.concatenate([phase_delay[0], jnp.where(parity == 0, low, high)], axis=0)
-    to_core = jnp.concatenate([phase_delay[0], jnp.where(parity == 0, high, low)], axis=0)
+    struct = jax.ShapeDtypeStruct
+    to_border, to_core = call(
+        pack, [struct((ROWS + REACH, columns), F32)] * 2, [where], [phase_delay], 0
+    )
+    beside = lax.ppermute(to_core, "space", in_chip)
     across = lax.ppermute(to_border, "space", over_border)
-    beside = lax.ppermute(to_core, "space", in_chip)
-    struct = jax.ShapeDtypeStruct
-    rows1, rows2, band = call(
-        tap_matrices,
+    own0, own1, along, over, rows1, rows2, band = call(
+        prepare,
         [
+            struct((2, ROWS, columns), F32),
+            struct((2, ROWS, columns + TILE), F32),
+            struct((angles, 2, WIDEST, TILE), F32),
+            struct((angles, 2, 8, columns), F32),
             struct((2, 2, 2 * WIDE, 2 * WIDEST), BF16),
             struct((2, 2, 2 * ROWS, 2 * WIDE), BF16),
             struct((2, 2, 512, 256), BF16),
         ],
-        [fresnel_taps],
-        [],
+        [where, tilts, fresnel_taps],
+        [phase_delay],
         10_000_000,
     )
     spread, wave0, wave1, turn1 = call(
-        functools.partial(forward, total_rows=total_rows, total_columns=columns),
+        functools.partial(forward, total_rows=total_rows),
         [
             struct((angles, 2, ROWS, columns + TILE), F32),
             struct((angles, 2, ROWS, columns), F32),
             struct((angles, 2, ROWS, columns + TILE), F32),
             struct((2, WIDE, columns + TILE), F32),
         ],
-        [where, tilts],
-        [phase_delay, across, beside, measured, rows1, rows2, band],
+        [where],
+        [across, beside, own0, own1, along, over, measured, rows1, rows2, band],
         4_000_000_000,
     )
+    beside = lax.ppermute(spread, "space", in_chip)
     across = lax.ppermute(spread, "space", over_border)
-    beside = lax.ppermute(spread, "space", in_chip)
     (tiles,) = call(
         backward,
         [struct((columns // TILE, 2, ROWS, TILE), F32)],

time: 80 us -> 76.8 us (0.960)
  waiting for transfers between devices: 20.4 us -> 16.8 us
  local copies, waits for them, and re-layouts: 1.07 us -> 4.66 us
  Pallas kernels: 13.5 us -> 11.9 us
  other arithmetic: 1.78 us -> 0.72 us
    unnamed x8 -> x10, local copies, waits for them, and re-layouts: 0.02 us -> 4.66 us
    ppermute x1, waiting for transfers between devices: 7.14 us -> 3.41 us  [body(): across = lax.ppermute(to_border, 'space', over_border)]
    pallas_call x3 -> x4, Pallas kernels: 13.5 us -> 11.9 us  [call(): pl.pallas_call(kernel, out_shape=shapes, in_specs=[pl.BlockSpec(memory_sp...]
    squeeze x1 -> x0, local copies, waits for them, and re-layouts: 1.06 us -> none  [body(): phase_delay[0]]
    select_n x1 -> x0, other arithmetic: 0.99 us -> none  [body(): jnp.where(parity == 0, high, low)]
  transfers between devices with their start and end apart: 4 -> 4, of which waited for: 2 -> 2; matrix products, arithmetic and copies ran while one was open for 0% -> 0% of each run, Pallas kernels for 1% -> 3%
where the time goes in v3:
time: 76.8 us; the launch traced here: 75.8 us
  starting transfers between devices  24.8 us (32%)
  blocking collectives  16.9 us (22%)
  waiting for transfers between devices  16.8 us (22%)
  Pallas kernels  11.9 us (15%)
  local copies, waits for them, and re-layouts  4.66 us (6%)
    all_to_all x1, blocking collectives, body(): return jnp.sum(lax.all_to_all(tiles, 'angle', 0, 0), axis=0)  16.9 us
    ppermute x1, waiting for transfers between devices, body(): across = lax.ppermute(spread, 'space', over_border)  13.4 us
    pallas_call x4, Pallas kernels, call(): pl.pallas_call(kernel, out_shape=shapes, in_specs=[pl.BlockSpec(memory_sp...  11.9 us
    ppermute x1, starting transfers between devices, body(): across = lax.ppermute(spread, 'space', over_border)  10.6 us
    ppermute x1, starting transfers between devices, body(): across = lax.ppermute(to_border, 'space', over_border)  10.4 us
    unnamed x10, local copies, waits for them, and re-layouts  4.66 us
    ppermute x1, waiting for transfers between devices, body(): across = lax.ppermute(to_border, 'space', over_border)  3.41 us
    ppermute x1, starting transfers between devices, body(): beside = lax.ppermute(to_core, 'space', in_chip)  1.92 us
  transfers between devices with their start and end apart: 4, of which 2 were waited for; matrix products, arithmetic and copies ran while one was open for 0% of the time, Pallas kernels for 3%

profile of v3, /device:TPU:57, one launch (start us, length us, event | category | flops | bytes accessed | tf_op | source)
XLA Modules:
  0.0 75.8 jit_solution(17790888855436833691)
XLA Ops:
  0.0 0.1 pad_add_fusion.where_ref
  0.1 0.0 copy-start
  0.1 1.0 %copy-done = f32[2,32,2048]{2,1,0:T(8,128)S(1)} copy-done((f32[2,32,2048]{2,1,0:T(8,128)S(1)}, f32[2,32,2048]{2,1,0:T(8,128)}, u32[]{:S(2)}) %copy-start) | copy-done | bytes 524312
  1.1 0.6 shard_map.46
  1.7 10.4 %collective-permute-start = (f32[48,2048]{1,0:T(8,128)S(1)}, f32[48,2048]{1,0:T(8,128)S(1)}, u32[]{:S(2)}, u32[]{:S(2)}) collective-permute-start(f32[48,2048]{1,0:T(8,128)S(1)} %get-tuple-element.18), channel_id=1, source_target_pairs={{16,32},{48,64},{80,96},{112,128},{144,160},{176,192},{208,224},{2... | collective-permute-start | bytes 1179656 | tf_op jit(solution)/shard_map/ppermute | solution.py:268
  12.1 1.9 %collective-permute-start.1 = (f32[48,2048]{1,0:T(8,128)S(1)}, f32[48,2048]{1,0:T(8,128)S(1)}, u32[]{:S(2)}, u32[]{:S(2)}) collective-permute-start(f32[48,2048]{1,0:T(8,128)S(1)} %get-tuple-element.19), channel_id=1, source_target_pairs={{0,16},{32,48},{64,80},{96,112},{128,144},{160,176},{192,208},{224... | collective-permute-start | bytes 1179656 | tf_op jit(solution)/shard_map/ppermute | solution.py:267
  14.1 0.0 copy-start.1
  14.1 0.7 copy-done.1
  14.7 0.7 copy-done.2
  15.4 2.1 %shard_map.47 = (f32[2,32,2048]{2,1,0:T(8,128)S(1)}, f32[2,32,2176]{2,1,0:T(8,128)S(1)}, f32[1,2,96,128]{3,2,1,0:T(8,128)S(1)}, f32[1,2,8,2048]{3,2,1,0:T(8,128)...) custom-call(s32[2]{0:T(128)S(1)} %pad_add_fusion.where_ref, ...), custom_call_target="tpu_custom_call" | custom-call | flops 10000000 | bytes 3145728 | tf_op jit(solution)/shard_map/pallas_call | solution.py:240
  17.5 3.4 %collective-permute-done.across_ref = f32[48,2048]{1,0:T(8,128)S(1)} collective-permute-done((f32[48,2048]{1,0:T(8,128)S(1)}, f32[48,2048]{1,0:T(8,128)S(1)}, u32[]{:S(2)}, u32[]{:S(2)}) %collective-permute-start) | collective-permute-done | bytes 393248 | tf_op jit(solution)/shard_map/ppermute | solution.py:268
  20.9 0.0 collective-permute-done.1.beside_ref
  20.9 0.0 copy-start.3
  20.9 1.0 %copy-done.3 = f32[1,2,32,2048]{3,2,1,0:T(8,128)S(1)} copy-done((f32[1,2,32,2048]{3,2,1,0:T(8,128)S(1)}, f32[1,2,32,2048]{3,2,1,0:T(8,128)}, u32[]{:S(2)}) %copy-start.3) | copy-done | bytes 524312
  21.9 6.5 %shard_map.48 = (f32[1,2,32,2176]{3,2,1,0:T(8,128)S(1)}, f32[1,2,32,2048]{3,2,1,0:T(8,128)S(1)}, f32[1,2,32,2176]{3,2,1,0:T(8,128)S(1)}, f32[2,64,2176]{2,1,0:T(8,128)}) custom-call(s32[2]{0:T(128)S(1)} %pad_add_fusion.where_ref, f32[48,2048]{1,0:T(8,128)S(1)} %collective-permute-done.across_ref, f32[48,2048]{1,0:T(8,128)S(1)} %collective-permute-done.1.beside_ref, ...), custom_call_target="tpu_custom_call" | custom-call | flops 4000000000 | bytes 6684672 | tf_op jit(solution)/shard_map/pallas_call | solution.py:240
  28.4 1.9 %collective-permute-start.3 = (f32[1,2,32,2176]{3,2,1,0:T(8,128)S(1)}, f32[1,2,32,2176]{3,2,1,0:T(8,128)S(1)}, u32[]{:S(2)}, u32[]{:S(2)}) collective-permute-start(f32[1,2,32,2176]{3,2,1,0:T(8,128)S(1)} %get-tuple-element.27.own_ref), channel_id=1, source_target_pairs={{0,16},{32,48},{64,80},{96,112},{128,144},{160,176},{192,208},{224... | collective-permute-start | bytes 1671176 | tf_op jit(solution)/shard_map/ppermute | solution.py:296
  30.3 10.6 %collective-permute-start.2 = (f32[1,2,32,2176]{3,2,1,0:T(8,128)S(1)}, f32[1,2,32,2176]{3,2,1,0:T(8,128)S(1)}, u32[]{:S(2)}, u32[]{:S(2)}) collective-permute-start(f32[1,2,32,2176]{3,2,1,0:T(8,128)S(1)} %get-tuple-element.27.own_ref), channel_id=1, source_target_pairs={{16,32},{48,64},{80,96},{112,128},{144,160},{176,192},{208,224},{2... | collective-permute-start | bytes 1671176 | tf_op jit(solution)/shard_map/ppermute | solution.py:297
  40.9 0.0 collective-permute-done.3.beside_ref
  40.9 13.4 %collective-permute-done.2.across_ref = f32[1,2,32,2176]{3,2,1,0:T(8,128)S(1)} collective-permute-done((f32[1,2,32,2176]{3,2,1,0:T(8,128)S(1)}, f32[1,2,32,2176]{3,2,1,0:T(8,128)S(1)}, u32[]{:S(2)}, u32[]{:S(2)}) %collective-permute-start.2) | collective-permute-done | bytes 557088 | tf_op jit(solution)/shard_map/ppermute | solution.py:297
  54.2 0.0 copy-start.4
  54.2 1.2 %copy-done.4 = f32[2,64,2176]{2,1,0:T(8,128)S(1)} copy-done((f32[2,64,2176]{2,1,0:T(8,128)S(1)}, f32[2,64,2176]{2,1,0:T(8,128)}, u32[]{:S(2)}) %copy-start.4) | copy-done | bytes 1114136
  55.5 2.8 %shard_map.49 = f32[16,2,32,128]{3,2,1,0:T(8,128)S(1)} custom-call(s32[2]{0:T(128)S(1)} %pad_add_fusion.where_ref, f32[1,2,32,2176]{3,2,1,0:T(8,128)S(1)} %get-tuple-element.27.own_ref, f32[1,2,32,2176]{3,2,1,0:T(8,128)S(1)} %collective-permute-done.2.across_ref, f32[1,2,32,2176]{3,2,1,0:T(8,128)S(1)} %collective-permute-done.3.beside_ref, ...), custom_call_target="tpu_custom_call" | custom-call | flops 3000000000 | bytes 5701632 | tf_op jit(solution)/shard_map/pallas_call | solution.py:240
  58.2 16.9 %all_to_all.5 = f32[16,2,32,128]{3,2,1,0:T(8,128)S(1)} all-to-all(f32[16,2,32,128]{3,2,1,0:T(8,128)S(1)} %shard_map.49), channel_id=1, replica_groups=mesh['space'=32,'angle'=16] {'angle'}, dimensions={0} | all-to-all | bytes 1048576 | tf_op jit(solution)/shard_map/all_to_all | solution.py:305
  75.1 0.6 reduce_sum.9
  (1 shorter events, 0.0 us)
Async XLA Ops:
  0.1 1.0 %copy-start = (f32[2,32,2048]{2,1,0:T(8,128)S(1)}, f32[2,32,2048]{2,1,0:T(8,128)}, u32[]{:S(2)}) copy-start(f32[2,32,2048]{2,1,0:T(8,128)} %phase_ref.3) | copy-start | bytes 1572868
  1.7 19.2 %collective-permute-start = (f32[48,2048]{1,0:T(8,128)S(1)}, f32[48,2048]{1,0:T(8,128)S(1)}, u32[]{:S(2)}, u32[]{:S(2)}) collective-permute-start(f32[48,2048]{1,0:T(8,128)S(1)} %get-tuple-element.18), channel_id=1, source_target_pairs={{16,32},{48,64},{80,96},{112,128},{144,160},{176,192},{208,224},{2... | collective-permute-start | bytes 1179656 | tf_op jit(solution)/shard_map/ppermute | solution.py:268
  12.1 8.8 %collective-permute-start.1 = (f32[48,2048]{1,0:T(8,128)S(1)}, f32[48,2048]{1,0:T(8,128)S(1)}, u32[]{:S(2)}, u32[]{:S(2)}) collective-permute-start(f32[48,2048]{1,0:T(8,128)S(1)} %get-tuple-element.19), channel_id=1, source_target_pairs={{0,16},{32,48},{64,80},{96,112},{128,144},{160,176},{192,208},{224... | collective-permute-start | bytes 1179656 | tf_op jit(solution)/shard_map/ppermute | solution.py:267
  14.1 0.7 copy-start.1
  14.7 0.7 copy-start.2
  20.9 1.0 %copy-start.3 = (f32[1,2,32,2048]{3,2,1,0:T(8,128)S(1)}, f32[1,2,32,2048]{3,2,1,0:T(8,128)}, u32[]{:S(2)}) copy-start(f32[1,2,32,2048]{3,2,1,0:T(8,128)} %measured_ref.1) | copy-start | bytes 1572868
  28.4 12.5 %collective-permute-start.3 = (f32[1,2,32,2176]{3,2,1,0:T(8,128)S(1)}, f32[1,2,32,2176]{3,2,1,0:T(8,128)S(1)}, u32[]{:S(2)}, u32[]{:S(2)}) collective-permute-start(f32[1,2,32,2176]{3,2,1,0:T(8,128)S(1)} %get-tuple-element.27.own_ref), channel_id=1, source_target_pairs={{0,16},{32,48},{64,80},{96,112},{128,144},{160,176},{192,208},{224... | collective-permute-start | bytes 1671176 | tf_op jit(solution)/shard_map/ppermute | solution.py:296
  30.3 23.9 %collective-permute-start.2 = (f32[1,2,32,2176]{3,2,1,0:T(8,128)S(1)}, f32[1,2,32,2176]{3,2,1,0:T(8,128)S(1)}, u32[]{:S(2)}, u32[]{:S(2)}) collective-permute-start(f32[1,2,32,2176]{3,2,1,0:T(8,128)S(1)} %get-tuple-element.27.own_ref), channel_id=1, source_target_pairs={{16,32},{48,64},{80,96},{112,128},{144,160},{176,192},{208,224},{2... | collective-permute-start | bytes 1671176 | tf_op jit(solution)/shard_map/ppermute | solution.py:297
  54.2 1.2 %copy-start.4 = (f32[2,64,2176]{2,1,0:T(8,128)S(1)}, f32[2,64,2176]{2,1,0:T(8,128)}, u32[]{:S(2)}) copy-start(f32[2,64,2176]{2,1,0:T(8,128)} %get-tuple-element.30.turn1_ref) | copy-start | bytes 3342340

commit v4 on v3

v4 whole, which is shorter than its diff:
```python
import functools

import jax
import jax.numpy as jnp
from jax import lax
from jax.experimental import pallas as pl
from jax.experimental.pallas import tpu as pltpu
from jax.sharding import PartitionSpec as P

TILE = 128
REACH = 16
TAPS = 2 * REACH + 1
ROWS = 32
WIDE = ROWS + 2 * REACH
WIDEST = ROWS + 4 * REACH
F32 = jnp.float32
BF16 = jnp.bfloat16
GROUP = 4
BLOCK = 512
FRAME0 = BLOCK + 2 * TILE
FRAME1 = BLOCK + TILE
VMEM_LIMIT = 32 * 1024 * 1024


def split(x):
    high = x.astype(BF16)
    return high, (x - high.astype(F32)).astype(BF16)


def cos_sin(x):
    turns = jnp.round(x * 0.6366197723675814)
    rest = ((x - turns * 1.5703125) - turns * 4.837512969970703125e-4) - turns * 7.54978995489188216e-8
    square = rest * rest
    sine = rest + rest * square * (
        -1.6666654611e-1 + square * (8.3321608736e-3 + square * -1.9515295891e-4)
    )
    cosine = (1.0 - 0.5 * square) + square * square * (
        4.166664568298827e-2 + square * (-1.388731625493765e-3 + square * 2.443315711809948e-5)
    )
    quarter = turns.astype(jnp.int32)
    odd = (quarter & 1) == 1
    cos_part, sin_part = jnp.where(odd, sine, cosine), jnp.where(odd, cosine, sine)
    return (
        jnp.where(((quarter + 1) & 2) == 2, -cos_part, cos_part),
        jnp.where((quarter & 2) == 2, -sin_part, sin_part),
    )


def matmul(a, b):
    return jnp.dot(a, b, preferred_element_type=F32)


def tap_matrices(taps_ref, into1_ref, into2_ref, out1_ref, out2_ref, band_ref):
    lane = lax.broadcasted_iota(jnp.int32, (8, 256), 1)

    def laid(direction, part, start, step):
        out = jnp.zeros((8, 256), F32)
        for tap in range(TAPS):
            out = jnp.where(lane == (start + step * tap) % 256, taps_ref[direction, part, tap], out)
        return out

    def toeplitz(vector, rows):
        full = jnp.broadcast_to(vector[:1], (rows, 256))
        return pltpu.roll(full, 0, 1, stride=1, stride_axis=0)

    def put(ref, index, value):
        high, low = split(value)
        ref[index, 0] = high
        ref[index, 1] = low

    for ref, out_rows, in_rows, last, step, sign in (
        (into1_ref, WIDE, WIDEST, TAPS - 1, -1, 1.0),
        (into2_ref, ROWS, WIDE, TAPS - 1, -1, 1.0),
        (out1_ref, WIDE, ROWS, 1 - TAPS, 1, -1.0),
        (out2_ref, WIDEST, WIDE, 1 - TAPS, 1, -1.0),
    ):
        column = lax.broadcasted_iota(jnp.int32, (out_rows, 256), 1)
        real, imag = laid(0, 0, last, step), laid(0, 1, last, step) * sign
        real_2, imag_2 = laid(0, 0, in_rows + last, step), laid(0, 1, in_rows + last, step) * sign
        first = column < in_rows
        top = jnp.where(first, toeplitz(real, out_rows), -toeplitz(imag_2, out_rows))
        bottom = jnp.where(first, toeplitz(imag, out_rows), toeplitz(real_2, out_rows))
        put(ref, 0, jnp.concatenate([top, bottom], axis=0)[:, : 2 * in_rows])
    for index, sign in ((0, 1.0), (1, -1.0)):
        first = 256 - TILE // 2 - REACH
        start, step = (first, 1) if index == 0 else (first + TAPS - 1, -1)
        real = toeplitz(laid(1, 0, start, step), 256)[:, :TILE]
        imag = toeplitz(laid(1, 1, start, step) * sign, 256)[:, :TILE]
        put(
            band_ref,
            index,
            jnp.concatenate(
                [
                    jnp.concatenate([real, imag], axis=1),
                    jnp.concatenate([-imag, real], axis=1),
                ],
                axis=0,
            ),
        )


def row_pass(real, imag, matrix_ref):
    high, low = split(jnp.concatenate([real, imag], axis=0))
    matrix_high = matrix_ref[0, 0]
    both = jnp.concatenate([matrix_high, matrix_ref[0, 1]], axis=0)
    count = matrix_high.shape[0]
    product = matmul(both, high)
    total = product[:count] + (product[count:] + matmul(matrix_high, low))
    return total[: count // 2], total[count // 2 :]


def column_pass(real, imag, band_ref, index, tiles, first):
    rows = real.shape[0]
    have = real.shape[1] // TILE
    blank = jnp.zeros((rows, TILE), BF16)
    parts = [split(real), split(imag)]

    def stacked(level):
        def tile(part, j):
            if 0 <= j < have:
                return parts[part][level][:, j * TILE : (j + 1) * TILE]
            return blank

        return jnp.concatenate(
            [
                jnp.concatenate(
                    [tile(0, first + j), tile(0, first + j + 1), tile(1, first + j), tile(1, first + j + 1)],
                    axis=1,
                )
                for j in range(tiles)
            ],
            axis=0,
        )

    high, low = stacked(0), stacked(1)
    band_high = band_ref[index, 0]
    out = matmul(high, band_high) + (matmul(low, band_high) + matmul(high, band_ref[index, 1]))
    pieces = [out[j * rows : (j + 1) * rows] for j in range(tiles)]
    return (
        jnp.concatenate([p[:, :TILE] for p in pieces], axis=1),
        jnp.concatenate([p[:, TILE:] for p in pieces], axis=1),
    )


def neighbours(even, across, beside):
    return jnp.where(even, across, beside), jnp.where(even, beside, across)


def half_tile(x):
    blank = jnp.zeros((x.shape[0], TILE // 2), x.dtype)
    return jnp.concatenate([blank, x, blank], axis=1)


def padded_columns(source_ref, room_ref, semaphore):
    columns = source_ref.shape[-1]
    copy = pltpu.make_async_copy(source_ref, room_ref.at[:, :, TILE : TILE + columns], semaphore)
    copy.start()
    blank = jnp.zeros(room_ref.shape[:2] + (TILE,), F32)
    room_ref[:, :, :TILE] = blank
    room_ref[:, :, TILE + columns :] = blank
    copy.wait()


def block_of(room_ref, part, block):
    start = pl.multiple_of(block * BLOCK, TILE)
    return room_ref[part, :, pl.ds(start, FRAME0)][:, TILE // 2 : TILE // 2 + FRAME1]


def pack_phase(where_ref, phase_ref, border_ref, core_ref, own_ref, room_ref, semaphore):
    even = where_ref[1] == 0
    padded_columns(phase_ref, room_ref, semaphore)
    own_ref[0] = block_of(room_ref, 0, where_ref[2])
    own_ref[1] = block_of(room_ref, 1, where_ref[2])
    low, high = own_ref[1, :REACH], own_ref[1, ROWS - REACH :]
    for ref, nearest in ((border_ref, jnp.where(even, low, high)), (core_ref, jnp.where(even, high, low))):
        ref[:ROWS] = own_ref[0]
        ref[ROWS:] = nearest


def pack_measured(where_ref, tilts_ref, measured_ref, *refs):
    block_refs, room_ref, semaphore = refs[:GROUP], refs[GROUP], refs[GROUP + 1]
    padded_columns(measured_ref.at[0], room_ref, semaphore)
    lane = lax.broadcasted_iota(jnp.int32, (8, TILE), 1)
    row = lax.broadcasted_iota(jnp.int32, (8, TILE), 0)
    for shift, ref in enumerate(block_refs):
        block = lax.rem(where_ref[2] + shift, GROUP)
        ref[0] = block_of(room_ref, 0, block)
        ref[1] = block_of(room_ref, 1, block)
        corner = ref[0, :8, :TILE]
        corner = jnp.where((row == 0) & (lane == 0), tilts_ref[0, 0], corner)
        ref[0, :8, :TILE] = jnp.where((row == 0) & (lane == 1), tilts_ref[0, 1], corner)


def prepare(where_ref, taps_ref, own_ref, turn_ref, into1_ref, into2_ref, out1_ref, out2_ref, band_ref):
    tap_matrices(taps_ref, into1_ref, into2_ref, out1_ref, out2_ref, band_ref)
    for layer in range(2):
        turn_ref[layer, 0], turn_ref[layer, 1] = inside_grid(where_ref, *cos_sin(own_ref[layer]))


def inside_grid(where_ref, *fields):
    count = fields[0].shape[1]
    margin = (count - BLOCK) // 2
    lane = lax.broadcasted_iota(jnp.int32, (1, count), 1)
    there = ((lane >= margin) | (where_ref[2] != 0)) & ((lane < margin + BLOCK) | (where_ref[2] != GROUP - 1))
    return [jnp.where(there, field, 0.0) for field in fields]


def turns(where_ref, across_ref, beside_ref, own_ref, turn0_ref, turn1_ref, total_rows):
    even = where_ref[1] == 0
    first_row = where_ref[0]
    below, above = neighbours(even, across_ref[...], beside_ref[...])
    below = [jnp.where(first_row > 0, x, 0.0) for x in inside_grid(where_ref, *cos_sin(below))]
    above = [jnp.where(first_row + ROWS < total_rows, x, 0.0) for x in inside_grid(where_ref, *cos_sin(above))]
    for part in range(2):
        turn0_ref[part] = half_tile(jnp.concatenate([below[part][:ROWS], own_ref[0, part], above[part][:ROWS]], axis=0))
        turn1_ref[part] = jnp.concatenate([below[part][ROWS:], own_ref[1, part], above[part][ROWS:]], axis=0)


def sweep(where_ref, measured_ref, turn0_ref, turn1_ref, into1_ref, into2_ref, out1_ref, out2_ref, band_ref):
    row = (where_ref[0] - 2 * REACH + lax.broadcasted_iota(jnp.int32, (WIDEST, TILE), 0)).astype(F32)
    column = where_ref[2] * BLOCK - TILE + lax.broadcasted_iota(jnp.int32, (8, FRAME0), 1)
    cos_r, sin_r = cos_sin(measured_ref[0, :1, :1] * row)
    cos_c, sin_c = cos_sin(measured_ref[0, :1, 1:2] * column.astype(F32))
    cos_r, sin_r, cos_c, sin_c = cos_r[:, :1], sin_r[:, :1], cos_c[:1], sin_c[:1]
    cos0, sin0, cos1, sin1 = turn0_ref[0], turn0_ref[1], turn1_ref[0], turn1_ref[1]
    left_r, left_i = cos0 * cos_r - sin0 * sin_r, sin0 * cos_r + cos0 * sin_r
    wave0 = left_r * cos_c - left_i * sin_c, left_r * sin_c + left_i * cos_c
    real, imag = row_pass(*wave0, into1_ref)
    real, imag = column_pass(real, imag, band_ref, 0, FRAME1 // TILE, 0)
    wave1 = cos1 * real - sin1 * imag, cos1 * imag + sin1 * real
    real, imag = row_pass(*wave1, into2_ref)
    real, imag = column_pass(real, imag, band_ref, 0, FRAME0 // TILE, -1)
    real, imag = inside_grid(
        where_ref, real - half_tile(measured_ref[0]), imag - half_tile(measured_ref[1])
    )
    real, imag = column_pass(real, imag, band_ref, 1, FRAME1 // TILE, 0)
    real, imag = row_pass(real, imag, out1_ref)
    term1 = wave1[0] * imag - wave1[1] * real
    real, imag = cos1 * real + sin1 * imag, cos1 * imag - sin1 * real
    real, imag = column_pass(real, imag, band_ref, 1, BLOCK // TILE, 0)
    real, imag = row_pass(real, imag, out2_ref)
    middle = slice(TILE, TILE + BLOCK)
    return wave0[0][:, middle] * imag - wave0[1][:, middle] * real, term1


def first_angle(
    where_ref, across_ref, beside_ref, own_ref, measured_ref, into1_ref, into2_ref, out1_ref, out2_ref, band_ref,
    turn0_ref, turn1_ref, total0_ref, total1_ref, *, total_rows,
):
    turns(where_ref, across_ref, beside_ref, own_ref, turn0_ref, turn1_ref, total_rows)
    total0_ref[...], total1_ref[...] = sweep(
        where_ref, measured_ref, turn0_ref, turn1_ref, into1_ref, into2_ref, out1_ref, out2_ref, band_ref
    )


def other_angles(where_ref, *refs):
    measured_refs, (total0_ref, total1_ref), rest = refs[: GROUP - 1], refs[GROUP - 1 : GROUP + 1], refs[GROUP + 1 : -1]
    out_ref = refs[-1]
    total0, total1 = total0_ref[...], total1_ref[...]
    for measured_ref in measured_refs:
        term0, term1 = sweep(where_ref, measured_ref, *rest)
        total0, total1 = total0 + term0, total1 + term1
    total1 = total1[:, TILE // 2 : TILE // 2 + BLOCK]
    for j in range(BLOCK // TILE):
        out_ref[j, :WIDEST] = total0[:, j * TILE : (j + 1) * TILE]
        out_ref[j, WIDEST:] = total1[:, j * TILE : (j + 1) * TILE]


def add_angles(where_ref, tiles_ref, own_ref, border_ref, core_ref):
    even = where_ref[1] == 0
    total = tiles_ref[0]
    for j in range(1, tiles_ref.shape[0]):
        total = total + tiles_ref[j]
    slice0, slice1 = total[:WIDEST], total[WIDEST:]
    own_ref[0] = slice0[ROWS : 2 * ROWS]
    own_ref[1] = slice1[REACH : REACH + ROWS]
    low = jnp.concatenate([slice0[:ROWS], slice1[:REACH]], axis=0)
    high = jnp.concatenate([slice0[2 * ROWS :], slice1[REACH + ROWS :]], axis=0)
    border_ref[...] = jnp.where(even, low, high)
    core_ref[...] = jnp.where(even, high, low)


def add_strips(where_ref, own_ref, across_ref, beside_ref, out_ref):
    below, above = neighbours(where_ref[1] == 0, across_ref[...], beside_ref[...])
    out_ref[0] = own_ref[0] + (below[:ROWS] + above[:ROWS])
    out_ref[1, :REACH] = own_ref[1, :REACH] + below[ROWS:]
    out_ref[1, REACH:] = own_ref[1, REACH:] + above[ROWS:]


def call(kernel, shapes, scalars, arrays, flops, scratch=(), space=pltpu.VMEM):
    moved = sum(a.size * a.dtype.itemsize for a in arrays)
    moved += sum(int(s.size) * s.dtype.itemsize for s in shapes)
    return pl.pallas_call(
        kernel,
        out_shape=shapes,
        in_specs=[pl.BlockSpec(memory_space=pltpu.SMEM)] * len(scalars)
        + [pl.BlockSpec(memory_space=space)] * len(arrays),
        out_specs=[pl.BlockSpec(memory_space=pltpu.VMEM)] * len(shapes),
        scratch_shapes=list(scratch),
        compiler_params=pltpu.CompilerParams(vmem_limit_bytes=VMEM_LIMIT),
        cost_estimate=pl.CostEstimate(flops=flops, bytes_accessed=moved, transcendentals=0),
    )(*scalars, *arrays)


def swaps(pairs):
    return pairs + [(b, a) for a, b in pairs]


def body(total_rows, phase_delay, measured, tilts, fresnel_taps):
    columns = phase_delay.shape[2]
    strips = lax.axis_size("space")
    along = lax.axis_size("angle") // GROUP
    strip = lax.axis_index("space")
    block = lax.axis_index("angle") // along
    where = jnp.stack([strip * ROWS, strip & 1, block]).astype(jnp.int32)
    over_border = swaps([(i, i + 1) for i in range(1, strips - 1, 2)])
    in_chip = swaps([(i, i + 1) for i in range(0, strips, 2)])

    def shifted(shift):
        return [(g * along + i, (g + shift) % GROUP * along + i) for g in range(GROUP) for i in range(along)]

    struct = jax.ShapeDtypeStruct
    room = [pltpu.VMEM((2, ROWS, columns + 2 * TILE), F32), pltpu.SemaphoreType.DMA]
    to_border, to_core, own_phase = call(
        pack_phase,
        [struct((ROWS + REACH, FRAME1), F32)] * 2 + [struct((2, ROWS, FRAME1), F32)],
        [where],
        [phase_delay],
        0,
        room,
        pl.ANY,
    )
    beside = lax.ppermute(to_core, "space", in_chip)
    across = lax.ppermute(to_border, "space", over_border)
    blocks = call(
        pack_measured,
        [struct((2, ROWS, FRAME1), F32)] * GROUP,
        [where, tilts],
        [measured],
        0,
        room,
        pl.ANY,
    )
    arrived = [lax.ppermute(blocks[shift], "angle", shifted(shift)) for shift in range(1, GROUP)]
    own, *matrices = call(
        prepare,
        [
            struct((2, 2, ROWS, FRAME1), F32),
            struct((1, 2, 2 * WIDE, 2 * WIDEST), BF16),
            struct((1, 2, 2 * ROWS, 2 * WIDE), BF16),
            struct((1, 2, 2 * WIDE, 2 * ROWS), BF16),
            struct((1, 2, 2 * WIDEST, 2 * WIDE), BF16),
            struct((2, 2, 512, 256), BF16),
        ],
        [where, fresnel_taps],
        [own_phase],
        10_000_000,
    )
    turn0, turn1, total0, total1 = call(
        functools.partial(first_angle, total_rows=total_rows),
        [
            struct((2, WIDEST, FRAME0), F32),
            struct((2, WIDE, FRAME1), F32),
            struct((WIDEST, BLOCK), F32),
            struct((WIDE, FRAME1), F32),
        ],
        [where],
        [across, beside, own, blocks[0], *matrices],
        2_000_000_000,
    )
    (tiles,) = call(
        other_angles,
        [struct((BLOCK // TILE, WIDEST + WIDE, TILE), F32)],
        [where],
        [*arrived, total0, total1, turn0, turn1, *matrices],
        6_000_000_000,
    )
    beside_x = [[g * along + i for i in range(along)] for g in range(GROUP)]
    tiles = lax.all_to_all(tiles, "angle", 0, 0, axis_index_groups=beside_x)
    total, to_border, to_core = call(
        add_angles,
        [struct((2, ROWS, TILE), F32)] + [struct((ROWS + REACH, TILE), F32)] * 2,
        [where],
        [tiles],
        0,
    )
    beside = lax.ppermute(to_core, "space", in_chip)
    across = lax.ppermute(to_border, "space", over_border)
    (gradient,) = call(add_strips, [struct((2, ROWS, TILE), F32)], [where], [total, across, beside], 0)
    return gradient


def solution(mesh):
    def step(phase_delay, measured, tilts, fresnel_taps):
        return jax.shard_map(
            functools.partial(body, phase_delay.shape[1]),
            mesh=mesh,
            in_specs=(P(None, "space", None), P("angle", None, "space", None), P("angle", None), P()),
            out_specs=P(None, "space", "angle"),
            check_vma=False,
        )(phase_delay, measured, tilts, fresnel_taps)

    return step
```

time: 76.8 us -> 67.3 us (0.88)
  the two profiles are of different devices: /device:TPU:57 before, /device:TPU:121 now
where the time goes in v4:
time: 67.3 us; the launch traced here: 66.9 us
  starting transfers between devices  28.5 us (42%)
  Pallas kernels  18.6 us (28%)
  blocking collectives  10.5 us (16%)
  waiting for transfers between devices  8.01 us (12%)
  local copies, waits for them, and re-layouts  1.06 us (2%)
    pallas_call x7, Pallas kernels, call(): pl.pallas_call(kernel, out_shape=shapes, in_specs=[pl.BlockSpec(memory_sp...  18.6 us
    ppermute x2, starting transfers between devices, body(): across = lax.ppermute(to_border, 'space', over_border)  15.4 us
    all_to_all x1, blocking collectives, body(): tiles = lax.all_to_all(tiles, 'angle', 0, 0, axis_index_groups=beside_x)  10.5 us
    ppermute x3, starting transfers between devices, body(): lax.ppermute(blocks[shift], 'angle', shifted(shift))  9.29 us
    ppermute x3, waiting for transfers between devices, body(): lax.ppermute(blocks[shift], 'angle', shifted(shift))  4.68 us
    ppermute x2, starting transfers between devices, body(): beside = lax.ppermute(to_core, 'space', in_chip)  3.84 us
    ppermute x2, waiting for transfers between devices, body(): across = lax.ppermute(to_border, 'space', over_border)  3.32 us
  transfers between devices with their start and end apart: 7, of which 3 were waited for; matrix products, arithmetic and copies ran while one was open for 0% of the time, Pallas kernels for 9%

profile of v4, /device:TPU:121, one launch (start us, length us, event | category | flops | bytes accessed | tf_op | source)
XLA Modules:
  0.0 66.9 jit_solution(9901868085027664298)
XLA Ops:
  0.0 0.1 pad_add_fusion.where_ref
  0.1 1.0 %copy-done = f32[2,32,2048]{2,1,0:T(8,128)S(1)} copy-done((f32[2,32,2048]{2,1,0:T(8,128)S(1)}, f32[2,32,2048]{2,1,0:T(8,128)}, u32[]{:S(2)}) %copy-start) | copy-done | bytes 524312
  1.1 0.7 %shard_map.47 = (f32[48,640]{1,0:T(8,128)S(1)}, f32[48,640]{1,0:T(8,128)S(1)}, f32[2,32,640]{2,1,0:T(8,128)S(1)}) custom-call(s32[3]{0:T(128)S(1)} %pad_add_fusion.where_ref, f32[2,32,2048]{2,1,0:T(8,128)S(1)} %copy-done), custom_call_target="tpu_custom_call" | custom-call | bytes 933888 | tf_op jit(solution)/shard_map/pallas_call | solution.py:293
  1.8 0.0 copy-start.3
  1.9 9.5 %collective-permute-start.3 = (f32[48,640]{1,0:T(8,128)S(1)}, f32[48,640]{1,0:T(8,128)S(1)}, u32[]{:S(2)}, u32[]{:S(2)}) collective-permute-start(f32[48,640]{1,0:T(8,128)S(1)} %get-tuple-element.28), channel_id=1, source_target_pairs={{16,32},{48,64},{80,96},{112,128},{144,160},{176,192},{208,224},{2... | collective-permute-start | bytes 368648 | tf_op jit(solution)/shard_map/ppermute | solution.py:334
  11.4 1.9 %collective-permute-start.4 = (f32[48,640]{1,0:T(8,128)S(1)}, f32[48,640]{1,0:T(8,128)S(1)}, u32[]{:S(2)}, u32[]{:S(2)}) collective-permute-start(f32[48,640]{1,0:T(8,128)S(1)} %get-tuple-element.29), channel_id=1, source_target_pairs={{0,16},{32,48},{64,80},{96,112},{128,144},{160,176},{192,208},{224... | collective-permute-start | bytes 368648 | tf_op jit(solution)/shard_map/ppermute | solution.py:333
  13.3 0.9 %shard_map.46 = (f32[2,32,640]{2,1,0:T(8,128)S(1)}, f32[2,32,640]{2,1,0:T(8,128)S(1)}, f32[2,32,640]{2,1,0:T(8,128)S(1)}, f32[2,32,640]{2,1,0:T(8,128)S(1)}) custom-call(s32[3]{0:T(128)S(1)} %pad_add_fusion.where_ref, f32[1,2]{1,0:T(1,128)S(1)} %copy-done.3, f32[1,2,32,2048]{3,2,1,0:T(8,128)S(1)} %copy-done.1), custom_call_target="tpu_custom_call" | custom-call | bytes 1179648 | tf_op jit(solution)/shard_map/pallas_call | solution.py:293
  14.2 3.1 %collective-permute-start = (f32[2,32,640]{2,1,0:T(8,128)S(1)}, f32[2,32,640]{2,1,0:T(8,128)S(1)}, u32[]{:S(2)}, u32[]{:S(2)}) collective-permute-start(f32[2,32,640]{2,1,0:T(8,128)S(1)} %get-tuple-element.25), channel_id=1, source_target_pairs={{0,4},{1,5},{2,6},{3,7},{4,8},{5,9},{6,10},{7,11},{8,12},{9,13},{1... | collective-permute-start | bytes 491528 | tf_op jit(solution)/shard_map/ppermute | solution.py:344
  17.3 0.0 copy-start.2
  17.3 3.1 %collective-permute-start.1 = (f32[2,32,640]{2,1,0:T(8,128)S(1)}, f32[2,32,640]{2,1,0:T(8,128)S(1)}, u32[]{:S(2)}, u32[]{:S(2)}) collective-permute-start(f32[2,32,640]{2,1,0:T(8,128)S(1)} %get-tuple-element.26), channel_id=1, source_target_pairs={{0,8},{1,9},{2,10},{3,11},{4,12},{5,13},{6,14},{7,15},{8,0},{9,1},... | collective-permute-start | bytes 491528 | tf_op jit(solution)/shard_map/ppermute | solution.py:344
  20.4 3.1 %collective-permute-start.2 = (f32[2,32,640]{2,1,0:T(8,128)S(1)}, f32[2,32,640]{2,1,0:T(8,128)S(1)}, u32[]{:S(2)}, u32[]{:S(2)}) collective-permute-start(f32[2,32,640]{2,1,0:T(8,128)S(1)} %get-tuple-element.27), channel_id=1, source_target_pairs={{0,12},{1,13},{2,14},{3,15},{4,0},{5,1},{6,2},{7,3},{8,4},{9,5},{1... | collective-permute-start | bytes 491528 | tf_op jit(solution)/shard_map/ppermute | solution.py:344
  23.5 1.4 %shard_map.48 = (f32[2,2,32,640]{3,2,1,0:T(8,128)S(1)}, bf16[1,2,128,192]{3,2,1,0:T(8,128)(2,1)S(1)}, bf16[1,2,64,128]{3,2,1,0:T(8,128)(2,1)S(1)}, bf16[1,2,128,...) custom-call(s32[3]{0:T(128)S(1)} %pad_add_fusion.where_ref, ...), custom_call_target="tpu_custom_call" | custom-call | flops 10000000 | bytes 1802240 | tf_op jit(solution)/shard_map/pallas_call | solution.py:293
  24.9 0.0 collective-permute-done.3.across_ref
  24.9 4.1 %shard_map.49 = (f32[2,96,768]{2,1,0:T(8,128)S(1)}, f32[2,64,640]{2,1,0:T(8,128)S(1)}, f32[96,512]{1,0:T(8,128)S(1)}, f32[64,640]{1,0:T(8,128)S(1)}) custom-call(s32[3]{0:T(128)S(1)} %pad_add_fusion.where_ref, f32[48,640]{1,0:T(8,128)S(1)} %collective-permute-done.3.across_ref, f32[48,640]{1,0:T(8,128)S(1)} %collective-permute-done.4.beside_ref, ...), custom_call_target="tpu_custom_call" | custom-call | flops 2000000000 | bytes 3325952 | tf_op jit(solution)/shard_map/pallas_call | solution.py:293
  29.0 2.2 %collective-permute-done.1.refs_1_ = f32[2,32,640]{2,1,0:T(8,128)S(1)} collective-permute-done((f32[2,32,640]{2,1,0:T(8,128)S(1)}, f32[2,32,640]{2,1,0:T(8,128)S(1)}, u32[]{:S(2)}, u32[]{:S(2)}) %collective-permute-start.1) | collective-permute-done | bytes 163872 | tf_op jit(solution)/shard_map/ppermute | solution.py:344
  31.2 2.5 %collective-permute-done.2.refs_2_ = f32[2,32,640]{2,1,0:T(8,128)S(1)} collective-permute-done((f32[2,32,640]{2,1,0:T(8,128)S(1)}, f32[2,32,640]{2,1,0:T(8,128)S(1)}, u32[]{:S(2)}, u32[]{:S(2)}) %collective-permute-start.2) | collective-permute-done | bytes 163872 | tf_op jit(solution)/shard_map/ppermute | solution.py:344
  33.7 9.8 %shard_map.50 = f32[4,160,128]{2,1,0:T(8,128)S(1)} custom-call(s32[3]{0:T(128)S(1)} %pad_add_fusion.where_ref, f32[2,32,640]{2,1,0:T(8,128)S(1)} %collective-permute-done.refs_0_, f32[2,32,640]{2,1,0:T(8,128)S(1)} %collective-permute-done.1.refs_1_, f32[2,32,640]{2,1,0:T(8,128)S(1)} %collective-permute-done.2.refs_2_, ...), custom_call_target="tpu_custom_call" | custom-call | flops 6000000000 | bytes 3407872 | tf_op jit(solution)/shard_map/pallas_call | solution.py:293
  43.5 10.5 %all_to_all.5.tiles_ref = f32[4,160,128]{2,1,0:T(8,128)S(1)} all-to-all(f32[4,160,128]{2,1,0:T(8,128)S(1)} %shard_map.50), channel_id=1, replica_groups={{0,1,2,3},{4,5,6,7},{8,9,10,11},{12,13,14,15},{16,17,18,19},{20,21,22,2..., dimensions={0} | all-to-all | bytes 655360 | tf_op jit(solution)/shard_map/all_to_all | solution.py:379
  54.0 0.6 shard_map.51
  54.6 5.9 %collective-permute-start.5 = (f32[48,128]{1,0:T(8,128)S(1)}, f32[48,128]{1,0:T(8,128)S(1)}, u32[]{:S(2)}, u32[]{:S(2)}) collective-permute-start(f32[48,128]{1,0:T(8,128)S(1)} %get-tuple-element.43), channel_id=1, source_target_pairs={{16,32},{48,64},{80,96},{112,128},{144,160},{176,192},{208,224},{2... | collective-permute-start | bytes 73736 | tf_op jit(solution)/shard_map/ppermute | solution.py:388
  60.5 1.9 %collective-permute-start.6 = (f32[48,128]{1,0:T(8,128)S(1)}, f32[48,128]{1,0:T(8,128)S(1)}, u32[]{:S(2)}, u32[]{:S(2)}) collective-permute-start(f32[48,128]{1,0:T(8,128)S(1)} %get-tuple-element.44), channel_id=1, source_target_pairs={{0,16},{32,48},{64,80},{96,112},{128,144},{160,176},{192,208},{224... | collective-permute-start | bytes 73736 | tf_op jit(solution)/shard_map/ppermute | solution.py:387
  62.4 3.3 %collective-permute-done.5.across_ref = f32[48,128]{1,0:T(8,128)S(1)} collective-permute-done((f32[48,128]{1,0:T(8,128)S(1)}, f32[48,128]{1,0:T(8,128)S(1)}, u32[]{:S(2)}, u32[]{:S(2)}) %collective-permute-start.5) | collective-permute-done | bytes 24608 | tf_op jit(solution)/shard_map/ppermute | solution.py:388
  65.7 0.0 collective-permute-done.6.beside_ref
  65.7 1.2 %shard_map.52 = f32[2,32,128]{2,1,0:T(8,128)} custom-call(s32[3]{0:T(128)S(1)} %pad_add_fusion.where_ref, f32[2,32,128]{2,1,0:T(8,128)S(1)} %get-tuple-element.42.own_ref, f32[48,128]{1,0:T(8,128)S(1)} %collective-permute-done.5.across_ref, f32[48,128]{1,0:T(8,128)S(1)} %collective-permute-done.6.beside_ref), custom_call_target="tpu_custom_call" | custom-call | bytes 114688 | tf_op jit(solution)/shard_map/pallas_call | solution.py:293
  (7 shorter events, 0.0 us)
Async XLA Ops:
  0.1 1.0 %copy-start = (f32[2,32,2048]{2,1,0:T(8,128)S(1)}, f32[2,32,2048]{2,1,0:T(8,128)}, u32[]{:S(2)}) copy-start(f32[2,32,2048]{2,1,0:T(8,128)} %phase_ref.1) | copy-start | bytes 1572868
  1.1 12.2 %copy-start.1 = (f32[1,2,32,2048]{3,2,1,0:T(8,128)S(1)}, f32[1,2,32,2048]{3,2,1,0:T(8,128)}, u32[]{:S(2)}) copy-start(f32[1,2,32,2048]{3,2,1,0:T(8,128)} %measured_ref.1) | copy-start | bytes 1572868
  1.8 11.5 %copy-start.3 = (f32[1,2]{1,0:T(1,128)S(1)}, f32[1,2]{1,0:T(1,128)}, u32[]{:S(2)}) copy-start(f32[1,2]{1,0:T(1,128)} %tilts_ref.1) | copy-start | bytes 28
  1.9 23.0 %collective-permute-start.3 = (f32[48,640]{1,0:T(8,128)S(1)}, f32[48,640]{1,0:T(8,128)S(1)}, u32[]{:S(2)}, u32[]{:S(2)}) collective-permute-start(f32[48,640]{1,0:T(8,128)S(1)} %get-tuple-element.28), channel_id=1, source_target_pairs={{16,32},{48,64},{80,96},{112,128},{144,160},{176,192},{208,224},{2... | collective-permute-start | bytes 368648 | tf_op jit(solution)/shard_map/ppermute | solution.py:334
  11.4 13.6 %collective-permute-start.4 = (f32[48,640]{1,0:T(8,128)S(1)}, f32[48,640]{1,0:T(8,128)S(1)}, u32[]{:S(2)}, u32[]{:S(2)}) collective-permute-start(f32[48,640]{1,0:T(8,128)S(1)} %get-tuple-element.29), channel_id=1, source_target_pairs={{0,16},{32,48},{64,80},{96,112},{128,144},{160,176},{192,208},{224... | collective-permute-start | bytes 368648 | tf_op jit(solution)/shard_map/ppermute | solution.py:333
  14.2 14.8 %collective-permute-start = (f32[2,32,640]{2,1,0:T(8,128)S(1)}, f32[2,32,640]{2,1,0:T(8,128)S(1)}, u32[]{:S(2)}, u32[]{:S(2)}) collective-permute-start(f32[2,32,640]{2,1,0:T(8,128)S(1)} %get-tuple-element.25), channel_id=1, source_target_pairs={{0,4},{1,5},{2,6},{3,7},{4,8},{5,9},{6,10},{7,11},{8,12},{9,13},{1... | collective-permute-start | bytes 491528 | tf_op jit(solution)/shard_map/ppermute | solution.py:344
  17.3 6.2 %copy-start.2 = (f32[2,2,33]{2,1,0:T(2,128)S(1)}, f32[2,2,33]{2,1,0:T(2,128)}, u32[]{:S(2)}) copy-start(f32[2,2,33]{2,1,0:T(2,128)} %taps_ref.1) | copy-start | bytes 1588
  17.3 13.9 %collective-permute-start.1 = (f32[2,32,640]{2,1,0:T(8,128)S(1)}, f32[2,32,640]{2,1,0:T(8,128)S(1)}, u32[]{:S(2)}, u32[]{:S(2)}) collective-permute-start(f32[2,32,640]{2,1,0:T(8,128)S(1)} %get-tuple-element.26), channel_id=1, source_target_pairs={{0,8},{1,9},{2,10},{3,11},{4,12},{5,13},{6,14},{7,15},{8,0},{9,1},... | collective-permute-start | bytes 491528 | tf_op jit(solution)/shard_map/ppermute | solution.py:344
  20.4 13.3 %collective-permute-start.2 = (f32[2,32,640]{2,1,0:T(8,128)S(1)}, f32[2,32,640]{2,1,0:T(8,128)S(1)}, u32[]{:S(2)}, u32[]{:S(2)}) collective-permute-start(f32[2,32,640]{2,1,0:T(8,128)S(1)} %get-tuple-element.27), channel_id=1, source_target_pairs={{0,12},{1,13},{2,14},{3,15},{4,0},{5,1},{6,2},{7,3},{8,4},{9,5},{1... | collective-permute-start | bytes 491528 | tf_op jit(solution)/shard_map/ppermute | solution.py:344
  54.6 11.2 %collective-permute-start.5 = (f32[48,128]{1,0:T(8,128)S(1)}, f32[48,128]{1,0:T(8,128)S(1)}, u32[]{:S(2)}, u32[]{:S(2)}) collective-permute-start(f32[48,128]{1,0:T(8,128)S(1)} %get-tuple-element.43), channel_id=1, source_target_pairs={{16,32},{48,64},{80,96},{112,128},{144,160},{176,192},{208,224},{2... | collective-permute-start | bytes 73736 | tf_op jit(solution)/shard_map/ppermute | solution.py:388
  60.5 5.2 %collective-permute-start.6 = (f32[48,128]{1,0:T(8,128)S(1)}, f32[48,128]{1,0:T(8,128)S(1)}, u32[]{:S(2)}, u32[]{:S(2)}) collective-permute-start(f32[48,128]{1,0:T(8,128)S(1)} %get-tuple-element.44), channel_id=1, source_target_pairs={{0,16},{32,48},{64,80},{96,112},{128,144},{160,176},{192,208},{224... | collective-permute-start | bytes 73736 | tf_op jit(solution)/shard_map/ppermute | solution.py:387

commit v5 on v4

--- a/solution.py
+++ b/solution.py
@@ -80,7 +80,14 @@
         first = column < in_rows
         top = jnp.where(first, toeplitz(real, out_rows), -toeplitz(imag_2, out_rows))
         bottom = jnp.where(first, toeplitz(imag, out_rows), toeplitz(real_2, out_rows))
-        put(ref, 0, jnp.concatenate([top, bottom], axis=0)[:, : 2 * in_rows])
+        high, low = split(jnp.concatenate([top, bottom], axis=0)[:, : 2 * in_rows])
+        if ref.shape[1] == 2 * in_rows:
+            ref[...] = jnp.concatenate([high, low], axis=0)
+        else:
+            high = high.astype(F32)
+            low = low.astype(F32)
+            both = jnp.concatenate([high, low], axis=0), jnp.concatenate([high, jnp.zeros_like(low)], axis=0)
+            ref[...] = jnp.concatenate(both, axis=1).astype(BF16)
     for index, sign in ((0, 1.0), (1, -1.0)):
         first = 256 - TILE // 2 - REACH
         start, step = (first, 1) if index == 0 else (first + TAPS - 1, -1)
@@ -99,47 +106,54 @@
         )
 
 
-def row_pass(real, imag, matrix_ref):
-    high, low = split(jnp.concatenate([real, imag], axis=0))
-    matrix_high = matrix_ref[0, 0]
-    both = jnp.concatenate([matrix_high, matrix_ref[0, 1]], axis=0)
-    count = matrix_high.shape[0]
-    product = matmul(both, high)
-    total = product[:count] + (product[count:] + matmul(matrix_high, low))
-    return total[: count // 2], total[count // 2 :]
-
-
-def column_pass(real, imag, band_ref, index, tiles, first):
-    rows = real.shape[0]
-    have = real.shape[1] // TILE
+def row_pass(fields, matrix_ref):
+    columns = fields[0][0].shape[1]
+    high, low = split(jnp.concatenate([jnp.concatenate(field, axis=0) for field in fields], axis=1))
+    matrix = matrix_ref[...]
+    count = matrix.shape[0] // 2
+    if matrix.shape[1] == high.shape[0]:
+        product = matmul(matrix, high)
+        total = product[:count] + (product[count:] + matmul(matrix[:count], low))
+    else:
+        product = matmul(matrix, jnp.concatenate([high, low], axis=0))
+        total = product[:count] + product[count:]
+    pieces = [total[:, i * columns : (i + 1) * columns] for i in range(len(fields))]
+    return [(piece[: count // 2], piece[count // 2 :]) for piece in pieces]
+
+
+def column_pass(fields, band_ref, index, tiles, first):
+    rows = fields[0][0].shape[0]
+    have = fields[0][0].shape[1] // TILE
     blank = jnp.zeros((rows, TILE), BF16)
-    parts = [split(real), split(imag)]
-
-    def stacked(level):
+
+    def stacked(parts):
         def tile(part, j):
-            if 0 <= j < have:
-                return parts[part][level][:, j * TILE : (j + 1) * TILE]
-            return blank
+            return part[:, j * TILE : (j + 1) * TILE] if 0 <= j < have else blank
 
         return jnp.concatenate(
             [
-                jnp.concatenate(
-                    [tile(0, first + j), tile(0, first + j + 1), tile(1, first + j), tile(1, first + j + 1)],
-                    axis=1,
-                )
+                jnp.concatenate([tile(part, first + j + i) for part in field for i in range(2)], axis=1)
+                for field in parts
                 for j in range(tiles)
             ],
             axis=0,
         )
 
-    high, low = stacked(0), stacked(1)
+    levels = [[split(part) for part in field] for field in fields]
+    high = stacked([[part[0] for part in field] for field in levels])
+    low = stacked([[part[1] for part in field] for field in levels])
     band_high = band_ref[index, 0]
     out = matmul(high, band_high) + (matmul(low, band_high) + matmul(high, band_ref[index, 1]))
-    pieces = [out[j * rows : (j + 1) * rows] for j in range(tiles)]
-    return (
-        jnp.concatenate([p[:, :TILE] for p in pieces], axis=1),
-        jnp.concatenate([p[:, TILE:] for p in pieces], axis=1),
-    )
+    results = []
+    for i in range(len(fields)):
+        pieces = [out[(i * tiles + j) * rows : (i * tiles + j + 1) * rows] for j in range(tiles)]
+        results.append(
+            (
+                jnp.concatenate([p[:, :TILE] for p in pieces], axis=1),
+                jnp.concatenate([p[:, TILE:] for p in pieces], axis=1),
+            )
+        )
+    return results
 
 
 def neighbours(even, across, beside):
@@ -183,7 +197,7 @@
     lane = lax.broadcasted_iota(jnp.int32, (8, TILE), 1)
     row = lax.broadcasted_iota(jnp.int32, (8, TILE), 0)
     for shift, ref in enumerate(block_refs):
-        block = lax.rem(where_ref[2] + shift, GROUP)
+        block = where_ref[2] ^ shift
         ref[0] = block_of(room_ref, 0, block)
         ref[1] = block_of(room_ref, 1, block)
         corner = ref[0, :8, :TILE]
@@ -216,31 +230,33 @@
         turn1_ref[part] = jnp.concatenate([below[part][ROWS:], own_ref[1, part], above[part][ROWS:]], axis=0)
 
 
-def sweep(where_ref, measured_ref, turn0_ref, turn1_ref, into1_ref, into2_ref, out1_ref, out2_ref, band_ref):
+def sweep(where_ref, measured_refs, turn0_ref, turn1_ref, into1_ref, into2_ref, out1_ref, out2_ref, band_ref):
     row = (where_ref[0] - 2 * REACH + lax.broadcasted_iota(jnp.int32, (WIDEST, TILE), 0)).astype(F32)
     column = where_ref[2] * BLOCK - TILE + lax.broadcasted_iota(jnp.int32, (8, FRAME0), 1)
-    cos_r, sin_r = cos_sin(measured_ref[0, :1, :1] * row)
-    cos_c, sin_c = cos_sin(measured_ref[0, :1, 1:2] * column.astype(F32))
-    cos_r, sin_r, cos_c, sin_c = cos_r[:, :1], sin_r[:, :1], cos_c[:1], sin_c[:1]
     cos0, sin0, cos1, sin1 = turn0_ref[0], turn0_ref[1], turn1_ref[0], turn1_ref[1]
-    left_r, left_i = cos0 * cos_r - sin0 * sin_r, sin0 * cos_r + cos0 * sin_r
-    wave0 = left_r * cos_c - left_i * sin_c, left_r * sin_c + left_i * cos_c
-    real, imag = row_pass(*wave0, into1_ref)
-    real, imag = column_pass(real, imag, band_ref, 0, FRAME1 // TILE, 0)
-    wave1 = cos1 * real - sin1 * imag, cos1 * imag + sin1 * real
-    real, imag = row_pass(*wave1, into2_ref)
-    real, imag = column_pass(real, imag, band_ref, 0, FRAME0 // TILE, -1)
-    real, imag = inside_grid(
-        where_ref, real - half_tile(measured_ref[0]), imag - half_tile(measured_ref[1])
-    )
-    real, imag = column_pass(real, imag, band_ref, 1, FRAME1 // TILE, 0)
-    real, imag = row_pass(real, imag, out1_ref)
-    term1 = wave1[0] * imag - wave1[1] * real
-    real, imag = cos1 * real + sin1 * imag, cos1 * imag - sin1 * real
-    real, imag = column_pass(real, imag, band_ref, 1, BLOCK // TILE, 0)
-    real, imag = row_pass(real, imag, out2_ref)
+    waves0 = []
+    for measured_ref in measured_refs:
+        cos_r, sin_r = cos_sin(measured_ref[0, :1, :1] * row)
+        cos_c, sin_c = cos_sin(measured_ref[0, :1, 1:2] * column.astype(F32))
+        cos_r, sin_r, cos_c, sin_c = cos_r[:, :1], sin_r[:, :1], cos_c[:1], sin_c[:1]
+        left_r, left_i = cos0 * cos_r - sin0 * sin_r, sin0 * cos_r + cos0 * sin_r
+        waves0.append((left_r * cos_c - left_i * sin_c, left_r * sin_c + left_i * cos_c))
+    fields = column_pass(row_pass(waves0, into1_ref), band_ref, 0, FRAME1 // TILE, 0)
+    waves1 = [(cos1 * real - sin1 * imag, cos1 * imag + sin1 * real) for real, imag in fields]
+    fields = column_pass(row_pass(waves1, into2_ref), band_ref, 0, FRAME0 // TILE, -1)
+    fields = [
+        inside_grid(where_ref, real - half_tile(measured_ref[0]), imag - half_tile(measured_ref[1]))
+        for (real, imag), measured_ref in zip(fields, measured_refs)
+    ]
+    fields = row_pass(column_pass(fields, band_ref, 1, FRAME1 // TILE, 0), out1_ref)
+    total1 = sum(wave[0] * imag - wave[1] * real for wave, (real, imag) in zip(waves1, fields))
+    fields = [(cos1 * real + sin1 * imag, cos1 * imag - sin1 * real) for real, imag in fields]
+    fields = row_pass(column_pass(fields, band_ref, 1, BLOCK // TILE, 0), out2_ref)
     middle = slice(TILE, TILE + BLOCK)
-    return wave0[0][:, middle] * imag - wave0[1][:, middle] * real, term1
+    total0 = sum(
+        wave[0][:, middle] * imag - wave[1][:, middle] * real for wave, (real, imag) in zip(waves0, fields)
+    )
+    return total0, total1
 
 
 def first_angle(
@@ -249,17 +265,15 @@
 ):
     turns(where_ref, across_ref, beside_ref, own_ref, turn0_ref, turn1_ref, total_rows)
     total0_ref[...], total1_ref[...] = sweep(
-        where_ref, measured_ref, turn0_ref, turn1_ref, into1_ref, into2_ref, out1_ref, out2_ref, band_ref
+        where_ref, [measured_ref], turn0_ref, turn1_ref, into1_ref, into2_ref, out1_ref, out2_ref, band_ref
     )
 
 
 def other_angles(where_ref, *refs):
     measured_refs, (total0_ref, total1_ref), rest = refs[: GROUP - 1], refs[GROUP - 1 : GROUP + 1], refs[GROUP + 1 : -1]
     out_ref = refs[-1]
-    total0, total1 = total0_ref[...], total1_ref[...]
-    for measured_ref in measured_refs:
-        term0, term1 = sweep(where_ref, measured_ref, *rest)
-        total0, total1 = total0 + term0, total1 + term1
+    term0, term1 = sweep(where_ref, measured_refs, *rest)
+    total0, total1 = total0_ref[...] + term0, total1_ref[...] + term1
     total1 = total1[:, TILE // 2 : TILE // 2 + BLOCK]
     for j in range(BLOCK // TILE):
         out_ref[j, :WIDEST] = total0[:, j * TILE : (j + 1) * TILE]
@@ -316,8 +330,8 @@
     over_border = swaps([(i, i + 1) for i in range(1, strips - 1, 2)])
     in_chip = swaps([(i, i + 1) for i in range(0, strips, 2)])
 
-    def shifted(shift):
-        return [(g * along + i, (g + shift) % GROUP * along + i) for g in range(GROUP) for i in range(along)]
+    def swapped(shift):
+        return [(g * along + i, (g ^ shift) * along + i) for g in range(GROUP) for i in range(along)]
 
     struct = jax.ShapeDtypeStruct
     room = [pltpu.VMEM((2, ROWS, columns + 2 * TILE), F32), pltpu.SemaphoreType.DMA]
@@ -328,7 +342,7 @@
         [phase_delay],
         0,
         room,
-        pl.ANY,
+        pltpu.HBM,
     )
     beside = lax.ppermute(to_core, "space", in_chip)
     across = lax.ppermute(to_border, "space", over_border)
@@ -339,17 +353,17 @@
         [measured],
         0,
         room,
-        pl.ANY,
-    )
-    arrived = [lax.ppermute(blocks[shift], "angle", shifted(shift)) for shift in range(1, GROUP)]
+        pltpu.HBM,
+    )
+    arrived = [lax.ppermute(blocks[shift], "angle", swapped(shift)) for shift in range(1, GROUP)]
     own, *matrices = call(
         prepare,
         [
             struct((2, 2, ROWS, FRAME1), F32),
-            struct((1, 2, 2 * WIDE, 2 * WIDEST), BF16),
-            struct((1, 2, 2 * ROWS, 2 * WIDE), BF16),
-            struct((1, 2, 2 * WIDE, 2 * ROWS), BF16),
-            struct((1, 2, 2 * WIDEST, 2 * WIDE), BF16),
+            struct((4 * WIDE, 2 * WIDEST), BF16),
+            struct((4 * ROWS, 4 * WIDE), BF16),
+            struct((4 * WIDE, 4 * ROWS), BF16),
+            struct((4 * WIDEST, 4 * WIDE), BF16),
             struct((2, 2, 512, 256), BF16),
         ],
         [where, fresnel_taps],

time: 67.3 us -> 65.5 us (0.973)
  Pallas kernels: 18.6 us -> 15.9 us
  waiting for transfers between devices: 8.01 us -> 10.2 us
  blocking collectives: 10.5 us -> 9.7 us
    pallas_call x7, Pallas kernels: 18.6 us -> 15.9 us  [call(): pl.pallas_call(kernel, out_shape=shapes, in_specs=[pl.BlockSpec(memory_sp...]
    ppermute x3, waiting for transfers between devices: 4.68 us -> 7.26 us  [body(): lax.ppermute(blocks[shift], 'angle', swapped(shift))]
    ppermute x3, starting transfers between devices: 9.29 us -> 8.37 us  [body(): lax.ppermute(blocks[shift], 'angle', swapped(shift))]
    all_to_all x1, blocking collectives: 10.5 us -> 9.7 us  [body(): tiles = lax.all_to_all(tiles, 'angle', 0, 0, axis_index_groups=beside_x)]
where the time goes in v5:
time: 65.5 us; the launch traced here: 65.1 us
  starting transfers between devices  28 us (43%)
  Pallas kernels  15.9 us (24%)
  waiting for transfers between devices  10.2 us (16%)
  blocking collectives  9.7 us (15%)
  local copies, waits for them, and re-layouts  1.06 us (2%)
    pallas_call x7, Pallas kernels, call(): pl.pallas_call(kernel, out_shape=shapes, in_specs=[pl.BlockSpec(memory_sp...  15.9 us
    ppermute x2, starting transfers between devices, body(): across = lax.ppermute(to_border, 'space', over_border)  15.8 us
    all_to_all x1, blocking collectives, body(): tiles = lax.all_to_all(tiles, 'angle', 0, 0, axis_index_groups=beside_x)  9.7 us
    ppermute x3, starting transfers between devices, body(): lax.ppermute(blocks[shift], 'angle', swapped(shift))  8.37 us
    ppermute x3, waiting for transfers between devices, body(): lax.ppermute(blocks[shift], 'angle', swapped(shift))  7.26 us
    ppermute x2, starting transfers between devices, body(): beside = lax.ppermute(to_core, 'space', in_chip)  3.84 us
    ppermute x2, waiting for transfers between devices, body(): across = lax.ppermute(to_border, 'space', over_border)  2.96 us
  transfers between devices with their start and end apart: 7, of which 3 were waited for; matrix products, arithmetic and copies ran while one was open for 0% of the time, Pallas kernels for 9%

profile of v5, /device:TPU:121, one launch (start us, length us, event | category | flops | bytes accessed | tf_op | source)
XLA Modules:
  0.0 65.1 jit_solution(16599829554237888473)
XLA Ops:
  0.0 0.1 pad_add_fusion.where_ref
  0.1 1.0 %copy-done = f32[2,32,2048]{2,1,0:T(8,128)S(1)} copy-done((f32[2,32,2048]{2,1,0:T(8,128)S(1)}, f32[2,32,2048]{2,1,0:T(8,128)}, u32[]{:S(2)}) %copy-start) | copy-done | bytes 524312
  1.1 0.7 %shard_map.47 = (f32[48,640]{1,0:T(8,128)S(1)}, f32[48,640]{1,0:T(8,128)S(1)}, f32[2,32,640]{2,1,0:T(8,128)S(1)}) custom-call(s32[3]{0:T(128)S(1)} %pad_add_fusion.where_ref, f32[2,32,2048]{2,1,0:T(8,128)S(1)} %copy-done), custom_call_target="tpu_custom_call" | custom-call | bytes 933888 | tf_op jit(solution)/shard_map/pallas_call | solution.py:307
  1.8 0.0 copy-start.3
  1.9 9.5 %collective-permute-start.3 = (f32[48,640]{1,0:T(8,128)S(1)}, f32[48,640]{1,0:T(8,128)S(1)}, u32[]{:S(2)}, u32[]{:S(2)}) collective-permute-start(f32[48,640]{1,0:T(8,128)S(1)} %get-tuple-element.28), channel_id=1, source_target_pairs={{16,32},{48,64},{80,96},{112,128},{144,160},{176,192},{208,224},{2... | collective-permute-start | bytes 368648 | tf_op jit(solution)/shard_map/ppermute | solution.py:348
  11.4 1.9 %collective-permute-start.4 = (f32[48,640]{1,0:T(8,128)S(1)}, f32[48,640]{1,0:T(8,128)S(1)}, u32[]{:S(2)}, u32[]{:S(2)}) collective-permute-start(f32[48,640]{1,0:T(8,128)S(1)} %get-tuple-element.29), channel_id=1, source_target_pairs={{0,16},{32,48},{64,80},{96,112},{128,144},{160,176},{192,208},{224... | collective-permute-start | bytes 368648 | tf_op jit(solution)/shard_map/ppermute | solution.py:347
  13.3 0.9 %shard_map.46 = (f32[2,32,640]{2,1,0:T(8,128)S(1)}, f32[2,32,640]{2,1,0:T(8,128)S(1)}, f32[2,32,640]{2,1,0:T(8,128)S(1)}, f32[2,32,640]{2,1,0:T(8,128)S(1)}) custom-call(s32[3]{0:T(128)S(1)} %pad_add_fusion.where_ref, f32[1,2]{1,0:T(1,128)S(1)} %copy-done.3, f32[1,2,32,2048]{3,2,1,0:T(8,128)S(1)} %copy-done.1), custom_call_target="tpu_custom_call" | custom-call | bytes 1179648 | tf_op jit(solution)/shard_map/pallas_call | solution.py:307
  14.2 2.2 %collective-permute-start = (f32[2,32,640]{2,1,0:T(8,128)S(1)}, f32[2,32,640]{2,1,0:T(8,128)S(1)}, u32[]{:S(2)}, u32[]{:S(2)}) collective-permute-start(f32[2,32,640]{2,1,0:T(8,128)S(1)} %get-tuple-element.25), channel_id=1, source_target_pairs={{0,4},{1,5},{2,6},{3,7},{4,0},{5,1},{6,2},{7,3},{8,12},{9,13},{10,... | collective-permute-start | bytes 491528 | tf_op jit(solution)/shard_map/ppermute | solution.py:358
  16.4 0.0 copy-start.2
  16.4 4.0 %collective-permute-start.1 = (f32[2,32,640]{2,1,0:T(8,128)S(1)}, f32[2,32,640]{2,1,0:T(8,128)S(1)}, u32[]{:S(2)}, u32[]{:S(2)}) collective-permute-start(f32[2,32,640]{2,1,0:T(8,128)S(1)} %get-tuple-element.26), channel_id=1, source_target_pairs={{0,8},{1,9},{2,10},{3,11},{4,12},{5,13},{6,14},{7,15},{8,0},{9,1},... | collective-permute-start | bytes 491528 | tf_op jit(solution)/shard_map/ppermute | solution.py:358
  20.4 2.2 %collective-permute-start.2 = (f32[2,32,640]{2,1,0:T(8,128)S(1)}, f32[2,32,640]{2,1,0:T(8,128)S(1)}, u32[]{:S(2)}, u32[]{:S(2)}) collective-permute-start(f32[2,32,640]{2,1,0:T(8,128)S(1)} %get-tuple-element.27), channel_id=1, source_target_pairs={{0,12},{1,13},{2,14},{3,15},{4,8},{5,9},{6,10},{7,11},{8,4},{9,5},... | collective-permute-start | bytes 491528 | tf_op jit(solution)/shard_map/ppermute | solution.py:358
  22.6 1.4 %shard_map.48 = (f32[2,2,32,640]{3,2,1,0:T(8,128)S(1)}, bf16[256,192]{1,0:T(8,128)(2,1)S(1)}, bf16[128,256]{1,0:T(8,128)(2,1)S(1)}, bf16[256,128]{1,0:T(8,128)(2...) custom-call(s32[3]{0:T(128)S(1)} %pad_add_fusion.where_ref, f32[2,2,33]{2,1,0:T(2,128)S(1)} %copy-done.2, ...), custom_call_target="tpu_custom_call" | custom-call | flops 10000000 | bytes 1966080 | tf_op jit(solution)/shard_map/pallas_call | solution.py:307
  24.0 0.0 collective-permute-done.3.across_ref
  24.1 0.0 collective-permute-done.4.beside_ref
  24.1 3.8 %shard_map.49 = (f32[2,96,768]{2,1,0:T(8,128)S(1)}, f32[2,64,640]{2,1,0:T(8,128)S(1)}, f32[96,512]{1,0:T(8,128)S(1)}, f32[64,640]{1,0:T(8,128)S(1)}) custom-call(s32[3]{0:T(128)S(1)} %pad_add_fusion.where_ref, f32[48,640]{1,0:T(8,128)S(1)} %collective-permute-done.3.across_ref, f32[48,640]{1,0:T(8,128)S(1)} %collective-permute-done.4.beside_ref, ...), custom_call_target="tpu_custom_call" | custom-call | flops 2000000000 | bytes 3489792 | tf_op jit(solution)/shard_map/pallas_call | solution.py:307
  27.9 2.5 %collective-permute-done.1.refs_1_ = f32[2,32,640]{2,1,0:T(8,128)S(1)} collective-permute-done((f32[2,32,640]{2,1,0:T(8,128)S(1)}, f32[2,32,640]{2,1,0:T(8,128)S(1)}, u32[]{:S(2)}, u32[]{:S(2)}) %collective-permute-start.1) | collective-permute-done | bytes 163872 | tf_op jit(solution)/shard_map/ppermute | solution.py:358
  30.4 4.7 %collective-permute-done.2.refs_2_ = f32[2,32,640]{2,1,0:T(8,128)S(1)} collective-permute-done((f32[2,32,640]{2,1,0:T(8,128)S(1)}, f32[2,32,640]{2,1,0:T(8,128)S(1)}, u32[]{:S(2)}, u32[]{:S(2)}) %collective-permute-start.2) | collective-permute-done | bytes 163872 | tf_op jit(solution)/shard_map/ppermute | solution.py:358
  35.1 7.4 %shard_map.50 = f32[4,160,128]{2,1,0:T(8,128)S(1)} custom-call(s32[3]{0:T(128)S(1)} %pad_add_fusion.where_ref, f32[2,32,640]{2,1,0:T(8,128)S(1)} %collective-permute-done.refs_0_, f32[2,32,640]{2,1,0:T(8,128)S(1)} %collective-permute-done.1.refs_1_, f32[2,32,640]{2,1,0:T(8,128)S(1)} %collective-permute-done.2.refs_2_, ...), custom_call_target="tpu_custom_call" | custom-call | flops 6000000000 | bytes 3571712 | tf_op jit(solution)/shard_map/pallas_call | solution.py:307
  42.5 9.7 %all_to_all.5.tiles_ref = f32[4,160,128]{2,1,0:T(8,128)S(1)} all-to-all(f32[4,160,128]{2,1,0:T(8,128)S(1)} %shard_map.50), channel_id=1, replica_groups={{0,1,2,3},{4,5,6,7},{8,9,10,11},{12,13,14,15},{16,17,18,19},{20,21,22,2..., dimensions={0} | all-to-all | bytes 655360 | tf_op jit(solution)/shard_map/all_to_all | solution.py:393
  52.2 0.6 shard_map.51
  52.8 6.3 %collective-permute-start.5 = (f32[48,128]{1,0:T(8,128)S(1)}, f32[48,128]{1,0:T(8,128)S(1)}, u32[]{:S(2)}, u32[]{:S(2)}) collective-permute-start(f32[48,128]{1,0:T(8,128)S(1)} %get-tuple-element.43), channel_id=1, source_target_pairs={{16,32},{48,64},{80,96},{112,128},{144,160},{176,192},{208,224},{2... | collective-permute-start | bytes 73736 | tf_op jit(solution)/shard_map/ppermute | solution.py:402
  59.1 1.9 %collective-permute-start.6 = (f32[48,128]{1,0:T(8,128)S(1)}, f32[48,128]{1,0:T(8,128)S(1)}, u32[]{:S(2)}, u32[]{:S(2)}) collective-permute-start(f32[48,128]{1,0:T(8,128)S(1)} %get-tuple-element.44), channel_id=1, source_target_pairs={{0,16},{32,48},{64,80},{96,112},{128,144},{160,176},{192,208},{224... | collective-permute-start | bytes 73736 | tf_op jit(solution)/shard_map/ppermute | solution.py:401
  61.0 3.0 %collective-permute-done.5.across_ref = f32[48,128]{1,0:T(8,128)S(1)} collective-permute-done((f32[48,128]{1,0:T(8,128)S(1)}, f32[48,128]{1,0:T(8,128)S(1)}, u32[]{:S(2)}, u32[]{:S(2)}) %collective-permute-start.5) | collective-permute-done | bytes 24608 | tf_op jit(solution)/shard_map/ppermute | solution.py:402
  64.0 1.2 %shard_map.52 = f32[2,32,128]{2,1,0:T(8,128)} custom-call(s32[3]{0:T(128)S(1)} %pad_add_fusion.where_ref, f32[2,32,128]{2,1,0:T(8,128)S(1)} %get-tuple-element.42.own_ref, f32[48,128]{1,0:T(8,128)S(1)} %collective-permute-done.5.across_ref, f32[48,128]{1,0:T(8,128)S(1)} %collective-permute-done.6.beside_ref), custom_call_target="tpu_custom_call" | custom-call | bytes 114688 | tf_op jit(solution)/shard_map/pallas_call | solution.py:307
  (7 shorter events, 0.0 us)
Async XLA Ops:
  0.1 1.0 %copy-start = (f32[2,32,2048]{2,1,0:T(8,128)S(1)}, f32[2,32,2048]{2,1,0:T(8,128)}, u32[]{:S(2)}) copy-start(f32[2,32,2048]{2,1,0:T(8,128)} %phase_ref.1) | copy-start | bytes 1572868
  1.1 12.2 %copy-start.1 = (f32[1,2,32,2048]{3,2,1,0:T(8,128)S(1)}, f32[1,2,32,2048]{3,2,1,0:T(8,128)}, u32[]{:S(2)}) copy-start(f32[1,2,32,2048]{3,2,1,0:T(8,128)} %measured_ref.1) | copy-start | bytes 1572868
  1.8 11.5 %copy-start.3 = (f32[1,2]{1,0:T(1,128)S(1)}, f32[1,2]{1,0:T(1,128)}, u32[]{:S(2)}) copy-start(f32[1,2]{1,0:T(1,128)} %tilts_ref.1) | copy-start | bytes 28
  1.9 22.2 %collective-permute-start.3 = (f32[48,640]{1,0:T(8,128)S(1)}, f32[48,640]{1,0:T(8,128)S(1)}, u32[]{:S(2)}, u32[]{:S(2)}) collective-permute-start(f32[48,640]{1,0:T(8,128)S(1)} %get-tuple-element.28), channel_id=1, source_target_pairs={{16,32},{48,64},{80,96},{112,128},{144,160},{176,192},{208,224},{2... | collective-permute-start | bytes 368648 | tf_op jit(solution)/shard_map/ppermute | solution.py:348
  11.4 12.7 %collective-permute-start.4 = (f32[48,640]{1,0:T(8,128)S(1)}, f32[48,640]{1,0:T(8,128)S(1)}, u32[]{:S(2)}, u32[]{:S(2)}) collective-permute-start(f32[48,640]{1,0:T(8,128)S(1)} %get-tuple-element.29), channel_id=1, source_target_pairs={{0,16},{32,48},{64,80},{96,112},{128,144},{160,176},{192,208},{224... | collective-permute-start | bytes 368648 | tf_op jit(solution)/shard_map/ppermute | solution.py:347
  14.2 13.7 %collective-permute-start = (f32[2,32,640]{2,1,0:T(8,128)S(1)}, f32[2,32,640]{2,1,0:T(8,128)S(1)}, u32[]{:S(2)}, u32[]{:S(2)}) collective-permute-start(f32[2,32,640]{2,1,0:T(8,128)S(1)} %get-tuple-element.25), channel_id=1, source_target_pairs={{0,4},{1,5},{2,6},{3,7},{4,0},{5,1},{6,2},{7,3},{8,12},{9,13},{10,... | collective-permute-start | bytes 491528 | tf_op jit(solution)/shard_map/ppermute | solution.py:358
  16.4 6.2 %copy-start.2 = (f32[2,2,33]{2,1,0:T(2,128)S(1)}, f32[2,2,33]{2,1,0:T(2,128)}, u32[]{:S(2)}) copy-start(f32[2,2,33]{2,1,0:T(2,128)} %taps_ref.1) | copy-start | bytes 1588
  16.4 14.0 %collective-permute-start.1 = (f32[2,32,640]{2,1,0:T(8,128)S(1)}, f32[2,32,640]{2,1,0:T(8,128)S(1)}, u32[]{:S(2)}, u32[]{:S(2)}) collective-permute-start(f32[2,32,640]{2,1,0:T(8,128)S(1)} %get-tuple-element.26), channel_id=1, source_target_pairs={{0,8},{1,9},{2,10},{3,11},{4,12},{5,13},{6,14},{7,15},{8,0},{9,1},... | collective-permute-start | bytes 491528 | tf_op jit(solution)/shard_map/ppermute | solution.py:358
  20.4 14.7 %collective-permute-start.2 = (f32[2,32,640]{2,1,0:T(8,128)S(1)}, f32[2,32,640]{2,1,0:T(8,128)S(1)}, u32[]{:S(2)}, u32[]{:S(2)}) collective-permute-start(f32[2,32,640]{2,1,0:T(8,128)S(1)} %get-tuple-element.27), channel_id=1, source_target_pairs={{0,12},{1,13},{2,14},{3,15},{4,8},{5,9},{6,10},{7,11},{8,4},{9,5},... | collective-permute-start | bytes 491528 | tf_op jit(solution)/shard_map/ppermute | solution.py:358
  52.8 11.2 %collective-permute-start.5 = (f32[48,128]{1,0:T(8,128)S(1)}, f32[48,128]{1,0:T(8,128)S(1)}, u32[]{:S(2)}, u32[]{:S(2)}) collective-permute-start(f32[48,128]{1,0:T(8,128)S(1)} %get-tuple-element.43), channel_id=1, source_target_pairs={{16,32},{48,64},{80,96},{112,128},{144,160},{176,192},{208,224},{2... | collective-permute-start | bytes 73736 | tf_op jit(solution)/shard_map/ppermute | solution.py:402
  59.1 4.9 %collective-permute-start.6 = (f32[48,128]{1,0:T(8,128)S(1)}, f32[48,128]{1,0:T(8,128)S(1)}, u32[]{:S(2)}, u32[]{:S(2)}) collective-permute-start(f32[48,128]{1,0:T(8,128)S(1)} %get-tuple-element.44), channel_id=1, source_target_pairs={{0,16},{32,48},{64,80},{96,112},{128,144},{160,176},{192,208},{224... | collective-permute-start | bytes 73736 | tf_op jit(solution)/shard_map/ppermute | solution.py:401

commit v6 on v5

--- a/solution.py
+++ b/solution.py
@@ -20,6 +20,7 @@
 FRAME0 = BLOCK + 2 * TILE
 FRAME1 = BLOCK + TILE
 VMEM_LIMIT = 32 * 1024 * 1024
+PACK_LIMIT = 60 * 1024 * 1024
 
 
 def split(x):
@@ -172,7 +173,7 @@
     blank = jnp.zeros(room_ref.shape[:2] + (TILE,), F32)
     room_ref[:, :, :TILE] = blank
     room_ref[:, :, TILE + columns :] = blank
-    copy.wait()
+    return copy
 
 
 def block_of(room_ref, part, block):
@@ -180,35 +181,47 @@
     return room_ref[part, :, pl.ds(start, FRAME0)][:, TILE // 2 : TILE // 2 + FRAME1]
 
 
-def pack_phase(where_ref, phase_ref, border_ref, core_ref, own_ref, room_ref, semaphore):
+def measured_block(where_ref, tilts_ref, room_ref, shift, ref):
+    block = where_ref[2] ^ shift
+    ref[0] = block_of(room_ref, 0, block)
+    ref[1] = block_of(room_ref, 1, block)
+    lane = lax.broadcasted_iota(jnp.int32, (8, TILE), 1)
+    row = lax.broadcasted_iota(jnp.int32, (8, TILE), 0)
+    corner = ref[0, :8, :TILE]
+    corner = jnp.where((row == 0) & (lane == 0), tilts_ref[0, 0], corner)
+    ref[0, :8, :TILE] = jnp.where((row == 0) & (lane == 1), tilts_ref[0, 1], corner)
+
+
+def pack(
+    where_ref, tilts_ref, phase_ref, measured_ref, border_ref, core_ref, own_ref, far_ref,
+    phase_room, measured_room, phase_semaphore, measured_semaphore,
+):
     even = where_ref[1] == 0
-    padded_columns(phase_ref, room_ref, semaphore)
-    own_ref[0] = block_of(room_ref, 0, where_ref[2])
-    own_ref[1] = block_of(room_ref, 1, where_ref[2])
+    phase_copy = padded_columns(phase_ref, phase_room, phase_semaphore)
+    measured_copy = padded_columns(measured_ref.at[0], measured_room, measured_semaphore)
+    phase_copy.wait()
+    own_ref[0] = block_of(phase_room, 0, where_ref[2])
+    own_ref[1] = block_of(phase_room, 1, where_ref[2])
     low, high = own_ref[1, :REACH], own_ref[1, ROWS - REACH :]
     for ref, nearest in ((border_ref, jnp.where(even, low, high)), (core_ref, jnp.where(even, high, low))):
         ref[:ROWS] = own_ref[0]
         ref[ROWS:] = nearest
-
-
-def pack_measured(where_ref, tilts_ref, measured_ref, *refs):
-    block_refs, room_ref, semaphore = refs[:GROUP], refs[GROUP], refs[GROUP + 1]
-    padded_columns(measured_ref.at[0], room_ref, semaphore)
-    lane = lax.broadcasted_iota(jnp.int32, (8, TILE), 1)
-    row = lax.broadcasted_iota(jnp.int32, (8, TILE), 0)
-    for shift, ref in enumerate(block_refs):
-        block = where_ref[2] ^ shift
-        ref[0] = block_of(room_ref, 0, block)
-        ref[1] = block_of(room_ref, 1, block)
-        corner = ref[0, :8, :TILE]
-        corner = jnp.where((row == 0) & (lane == 0), tilts_ref[0, 0], corner)
-        ref[0, :8, :TILE] = jnp.where((row == 0) & (lane == 1), tilts_ref[0, 1], corner)
-
-
-def prepare(where_ref, taps_ref, own_ref, turn_ref, into1_ref, into2_ref, out1_ref, out2_ref, band_ref):
+    measured_copy.wait()
+    measured_block(where_ref, tilts_ref, measured_room, 2, far_ref)
+
+
+def prepare(
+    where_ref, tilts_ref, taps_ref, own_ref, measured_ref,
+    own_block_ref, block1_ref, block3_ref, turn_ref, into1_ref, into2_ref, out1_ref, out2_ref, band_ref,
+    room_ref, semaphore,
+):
+    copy = padded_columns(measured_ref.at[0], room_ref, semaphore)
     tap_matrices(taps_ref, into1_ref, into2_ref, out1_ref, out2_ref, band_ref)
     for layer in range(2):
         turn_ref[layer, 0], turn_ref[layer, 1] = inside_grid(where_ref, *cos_sin(own_ref[layer]))
+    copy.wait()
+    for shift, ref in ((0, own_block_ref), (1, block1_ref), (3, block3_ref)):
+        measured_block(where_ref, tilts_ref, room_ref, shift, ref)
 
 
 def inside_grid(where_ref, *fields):
@@ -259,20 +272,19 @@
     return total0, total1
 
 
-def first_angle(
-    where_ref, across_ref, beside_ref, own_ref, measured_ref, into1_ref, into2_ref, out1_ref, out2_ref, band_ref,
+def first_angles(
+    where_ref, across_ref, beside_ref, own_ref, near_ref, far_ref, into1_ref, into2_ref, out1_ref, out2_ref, band_ref,
     turn0_ref, turn1_ref, total0_ref, total1_ref, *, total_rows,
 ):
     turns(where_ref, across_ref, beside_ref, own_ref, turn0_ref, turn1_ref, total_rows)
     total0_ref[...], total1_ref[...] = sweep(
-        where_ref, [measured_ref], turn0_ref, turn1_ref, into1_ref, into2_ref, out1_ref, out2_ref, band_ref
-    )
-
-
-def other_angles(where_ref, *refs):
-    measured_refs, (total0_ref, total1_ref), rest = refs[: GROUP - 1], refs[GROUP - 1 : GROUP + 1], refs[GROUP + 1 : -1]
+        where_ref, [near_ref, far_ref], turn0_ref, turn1_ref, into1_ref, into2_ref, out1_ref, out2_ref, band_ref
+    )
+
+
+def other_angles(where_ref, near_ref, far_ref, total0_ref, total1_ref, *refs):
     out_ref = refs[-1]
-    term0, term1 = sweep(where_ref, measured_refs, *rest)
+    term0, term1 = sweep(where_ref, [near_ref, far_ref], *refs[:-1])
     total0, total1 = total0_ref[...] + term0, total1_ref[...] + term1
     total1 = total1[:, TILE // 2 : TILE // 2 + BLOCK]
     for j in range(BLOCK // TILE):
@@ -301,17 +313,17 @@
     out_ref[1, REACH:] = own_ref[1, REACH:] + above[ROWS:]
 
 
-def call(kernel, shapes, scalars, arrays, flops, scratch=(), space=pltpu.VMEM):
+def call(kernel, shapes, scalars, arrays, flops, scratch=(), in_hbm=0, limit=VMEM_LIMIT):
     moved = sum(a.size * a.dtype.itemsize for a in arrays)
     moved += sum(int(s.size) * s.dtype.itemsize for s in shapes)
+    spaces = [pltpu.SMEM] * len(scalars) + [pltpu.VMEM] * (len(arrays) - in_hbm) + [pltpu.HBM] * in_hbm
     return pl.pallas_call(
         kernel,
         out_shape=shapes,
-        in_specs=[pl.BlockSpec(memory_space=pltpu.SMEM)] * len(scalars)
-        + [pl.BlockSpec(memory_space=space)] * len(arrays),
+        in_specs=[pl.BlockSpec(memory_space=space) for space in spaces],
         out_specs=[pl.BlockSpec(memory_space=pltpu.VMEM)] * len(shapes),
         scratch_shapes=list(scratch),
-        compiler_params=pltpu.CompilerParams(vmem_limit_bytes=VMEM_LIMIT),
+        compiler_params=pltpu.CompilerParams(vmem_limit_bytes=limit),
         cost_estimate=pl.CostEstimate(flops=flops, bytes_accessed=moved, transcendentals=0),
     )(*scalars, *arrays)
 
@@ -334,31 +346,27 @@
         return [(g * along + i, (g ^ shift) * along + i) for g in range(GROUP) for i in range(along)]
 
     struct = jax.ShapeDtypeStruct
-    room = [pltpu.VMEM((2, ROWS, columns + 2 * TILE), F32), pltpu.SemaphoreType.DMA]
-    to_border, to_core, own_phase = call(
-        pack_phase,
-        [struct((ROWS + REACH, FRAME1), F32)] * 2 + [struct((2, ROWS, FRAME1), F32)],
-        [where],
-        [phase_delay],
+    room = pltpu.VMEM((2, ROWS, columns + 2 * TILE), F32)
+    measured_struct = struct((2, ROWS, FRAME1), F32)
+    to_border, to_core, own_phase, far = call(
+        pack,
+        [struct((ROWS + REACH, FRAME1), F32)] * 2 + [struct((2, ROWS, FRAME1), F32), measured_struct],
+        [where, tilts],
+        [phase_delay, measured],
         0,
-        room,
-        pltpu.HBM,
-    )
+        [room, room, pltpu.SemaphoreType.DMA, pltpu.SemaphoreType.DMA],
+        in_hbm=2,
+        limit=PACK_LIMIT,
+    )
+    far = lax.ppermute(far, "angle", swapped(2))
     beside = lax.ppermute(to_core, "space", in_chip)
     across = lax.ppermute(to_border, "space", over_border)
-    blocks = call(
-        pack_measured,
-        [struct((2, ROWS, FRAME1), F32)] * GROUP,
-        [where, tilts],
-        [measured],
-        0,
-        room,
-        pltpu.HBM,
-    )
-    arrived = [lax.ppermute(blocks[shift], "angle", swapped(shift)) for shift in range(1, GROUP)]
-    own, *matrices = call(
+    near, block1, block3, own, *matrices = call(
         prepare,
         [
+            measured_struct,
+            measured_struct,
+            measured_struct,
             struct((2, 2, ROWS, FRAME1), F32),
             struct((4 * WIDE, 2 * WIDEST), BF16),
             struct((4 * ROWS, 4 * WIDE), BF16),
@@ -366,12 +374,16 @@
             struct((4 * WIDEST, 4 * WIDE), BF16),
             struct((2, 2, 512, 256), BF16),
         ],
-        [where, fresnel_taps],
-        [own_phase],
+        [where, tilts, fresnel_taps],
+        [own_phase, measured],
         10_000_000,
-    )
+        [room, pltpu.SemaphoreType.DMA],
+        in_hbm=1,
+    )
+    block1 = lax.ppermute(block1, "angle", swapped(1))
+    block3 = lax.ppermute(block3, "angle", swapped(3))
     turn0, turn1, total0, total1 = call(
-        functools.partial(first_angle, total_rows=total_rows),
+        functools.partial(first_angles, total_rows=total_rows),
         [
             struct((2, WIDEST, FRAME0), F32),
             struct((2, WIDE, FRAME1), F32),
@@ -379,15 +391,15 @@
             struct((WIDE, FRAME1), F32),
         ],
         [where],
-        [across, beside, own, blocks[0], *matrices],
-        2_000_000_000,
+        [across, beside, own, near, far, *matrices],
+        4_000_000_000,
     )
     (tiles,) = call(
         other_angles,
         [struct((BLOCK // TILE, WIDEST + WIDE, TILE), F32)],
         [where],
-        [*arrived, total0, total1, turn0, turn1, *matrices],
-        6_000_000_000,
+        [block3, block1, total0, total1, turn0, turn1, *matrices],
+        4_000_000_000,
     )
     beside_x = [[g * along + i for i in range(along)] for g in range(GROUP)]
     tiles = lax.all_to_all(tiles, "angle", 0, 0, axis_index_groups=beside_x)

time: 65.5 us -> 65.4 us (level)
  the two profiles are of different devices: /device:TPU:121 before, /device:TPU:57 now
where the time goes in v6:
time: 65.4 us; the launch traced here: 65 us
  starting transfers between devices  28.3 us (43%)
  Pallas kernels  17.3 us (26%)
  blocking collectives  10.5 us (16%)
  waiting for transfers between devices  7.19 us (11%)
  local copies, waits for them, and re-layouts  0.93 us (1%)
    pallas_call x6, Pallas kernels, call(): pl.pallas_call(kernel, out_shape=shapes, in_specs=[pl.BlockSpec(memory_sp...  17.3 us
    ppermute x2, starting transfers between devices, body(): across = lax.ppermute(to_border, 'space', over_border)  13.6 us
    all_to_all x1, blocking collectives, body(): tiles = lax.all_to_all(tiles, 'angle', 0, 0, axis_index_groups=beside_x)  10.5 us
    ppermute x1, starting transfers between devices, body(): far = lax.ppermute(far, 'angle', swapped(2))  5.81 us
    ppermute x2, waiting for transfers between devices, body(): across = lax.ppermute(to_border, 'space', over_border)  4.48 us
    ppermute x2, starting transfers between devices, body(): beside = lax.ppermute(to_core, 'space', in_chip)  3.84 us
    ppermute x1, starting transfers between devices, body(): block3 = lax.ppermute(block3, 'angle', swapped(3))  3.08 us
    ppermute x1, waiting for transfers between devices, body(): block1 = lax.ppermute(block1, 'angle', swapped(1))  2.7 us
  transfers between devices with their start and end apart: 7, of which 2 were waited for; matrix products, arithmetic and copies ran while one was open for 0% of the time, Pallas kernels for 11%

profile of v6, /device:TPU:57, one launch (start us, length us, event | category | flops | bytes accessed | tf_op | source)
XLA Modules:
  0.0 65.0 jit_solution(7326960634083693968)
XLA Ops:
  0.0 0.6 pad_add_fusion.where_ref
  0.6 2.8 %shard_map.46 = (f32[48,640]{1,0:T(8,128)}, f32[48,640]{1,0:T(8,128)}, f32[2,32,640]{2,1,0:T(8,128)}, f32[2,32,640]{2,1,0:T(8,128)}) custom-call(s32[3]{0:T(128)} %pad_add_fusion.where_ref, f32[1,2]{1,0:T(1,128)} %tilts_ref.3, f32[2,32,2048]{2,1,0:T(8,128)} %phase_ref.1, f32[1,2,32,2048]{3,2,1,0:T(8,128)} %measured_ref.3), custom_call_target="tpu_custom_call" | custom-call | bytes 1622016 | tf_op jit(solution)/shard_map/pallas_call | solution.py:320
  3.5 5.8 %collective-permute-start.4 = (f32[2,32,640]{2,1,0:T(8,128)}, f32[2,32,640]{2,1,0:T(8,128)S(1)}, u32[]{:S(2)}, u32[]{:S(2)}) collective-permute-start(f32[2,32,640]{2,1,0:T(8,128)} %get-tuple-element.32), channel_id=1, source_target_pairs={{0,8},{1,9},{2,10},{3,11},{4,12},{5,13},{6,14},{7,15},{8,0},{9,1},... | collective-permute-start | bytes 491528 | tf_op jit(solution)/shard_map/ppermute | solution.py:361
  9.3 0.0 copy-start.4
  9.3 8.9 %collective-permute-start.2 = (f32[48,640]{1,0:T(8,128)}, f32[48,640]{1,0:T(8,128)S(1)}, u32[]{:S(2)}, u32[]{:S(2)}) collective-permute-start(f32[48,640]{1,0:T(8,128)} %get-tuple-element.28), channel_id=1, source_target_pairs={{16,32},{48,64},{80,96},{112,128},{144,160},{176,192},{208,224},{2... | collective-permute-start | bytes 368648 | tf_op jit(solution)/shard_map/ppermute | solution.py:363
  18.2 0.0 copy-start.3
  18.2 1.9 %collective-permute-start.3 = (f32[48,640]{1,0:T(8,128)}, f32[48,640]{1,0:T(8,128)S(1)}, u32[]{:S(2)}, u32[]{:S(2)}) collective-permute-start(f32[48,640]{1,0:T(8,128)} %get-tuple-element.29), channel_id=1, source_target_pairs={{0,16},{32,48},{64,80},{96,112},{128,144},{160,176},{192,208},{224... | collective-permute-start | bytes 368648 | tf_op jit(solution)/shard_map/ppermute | solution.py:362
  20.2 0.9 %copy-done.1 = f32[2,32,640]{2,1,0:T(8,128)S(1)} copy-done((f32[2,32,640]{2,1,0:T(8,128)S(1)}, f32[2,32,640]{2,1,0:T(8,128)}, u32[]{:S(2)}) %copy-start.1) | copy-done | bytes 163864
  21.1 1.7 %shard_map.47 = (f32[2,32,640]{2,1,0:T(8,128)S(1)}, f32[2,32,640]{2,1,0:T(8,128)S(1)}, f32[2,32,640]{2,1,0:T(8,128)S(1)}, f32[2,2,32,640]{3,2,1,0:T(8,128)S(1)},...) custom-call(s32[3]{0:T(128)S(1)} %copy-done.2, ...), custom_call_target="tpu_custom_call" | custom-call | flops 10000000 | bytes 2981888 | tf_op jit(solution)/shard_map/pallas_call | solution.py:320
  22.8 3.1 %collective-permute-start = (f32[2,32,640]{2,1,0:T(8,128)S(1)}, f32[2,32,640]{2,1,0:T(8,128)S(1)}, u32[]{:S(2)}, u32[]{:S(2)}) collective-permute-start(f32[2,32,640]{2,1,0:T(8,128)S(1)} %get-tuple-element.26), channel_id=1, source_target_pairs={{0,12},{1,13},{2,14},{3,15},{4,8},{5,9},{6,10},{7,11},{8,4},{9,5},... | collective-permute-start | bytes 491528 | tf_op jit(solution)/shard_map/ppermute | solution.py:384
  25.9 1.9 %collective-permute-start.1 = (f32[2,32,640]{2,1,0:T(8,128)S(1)}, f32[2,32,640]{2,1,0:T(8,128)S(1)}, u32[]{:S(2)}, u32[]{:S(2)}) collective-permute-start(f32[2,32,640]{2,1,0:T(8,128)S(1)} %get-tuple-element.27), channel_id=1, source_target_pairs={{0,4},{1,5},{2,6},{3,7},{4,0},{5,1},{6,2},{7,3},{8,12},{9,13},{10,... | collective-permute-start | bytes 491528 | tf_op jit(solution)/shard_map/ppermute | solution.py:383
  27.8 0.0 collective-permute-done.2.across_ref
  27.8 0.0 collective-permute-done.3.beside_ref
  27.8 0.0 collective-permute-done.4.far_ref
  27.9 5.6 %shard_map.48 = (f32[2,96,768]{2,1,0:T(8,128)S(1)}, f32[2,64,640]{2,1,0:T(8,128)S(1)}, f32[96,512]{1,0:T(8,128)S(1)}, f32[64,640]{1,0:T(8,128)S(1)}) custom-call(s32[3]{0:T(128)S(1)} %copy-done.2, f32[48,640]{1,0:T(8,128)S(1)} %collective-permute-done.2.across_ref, f32[48,640]{1,0:T(8,128)S(1)} %collective-permute-done.3.beside_ref, ...), custom_call_target="tpu_custom_call" | custom-call | flops 4000000000 | bytes 3653632 | tf_op jit(solution)/shard_map/pallas_call | solution.py:320
  33.5 0.0 collective-permute-done.near_ref
  33.5 2.7 %collective-permute-done.1.far_ref = f32[2,32,640]{2,1,0:T(8,128)S(1)} collective-permute-done((f32[2,32,640]{2,1,0:T(8,128)S(1)}, f32[2,32,640]{2,1,0:T(8,128)S(1)}, u32[]{:S(2)}, u32[]{:S(2)}) %collective-permute-start.1) | collective-permute-done | bytes 163872 | tf_op jit(solution)/shard_map/ppermute | solution.py:383
  36.2 5.4 %shard_map.49 = f32[4,160,128]{2,1,0:T(8,128)S(1)} custom-call(s32[3]{0:T(128)S(1)} %copy-done.2, f32[2,32,640]{2,1,0:T(8,128)S(1)} %collective-permute-done.near_ref, f32[2,32,640]{2,1,0:T(8,128)S(1)} %collective-permute-done.1.far_ref, f32[96,512]{1,0:T(8,128)S(1)} %get-tuple-element.38.total0_ref, f32[64,640]{1,0:T(8,128)S(1)} %get-tuple-element.39.total1_ref, ...), custom_call_target="tpu_custom_call" | custom-call | flops 4000000000 | bytes 3407872 | tf_op jit(solution)/shard_map/pallas_call | solution.py:320
  41.7 10.5 %all_to_all.5.tiles_ref = f32[4,160,128]{2,1,0:T(8,128)S(1)} all-to-all(f32[4,160,128]{2,1,0:T(8,128)S(1)} %shard_map.49), channel_id=1, replica_groups={{0,1,2,3},{4,5,6,7},{8,9,10,11},{12,13,14,15},{16,17,18,19},{20,21,22,2..., dimensions={0} | all-to-all | bytes 655360 | tf_op jit(solution)/shard_map/all_to_all | solution.py:405
  52.1 0.6 shard_map.50
  52.7 4.8 %collective-permute-start.5 = (f32[48,128]{1,0:T(8,128)S(1)}, f32[48,128]{1,0:T(8,128)S(1)}, u32[]{:S(2)}, u32[]{:S(2)}) collective-permute-start(f32[48,128]{1,0:T(8,128)S(1)} %get-tuple-element.43), channel_id=1, source_target_pairs={{16,32},{48,64},{80,96},{112,128},{144,160},{176,192},{208,224},{2... | collective-permute-start | bytes 73736 | tf_op jit(solution)/shard_map/ppermute | solution.py:414
  57.5 1.9 %collective-permute-start.6 = (f32[48,128]{1,0:T(8,128)S(1)}, f32[48,128]{1,0:T(8,128)S(1)}, u32[]{:S(2)}, u32[]{:S(2)}) collective-permute-start(f32[48,128]{1,0:T(8,128)S(1)} %get-tuple-element.44), channel_id=1, source_target_pairs={{0,16},{32,48},{64,80},{96,112},{128,144},{160,176},{192,208},{224... | collective-permute-start | bytes 73736 | tf_op jit(solution)/shard_map/ppermute | solution.py:413
  59.4 4.5 %collective-permute-done.5.across_ref = f32[48,128]{1,0:T(8,128)S(1)} collective-permute-done((f32[48,128]{1,0:T(8,128)S(1)}, f32[48,128]{1,0:T(8,128)S(1)}, u32[]{:S(2)}, u32[]{:S(2)}) %collective-permute-start.5) | collective-permute-done | bytes 24608 | tf_op jit(solution)/shard_map/ppermute | solution.py:414
  63.9 1.2 %shard_map.51 = f32[2,32,128]{2,1,0:T(8,128)} custom-call(s32[3]{0:T(128)S(1)} %copy-done.2, f32[2,32,128]{2,1,0:T(8,128)S(1)} %get-tuple-element.42.own_ref, f32[48,128]{1,0:T(8,128)S(1)} %collective-permute-done.5.across_ref, f32[48,128]{1,0:T(8,128)S(1)} %collective-permute-done.6.beside_ref), custom_call_target="tpu_custom_call" | custom-call | bytes 114688 | tf_op jit(solution)/shard_map/pallas_call | solution.py:320
  (8 shorter events, 0.0 us)
Async XLA Ops:
  0.6 19.5 %copy-start = (f32[1,2,32,2048]{3,2,1,0:T(8,128)S(1)}, f32[1,2,32,2048]{3,2,1,0:T(8,128)}, u32[]{:S(2)}) copy-start(f32[1,2,32,2048]{3,2,1,0:T(8,128)} %measured_ref.3) | copy-start | bytes 1572868
  3.5 24.4 %collective-permute-start.4 = (f32[2,32,640]{2,1,0:T(8,128)}, f32[2,32,640]{2,1,0:T(8,128)S(1)}, u32[]{:S(2)}, u32[]{:S(2)}) collective-permute-start(f32[2,32,640]{2,1,0:T(8,128)} %get-tuple-element.32), channel_id=1, source_target_pairs={{0,8},{1,9},{2,10},{3,11},{4,12},{5,13},{6,14},{7,15},{8,0},{9,1},... | collective-permute-start | bytes 491528 | tf_op jit(solution)/shard_map/ppermute | solution.py:361
  9.3 10.9 %copy-start.4 = (f32[2,2,33]{2,1,0:T(2,128)S(1)}, f32[2,2,33]{2,1,0:T(2,128)}, u32[]{:S(2)}) copy-start(f32[2,2,33]{2,1,0:T(2,128)} %taps_ref.1) | copy-start | bytes 1588
  9.3 18.5 %collective-permute-start.2 = (f32[48,640]{1,0:T(8,128)}, f32[48,640]{1,0:T(8,128)S(1)}, u32[]{:S(2)}, u32[]{:S(2)}) collective-permute-start(f32[48,640]{1,0:T(8,128)} %get-tuple-element.28), channel_id=1, source_target_pairs={{16,32},{48,64},{80,96},{112,128},{144,160},{176,192},{208,224},{2... | collective-permute-start | bytes 368648 | tf_op jit(solution)/shard_map/ppermute | solution.py:363
  18.2 2.0 %copy-start.2 = (s32[3]{0:T(128)S(1)}, s32[3]{0:T(128)}, u32[]{:S(2)}) copy-start(s32[3]{0:T(128)} %pad_add_fusion.where_ref) | copy-start | bytes 40
  18.2 2.0 %copy-start.3 = (f32[1,2]{1,0:T(1,128)S(1)}, f32[1,2]{1,0:T(1,128)}, u32[]{:S(2)}) copy-start(f32[1,2]{1,0:T(1,128)} %tilts_ref.3) | copy-start | bytes 28
  18.2 9.6 %collective-permute-start.3 = (f32[48,640]{1,0:T(8,128)}, f32[48,640]{1,0:T(8,128)S(1)}, u32[]{:S(2)}, u32[]{:S(2)}) collective-permute-start(f32[48,640]{1,0:T(8,128)} %get-tuple-element.29), channel_id=1, source_target_pairs={{0,16},{32,48},{64,80},{96,112},{128,144},{160,176},{192,208},{224... | collective-permute-start | bytes 368648 | tf_op jit(solution)/shard_map/ppermute | solution.py:362
  20.2 0.9 %copy-start.1 = (f32[2,32,640]{2,1,0:T(8,128)S(1)}, f32[2,32,640]{2,1,0:T(8,128)}, u32[]{:S(2)}) copy-start(f32[2,32,640]{2,1,0:T(8,128)} %get-tuple-element.25.own_ref) | copy-start | bytes 491524
  22.8 10.7 %collective-permute-start = (f32[2,32,640]{2,1,0:T(8,128)S(1)}, f32[2,32,640]{2,1,0:T(8,128)S(1)}, u32[]{:S(2)}, u32[]{:S(2)}) collective-permute-start(f32[2,32,640]{2,1,0:T(8,128)S(1)} %get-tuple-element.26), channel_id=1, source_target_pairs={{0,12},{1,13},{2,14},{3,15},{4,8},{5,9},{6,10},{7,11},{8,4},{9,5},... | collective-permute-start | bytes 491528 | tf_op jit(solution)/shard_map/ppermute | solution.py:384
  25.9 10.3 %collective-permute-start.1 = (f32[2,32,640]{2,1,0:T(8,128)S(1)}, f32[2,32,640]{2,1,0:T(8,128)S(1)}, u32[]{:S(2)}, u32[]{:S(2)}) collective-permute-start(f32[2,32,640]{2,1,0:T(8,128)S(1)} %get-tuple-element.27), channel_id=1, source_target_pairs={{0,4},{1,5},{2,6},{3,7},{4,0},{5,1},{6,2},{7,3},{8,12},{9,13},{10,... | collective-permute-start | bytes 491528 | tf_op jit(solution)/shard_map/ppermute | solution.py:383
  52.7 11.2 %collective-permute-start.5 = (f32[48,128]{1,0:T(8,128)S(1)}, f32[48,128]{1,0:T(8,128)S(1)}, u32[]{:S(2)}, u32[]{:S(2)}) collective-permute-start(f32[48,128]{1,0:T(8,128)S(1)} %get-tuple-element.43), channel_id=1, source_target_pairs={{16,32},{48,64},{80,96},{112,128},{144,160},{176,192},{208,224},{2... | collective-permute-start | bytes 73736 | tf_op jit(solution)/shard_map/ppermute | solution.py:414
  57.5 6.4 %collective-permute-start.6 = (f32[48,128]{1,0:T(8,128)S(1)}, f32[48,128]{1,0:T(8,128)S(1)}, u32[]{:S(2)}, u32[]{:S(2)}) collective-permute-start(f32[48,128]{1,0:T(8,128)S(1)} %get-tuple-element.44), channel_id=1, source_target_pairs={{0,16},{32,48},{64,80},{96,112},{128,144},{160,176},{192,208},{224... | collective-permute-start | bytes 73736 | tf_op jit(solution)/shard_map/ppermute | solution.py:413

commit v7 on v5

--- a/solution.py
+++ b/solution.py
@@ -172,7 +172,7 @@
     blank = jnp.zeros(room_ref.shape[:2] + (TILE,), F32)
     room_ref[:, :, :TILE] = blank
     room_ref[:, :, TILE + columns :] = blank
-    copy.wait()
+    return copy
 
 
 def block_of(room_ref, part, block):
@@ -182,18 +182,20 @@
 
 def pack_phase(where_ref, phase_ref, border_ref, core_ref, own_ref, room_ref, semaphore):
     even = where_ref[1] == 0
-    padded_columns(phase_ref, room_ref, semaphore)
+    padded_columns(phase_ref, room_ref, semaphore).wait()
+    low, high = slice(0, REACH), slice(ROWS - REACH, ROWS)
+    border_ref[:ROWS] = block_of(room_ref, 0, where_ref[3])
+    slice1 = block_of(room_ref, 1, where_ref[3])
+    border_ref[ROWS:] = jnp.where(even, slice1[low], slice1[high])
     own_ref[0] = block_of(room_ref, 0, where_ref[2])
     own_ref[1] = block_of(room_ref, 1, where_ref[2])
-    low, high = own_ref[1, :REACH], own_ref[1, ROWS - REACH :]
-    for ref, nearest in ((border_ref, jnp.where(even, low, high)), (core_ref, jnp.where(even, high, low))):
-        ref[:ROWS] = own_ref[0]
-        ref[ROWS:] = nearest
-
-
-def pack_measured(where_ref, tilts_ref, measured_ref, *refs):
+    core_ref[:ROWS] = own_ref[0]
+    core_ref[ROWS:] = jnp.where(even, own_ref[1, high], own_ref[1, low])
+
+
+def pack_measured(where_ref, tilts_ref, measured_ref, after_ref, *refs):
     block_refs, room_ref, semaphore = refs[:GROUP], refs[GROUP], refs[GROUP + 1]
-    padded_columns(measured_ref.at[0], room_ref, semaphore)
+    padded_columns(measured_ref.at[0], room_ref, semaphore).wait()
     lane = lax.broadcasted_iota(jnp.int32, (8, TILE), 1)
     row = lax.broadcasted_iota(jnp.int32, (8, TILE), 0)
     for shift, ref in enumerate(block_refs):
@@ -269,10 +271,15 @@
     )
 
 
-def other_angles(where_ref, *refs):
-    measured_refs, (total0_ref, total1_ref), rest = refs[: GROUP - 1], refs[GROUP - 1 : GROUP + 1], refs[GROUP + 1 : -1]
+def next_angle(where_ref, measured_ref, total0_ref, total1_ref, *refs):
+    term0, term1 = sweep(where_ref, [measured_ref], *refs[:-2])
+    refs[-2][...] = total0_ref[...] + term0
+    refs[-1][...] = total1_ref[...] + term1
+
+
+def last_angles(where_ref, near_ref, far_ref, total0_ref, total1_ref, *refs):
     out_ref = refs[-1]
-    term0, term1 = sweep(where_ref, measured_refs, *rest)
+    term0, term1 = sweep(where_ref, [near_ref, far_ref], *refs[:-1])
     total0, total1 = total0_ref[...] + term0, total1_ref[...] + term1
     total1 = total1[:, TILE // 2 : TILE // 2 + BLOCK]
     for j in range(BLOCK // TILE):
@@ -301,14 +308,14 @@
     out_ref[1, REACH:] = own_ref[1, REACH:] + above[ROWS:]
 
 
-def call(kernel, shapes, scalars, arrays, flops, scratch=(), space=pltpu.VMEM):
+def call(kernel, shapes, scalars, arrays, flops, scratch=()):
     moved = sum(a.size * a.dtype.itemsize for a in arrays)
     moved += sum(int(s.size) * s.dtype.itemsize for s in shapes)
     return pl.pallas_call(
         kernel,
         out_shape=shapes,
         in_specs=[pl.BlockSpec(memory_space=pltpu.SMEM)] * len(scalars)
-        + [pl.BlockSpec(memory_space=space)] * len(arrays),
+        + [pl.BlockSpec(memory_space=pltpu.VMEM)] * len(arrays),
         out_specs=[pl.BlockSpec(memory_space=pltpu.VMEM)] * len(shapes),
         scratch_shapes=list(scratch),
         compiler_params=pltpu.CompilerParams(vmem_limit_bytes=VMEM_LIMIT),
@@ -326,9 +333,19 @@
     along = lax.axis_size("angle") // GROUP
     strip = lax.axis_index("space")
     block = lax.axis_index("angle") // along
-    where = jnp.stack([strip * ROWS, strip & 1, block]).astype(jnp.int32)
+    middle = strips // 2
+    far = (strip == middle - 1) | (strip == middle)
+    where = jnp.stack([strip * ROWS, strip & 1, block, jnp.where(far, GROUP - 1 - block, block)]).astype(jnp.int32)
     over_border = swaps([(i, i + 1) for i in range(1, strips - 1, 2)])
     in_chip = swaps([(i, i + 1) for i in range(0, strips, 2)])
+    over_border_nearest = swaps(
+        [
+            ((i * GROUP + g) * along + j, ((i + 1) * GROUP + (GROUP - 1 - g if i + 1 == middle else g)) * along + j)
+            for i in range(1, strips - 1, 2)
+            for g in range(GROUP)
+            for j in range(along)
+        ]
+    )
 
     def swapped(shift):
         return [(g * along + i, (g ^ shift) * along + i) for g in range(GROUP) for i in range(along)]
@@ -342,20 +359,15 @@
         [phase_delay],
         0,
         room,
-        pltpu.HBM,
     )
     beside = lax.ppermute(to_core, "space", in_chip)
-    across = lax.ppermute(to_border, "space", over_border)
+    across = lax.ppermute(to_border, ("space", "angle"), over_border_nearest)
     blocks = call(
-        pack_measured,
-        [struct((2, ROWS, FRAME1), F32)] * GROUP,
-        [where, tilts],
-        [measured],
-        0,
-        room,
-        pltpu.HBM,
-    )
-    arrived = [lax.ppermute(blocks[shift], "angle", swapped(shift)) for shift in range(1, GROUP)]
+        pack_measured, [struct((2, ROWS, FRAME1), F32)] * GROUP, [where, tilts], [measured, own_phase], 0, room
+    )
+    near, block1, block2, block3 = [blocks[0]] + [
+        lax.ppermute(blocks[shift], "angle", swapped(shift)) for shift in range(1, GROUP)
+    ]
     own, *matrices = call(
         prepare,
         [
@@ -370,24 +382,23 @@
         [own_phase],
         10_000_000,
     )
+    totals = [struct((WIDEST, BLOCK), F32), struct((WIDE, FRAME1), F32)]
     turn0, turn1, total0, total1 = call(
         functools.partial(first_angle, total_rows=total_rows),
-        [
-            struct((2, WIDEST, FRAME0), F32),
-            struct((2, WIDE, FRAME1), F32),
-            struct((WIDEST, BLOCK), F32),
-            struct((WIDE, FRAME1), F32),
-        ],
+        [struct((2, WIDEST, FRAME0), F32), struct((2, WIDE, FRAME1), F32)] + totals,
         [where],
-        [across, beside, own, blocks[0], *matrices],
+        [across, beside, own, near, *matrices],
         2_000_000_000,
     )
+    total0, total1 = call(
+        next_angle, totals, [where], [block1, total0, total1, turn0, turn1, *matrices], 2_000_000_000
+    )
     (tiles,) = call(
-        other_angles,
+        last_angles,
         [struct((BLOCK // TILE, WIDEST + WIDE, TILE), F32)],
         [where],
-        [*arrived, total0, total1, turn0, turn1, *matrices],
-        6_000_000_000,
+        [block2, block3, total0, total1, turn0, turn1, *matrices],
+        4_000_000_000,
     )
     beside_x = [[g * along + i for i in range(along)] for g in range(GROUP)]
     tiles = lax.all_to_all(tiles, "angle", 0, 0, axis_index_groups=beside_x)

time: 65.5 us -> 67.5 us (1.031)
  the two profiles are of different devices: /device:TPU:121 before, /device:TPU:57 now
where the time goes in v7:
time: 67.5 us; the launch traced here: 67.1 us
  starting transfers between devices  28.8 us (43%)
  Pallas kernels  17.6 us (26%)
  blocking collectives  10.5 us (16%)
  waiting for transfers between devices  8.91 us (13%)
  local copies, waits for them, and re-layouts  1.06 us (2%)
    pallas_call x8, Pallas kernels, call(): pl.pallas_call(kernel, out_shape=shapes, in_specs=[pl.BlockSpec(memory_sp...  17.6 us
    all_to_all x1, blocking collectives, body(): tiles = lax.all_to_all(tiles, 'angle', 0, 0, axis_index_groups=beside_x)  10.5 us
    ppermute x1, starting transfers between devices, body(): across = lax.ppermute(to_border, ('space', 'angle'), over_border_nearest)  10.4 us
    ppermute x3, starting transfers between devices, body(): lax.ppermute(blocks[shift], 'angle', swapped(shift))  8.99 us
    ppermute x1, starting transfers between devices, body(): across = lax.ppermute(to_border, 'space', over_border)  5.52 us
    ppermute x3, waiting for transfers between devices, body(): lax.ppermute(blocks[shift], 'angle', swapped(shift))  5.19 us
    ppermute x2, starting transfers between devices, body(): beside = lax.ppermute(to_core, 'space', in_chip)  3.84 us
    ppermute x1, waiting for transfers between devices, body(): across = lax.ppermute(to_border, 'space', over_border)  3.71 us
  transfers between devices with their start and end apart: 7, of which 2 were waited for; matrix products, arithmetic and copies ran while one was open for 0% of the time, Pallas kernels for 14%

profile of v7, /device:TPU:57, one launch (start us, length us, event | category | flops | bytes accessed | tf_op | source)
XLA Modules:
  0.0 67.1 jit_solution(6237595063556088460)
XLA Ops:
  0.0 0.1 pad_add_fusion.where_ref
  0.1 1.0 %copy-done = f32[2,32,2048]{2,1,0:T(8,128)S(1)} copy-done((f32[2,32,2048]{2,1,0:T(8,128)S(1)}, f32[2,32,2048]{2,1,0:T(8,128)}, u32[]{:S(2)}) %copy-start) | copy-done | bytes 524312
  1.1 0.8 %shard_map.46 = (f32[48,640]{1,0:T(8,128)S(1)}, f32[48,640]{1,0:T(8,128)S(1)}, f32[2,32,640]{2,1,0:T(8,128)S(1)}) custom-call(s32[4]{0:T(128)S(1)} %pad_add_fusion.where_ref, f32[2,32,2048]{2,1,0:T(8,128)S(1)} %copy-done), custom_call_target="tpu_custom_call" | custom-call | bytes 933888 | tf_op jit(solution)/shard_map/pallas_call | solution.py:314
  1.9 10.4 %collective-permute-start.3 = (f32[48,640]{1,0:T(8,128)S(1)}, f32[48,640]{1,0:T(8,128)S(1)}, u32[]{:S(2)}, u32[]{:S(2)}) collective-permute-start(f32[48,640]{1,0:T(8,128)S(1)} %get-tuple-element.31), channel_id=1, source_target_pairs={{16,32},{17,33},{18,34},{19,35},{20,36},{21,37},{22,38},{23,39},{2... | collective-permute-start | bytes 368648 | tf_op jit(solution)/shard_map/ppermute | solution.py:364
  12.3 0.0 copy-start.3
  12.3 1.9 %collective-permute-start.4 = (f32[48,640]{1,0:T(8,128)S(1)}, f32[48,640]{1,0:T(8,128)S(1)}, u32[]{:S(2)}, u32[]{:S(2)}) collective-permute-start(f32[48,640]{1,0:T(8,128)S(1)} %get-tuple-element.32), channel_id=1, source_target_pairs={{0,16},{32,48},{64,80},{96,112},{128,144},{160,176},{192,208},{224... | collective-permute-start | bytes 368648 | tf_op jit(solution)/shard_map/ppermute | solution.py:363
  14.3 0.9 %shard_map.47 = (f32[2,32,640]{2,1,0:T(8,128)S(1)}, f32[2,32,640]{2,1,0:T(8,128)S(1)}, f32[2,32,640]{2,1,0:T(8,128)S(1)}, f32[2,32,640]{2,1,0:T(8,128)S(1)}) custom-call(s32[4]{0:T(128)S(1)} %pad_add_fusion.where_ref, f32[1,2]{1,0:T(1,128)S(1)} %copy-done.3, f32[1,2,32,2048]{3,2,1,0:T(8,128)S(1)} %copy-done.1, ...), custom_call_target="tpu_custom_call" | custom-call | bytes 1343488 | tf_op jit(solution)/shard_map/pallas_call | solution.py:314
  15.2 0.0 copy-start.2
  15.2 3.1 %collective-permute-start = (f32[2,32,640]{2,1,0:T(8,128)S(1)}, f32[2,32,640]{2,1,0:T(8,128)S(1)}, u32[]{:S(2)}, u32[]{:S(2)}) collective-permute-start(f32[2,32,640]{2,1,0:T(8,128)S(1)} %get-tuple-element.28), channel_id=1, source_target_pairs={{0,8},{1,9},{2,10},{3,11},{4,12},{5,13},{6,14},{7,15},{8,0},{9,1},... | collective-permute-start | bytes 491528 | tf_op jit(solution)/shard_map/ppermute | solution.py:369
  18.3 4.0 %collective-permute-start.1 = (f32[2,32,640]{2,1,0:T(8,128)S(1)}, f32[2,32,640]{2,1,0:T(8,128)S(1)}, u32[]{:S(2)}, u32[]{:S(2)}) collective-permute-start(f32[2,32,640]{2,1,0:T(8,128)S(1)} %get-tuple-element.29), channel_id=1, source_target_pairs={{0,12},{1,13},{2,14},{3,15},{4,8},{5,9},{6,10},{7,11},{8,4},{9,5},... | collective-permute-start | bytes 491528 | tf_op jit(solution)/shard_map/ppermute | solution.py:369
  22.3 1.9 %collective-permute-start.2 = (f32[2,32,640]{2,1,0:T(8,128)S(1)}, f32[2,32,640]{2,1,0:T(8,128)S(1)}, u32[]{:S(2)}, u32[]{:S(2)}) collective-permute-start(f32[2,32,640]{2,1,0:T(8,128)S(1)} %get-tuple-element.30), channel_id=1, source_target_pairs={{0,4},{1,5},{2,6},{3,7},{4,0},{5,1},{6,2},{7,3},{8,12},{9,13},{10,... | collective-permute-start | bytes 491528 | tf_op jit(solution)/shard_map/ppermute | solution.py:369
  24.2 1.4 %shard_map.48 = (f32[2,2,32,640]{3,2,1,0:T(8,128)S(1)}, bf16[256,192]{1,0:T(8,128)(2,1)S(1)}, bf16[128,256]{1,0:T(8,128)(2,1)S(1)}, bf16[256,128]{1,0:T(8,128)(2...) custom-call(s32[4]{0:T(128)S(1)} %pad_add_fusion.where_ref, f32[2,2,33]{2,1,0:T(2,128)S(1)} %copy-done.2, ...), custom_call_target="tpu_custom_call" | custom-call | flops 10000000 | bytes 1966080 | tf_op jit(solution)/shard_map/pallas_call | solution.py:314
  25.6 0.0 collective-permute-done.4.beside_ref
  25.7 3.8 %shard_map.49 = (f32[2,96,768]{2,1,0:T(8,128)S(1)}, f32[2,64,640]{2,1,0:T(8,128)S(1)}, f32[96,512]{1,0:T(8,128)S(1)}, f32[64,640]{1,0:T(8,128)S(1)}) custom-call(s32[4]{0:T(128)S(1)} %pad_add_fusion.where_ref, f32[48,640]{1,0:T(8,128)S(1)} %collective-permute-done.3.across_ref, f32[48,640]{1,0:T(8,128)S(1)} %collective-permute-done.4.beside_ref, ...), custom_call_target="tpu_custom_call" | custom-call | flops 2000000000 | bytes 3489792 | tf_op jit(solution)/shard_map/pallas_call | solution.py:314
  29.4 5.2 %collective-permute-done.2.measured_ref = f32[2,32,640]{2,1,0:T(8,128)S(1)} collective-permute-done((f32[2,32,640]{2,1,0:T(8,128)S(1)}, f32[2,32,640]{2,1,0:T(8,128)S(1)}, u32[]{:S(2)}, u32[]{:S(2)}) %collective-permute-start.2) | collective-permute-done | bytes 163872 | tf_op jit(solution)/shard_map/ppermute | solution.py:369
  34.6 3.6 %shard_map.50 = (f32[96,512]{1,0:T(8,128)S(1)}, f32[64,640]{1,0:T(8,128)S(1)}) custom-call(s32[4]{0:T(128)S(1)} %pad_add_fusion.where_ref, f32[2,32,640]{2,1,0:T(8,128)S(1)} %collective-permute-done.2.measured_ref, f32[96,512]{1,0:T(8,128)S(1)} %get-tuple-element.40.total0_ref, f32[64,640]{1,0:T(8,128)S(1)} %get-tuple-element.41.total1_ref, ...), custom_call_target="tpu_custom_call" | custom-call | flops 2000000000 | bytes 3276800 | tf_op jit(solution)/shard_map/pallas_call | solution.py:314
  38.3 0.0 collective-permute-done.near_ref
  38.3 5.5 %shard_map.51 = f32[4,160,128]{2,1,0:T(8,128)S(1)} custom-call(s32[4]{0:T(128)S(1)} %pad_add_fusion.where_ref, f32[2,32,640]{2,1,0:T(8,128)S(1)} %collective-permute-done.near_ref, f32[2,32,640]{2,1,0:T(8,128)S(1)} %collective-permute-done.1.far_ref, f32[96,512]{1,0:T(8,128)S(1)} %get-tuple-element.44.total0_ref, ...), custom_call_target="tpu_custom_call" | custom-call | flops 4000000000 | bytes 3407872 | tf_op jit(solution)/shard_map/pallas_call | solution.py:314
  43.8 10.5 %all_to_all.5.tiles_ref = f32[4,160,128]{2,1,0:T(8,128)S(1)} all-to-all(f32[4,160,128]{2,1,0:T(8,128)S(1)} %shard_map.51), channel_id=1, replica_groups={{0,1,2,3},{4,5,6,7},{8,9,10,11},{12,13,14,15},{16,17,18,19},{20,21,22,2..., dimensions={0} | all-to-all | bytes 655360 | tf_op jit(solution)/shard_map/all_to_all | solution.py:404
  54.2 0.6 shard_map.52
  54.8 5.5 %collective-permute-start.5 = (f32[48,128]{1,0:T(8,128)S(1)}, f32[48,128]{1,0:T(8,128)S(1)}, u32[]{:S(2)}, u32[]{:S(2)}) collective-permute-start(f32[48,128]{1,0:T(8,128)S(1)} %get-tuple-element.47), channel_id=1, source_target_pairs={{16,32},{48,64},{80,96},{112,128},{144,160},{176,192},{208,224},{2... | collective-permute-start | bytes 73736 | tf_op jit(solution)/shard_map/ppermute | solution.py:413
  60.3 1.9 %collective-permute-start.6 = (f32[48,128]{1,0:T(8,128)S(1)}, f32[48,128]{1,0:T(8,128)S(1)}, u32[]{:S(2)}, u32[]{:S(2)}) collective-permute-start(f32[48,128]{1,0:T(8,128)S(1)} %get-tuple-element.48), channel_id=1, source_target_pairs={{0,16},{32,48},{64,80},{96,112},{128,144},{160,176},{192,208},{224... | collective-permute-start | bytes 73736 | tf_op jit(solution)/shard_map/ppermute | solution.py:412
  62.3 3.7 %collective-permute-done.5.across_ref = f32[48,128]{1,0:T(8,128)S(1)} collective-permute-done((f32[48,128]{1,0:T(8,128)S(1)}, f32[48,128]{1,0:T(8,128)S(1)}, u32[]{:S(2)}, u32[]{:S(2)}) %collective-permute-start.5) | collective-permute-done | bytes 24608 | tf_op jit(solution)/shard_map/ppermute | solution.py:413
  66.0 1.2 %shard_map.53 = f32[2,32,128]{2,1,0:T(8,128)} custom-call(s32[4]{0:T(128)S(1)} %pad_add_fusion.where_ref, f32[2,32,128]{2,1,0:T(8,128)S(1)} %get-tuple-element.46.own_ref, f32[48,128]{1,0:T(8,128)S(1)} %collective-permute-done.5.across_ref, f32[48,128]{1,0:T(8,128)S(1)} %collective-permute-done.6.beside_ref), custom_call_target="tpu_custom_call" | custom-call | bytes 114688 | tf_op jit(solution)/shard_map/pallas_call | solution.py:314
  (8 shorter events, 0.0 us)
Async XLA Ops:
  0.1 1.0 %copy-start = (f32[2,32,2048]{2,1,0:T(8,128)S(1)}, f32[2,32,2048]{2,1,0:T(8,128)}, u32[]{:S(2)}) copy-start(f32[2,32,2048]{2,1,0:T(8,128)} %phase_ref.1) | copy-start | bytes 1572868
  1.1 13.1 %copy-start.1 = (f32[1,2,32,2048]{3,2,1,0:T(8,128)S(1)}, f32[1,2,32,2048]{3,2,1,0:T(8,128)}, u32[]{:S(2)}) copy-start(f32[1,2,32,2048]{3,2,1,0:T(8,128)} %measured_ref.1) | copy-start | bytes 1572868
  1.9 23.7 %collective-permute-start.3 = (f32[48,640]{1,0:T(8,128)S(1)}, f32[48,640]{1,0:T(8,128)S(1)}, u32[]{:S(2)}, u32[]{:S(2)}) collective-permute-start(f32[48,640]{1,0:T(8,128)S(1)} %get-tuple-element.31), channel_id=1, source_target_pairs={{16,32},{17,33},{18,34},{19,35},{20,36},{21,37},{22,38},{23,39},{2... | collective-permute-start | bytes 368648 | tf_op jit(solution)/shard_map/ppermute | solution.py:364
  12.3 2.0 %copy-start.3 = (f32[1,2]{1,0:T(1,128)S(1)}, f32[1,2]{1,0:T(1,128)}, u32[]{:S(2)}) copy-start(f32[1,2]{1,0:T(1,128)} %tilts_ref.1) | copy-start | bytes 28
  12.3 13.3 %collective-permute-start.4 = (f32[48,640]{1,0:T(8,128)S(1)}, f32[48,640]{1,0:T(8,128)S(1)}, u32[]{:S(2)}, u32[]{:S(2)}) collective-permute-start(f32[48,640]{1,0:T(8,128)S(1)} %get-tuple-element.32), channel_id=1, source_target_pairs={{0,16},{32,48},{64,80},{96,112},{128,144},{160,176},{192,208},{224... | collective-permute-start | bytes 368648 | tf_op jit(solution)/shard_map/ppermute | solution.py:363
  15.2 9.0 %copy-start.2 = (f32[2,2,33]{2,1,0:T(2,128)S(1)}, f32[2,2,33]{2,1,0:T(2,128)}, u32[]{:S(2)}) copy-start(f32[2,2,33]{2,1,0:T(2,128)} %taps_ref.1) | copy-start | bytes 1588
  15.2 23.1 %collective-permute-start = (f32[2,32,640]{2,1,0:T(8,128)S(1)}, f32[2,32,640]{2,1,0:T(8,128)S(1)}, u32[]{:S(2)}, u32[]{:S(2)}) collective-permute-start(f32[2,32,640]{2,1,0:T(8,128)S(1)} %get-tuple-element.28), channel_id=1, source_target_pairs={{0,8},{1,9},{2,10},{3,11},{4,12},{5,13},{6,14},{7,15},{8,0},{9,1},... | collective-permute-start | bytes 491528 | tf_op jit(solution)/shard_map/ppermute | solution.py:369
  18.3 20.0 %collective-permute-start.1 = (f32[2,32,640]{2,1,0:T(8,128)S(1)}, f32[2,32,640]{2,1,0:T(8,128)S(1)}, u32[]{:S(2)}, u32[]{:S(2)}) collective-permute-start(f32[2,32,640]{2,1,0:T(8,128)S(1)} %get-tuple-element.29), channel_id=1, source_target_pairs={{0,12},{1,13},{2,14},{3,15},{4,8},{5,9},{6,10},{7,11},{8,4},{9,5},... | collective-permute-start | bytes 491528 | tf_op jit(solution)/shard_map/ppermute | solution.py:369
  22.3 12.4 %collective-permute-start.2 = (f32[2,32,640]{2,1,0:T(8,128)S(1)}, f32[2,32,640]{2,1,0:T(8,128)S(1)}, u32[]{:S(2)}, u32[]{:S(2)}) collective-permute-start(f32[2,32,640]{2,1,0:T(8,128)S(1)} %get-tuple-element.30), channel_id=1, source_target_pairs={{0,4},{1,5},{2,6},{3,7},{4,0},{5,1},{6,2},{7,3},{8,12},{9,13},{10,... | collective-permute-start | bytes 491528 | tf_op jit(solution)/shard_map/ppermute | solution.py:369
  54.8 11.2 %collective-permute-start.5 = (f32[48,128]{1,0:T(8,128)S(1)}, f32[48,128]{1,0:T(8,128)S(1)}, u32[]{:S(2)}, u32[]{:S(2)}) collective-permute-start(f32[48,128]{1,0:T(8,128)S(1)} %get-tuple-element.47), channel_id=1, source_target_pairs={{16,32},{48,64},{80,96},{112,128},{144,160},{176,192},{208,224},{2... | collective-permute-start | bytes 73736 | tf_op jit(solution)/shard_map/ppermute | solution.py:413
  60.3 5.6 %collective-permute-start.6 = (f32[48,128]{1,0:T(8,128)S(1)}, f32[48,128]{1,0:T(8,128)S(1)}, u32[]{:S(2)}, u32[]{:S(2)}) collective-permute-start(f32[48,128]{1,0:T(8,128)S(1)} %get-tuple-element.48), channel_id=1, source_target_pairs={{0,16},{32,48},{64,80},{96,112},{128,144},{160,176},{192,208},{224... | collective-permute-start | bytes 73736 | tf_op jit(solution)/shard_map/ppermute | solution.py:412

commit v8 on v7

--- a/solution.py
+++ b/solution.py
@@ -15,10 +15,14 @@
 WIDEST = ROWS + 4 * REACH
 F32 = jnp.float32
 BF16 = jnp.bfloat16
+SIDE = 2 * REACH
 GROUP = 4
 BLOCK = 512
 FRAME0 = BLOCK + 2 * TILE
 FRAME1 = BLOCK + TILE
+SIDES_AT = 2 * ROWS * BLOCK // TILE
+TILTS_AT = SIDES_AT + ROWS
+MESSAGE = TILTS_AT + 8
 VMEM_LIMIT = 32 * 1024 * 1024
 
 
@@ -196,15 +200,33 @@
 def pack_measured(where_ref, tilts_ref, measured_ref, after_ref, *refs):
     block_refs, room_ref, semaphore = refs[:GROUP], refs[GROUP], refs[GROUP + 1]
     padded_columns(measured_ref.at[0], room_ref, semaphore).wait()
-    lane = lax.broadcasted_iota(jnp.int32, (8, TILE), 1)
-    row = lax.broadcasted_iota(jnp.int32, (8, TILE), 0)
+    lane = lax.broadcasted_iota(jnp.int32, (ROWS, TILE), 1)
+    tilts = jnp.where(lane[:8] == 0, tilts_ref[0, 0], tilts_ref[0, 1])
     for shift, ref in enumerate(block_refs):
-        block = where_ref[2] ^ shift
-        ref[0] = block_of(room_ref, 0, block)
-        ref[1] = block_of(room_ref, 1, block)
-        corner = ref[0, :8, :TILE]
-        corner = jnp.where((row == 0) & (lane == 0), tilts_ref[0, 0], corner)
-        ref[0, :8, :TILE] = jnp.where((row == 0) & (lane == 1), tilts_ref[0, 1], corner)
+        start = (where_ref[2] ^ shift) * BLOCK
+
+        def tile(part, index):
+            return room_ref[part, :, pl.ds(pl.multiple_of(start + index * TILE, TILE), TILE)]
+
+        for part in range(2):
+            for j in range(BLOCK // TILE):
+                ref[pl.ds((part * (BLOCK // TILE) + j) * ROWS, ROWS)] = tile(part, 1 + j)
+        sides = [
+            pltpu.roll(tile(part, index), SIDE + 2 * SIDE * part, 1)
+            for part in range(2)
+            for index in (0, 1 + BLOCK // TILE)
+        ]
+        left, right = jnp.where(lane < SIDE, sides[0], sides[1]), jnp.where(lane < 3 * SIDE, sides[2], sides[3])
+        ref[pl.ds(SIDES_AT, ROWS)] = jnp.where(lane < 2 * SIDE, left, right)
+        ref[pl.ds(TILTS_AT, 8)] = tilts
+
+
+def measured_part(ref, part):
+    lane = lax.broadcasted_iota(jnp.int32, (ROWS, TILE), 1)
+    sides = pltpu.roll(ref[pl.ds(SIDES_AT, ROWS)], 3 * SIDE - 2 * SIDE * part, 1)
+    tiles = [ref[pl.ds((part * (BLOCK // TILE) + j) * ROWS, ROWS)] for j in range(BLOCK // TILE)]
+    left, right = jnp.where(lane >= TILE - SIDE, sides, 0.0), jnp.where(lane < SIDE, sides, 0.0)
+    return jnp.concatenate([left, *tiles, right], axis=1)
 
 
 def prepare(where_ref, taps_ref, own_ref, turn_ref, into1_ref, into2_ref, out1_ref, out2_ref, band_ref):
@@ -238,8 +260,8 @@
     cos0, sin0, cos1, sin1 = turn0_ref[0], turn0_ref[1], turn1_ref[0], turn1_ref[1]
     waves0 = []
     for measured_ref in measured_refs:
-        cos_r, sin_r = cos_sin(measured_ref[0, :1, :1] * row)
-        cos_c, sin_c = cos_sin(measured_ref[0, :1, 1:2] * column.astype(F32))
+        cos_r, sin_r = cos_sin(measured_ref[TILTS_AT : TILTS_AT + 1, :1] * row)
+        cos_c, sin_c = cos_sin(measured_ref[TILTS_AT : TILTS_AT + 1, 1:2] * column.astype(F32))
         cos_r, sin_r, cos_c, sin_c = cos_r[:, :1], sin_r[:, :1], cos_c[:1], sin_c[:1]
         left_r, left_i = cos0 * cos_r - sin0 * sin_r, sin0 * cos_r + cos0 * sin_r
         waves0.append((left_r * cos_c - left_i * sin_c, left_r * sin_c + left_i * cos_c))
@@ -247,7 +269,7 @@
     waves1 = [(cos1 * real - sin1 * imag, cos1 * imag + sin1 * real) for real, imag in fields]
     fields = column_pass(row_pass(waves1, into2_ref), band_ref, 0, FRAME0 // TILE, -1)
     fields = [
-        inside_grid(where_ref, real - half_tile(measured_ref[0]), imag - half_tile(measured_ref[1]))
+        inside_grid(where_ref, real - measured_part(measured_ref, 0), imag - measured_part(measured_ref, 1))
         for (real, imag), measured_ref in zip(fields, measured_refs)
     ]
     fields = row_pass(column_pass(fields, band_ref, 1, FRAME1 // TILE, 0), out1_ref)
@@ -363,7 +385,7 @@
     beside = lax.ppermute(to_core, "space", in_chip)
     across = lax.ppermute(to_border, ("space", "angle"), over_border_nearest)
     blocks = call(
-        pack_measured, [struct((2, ROWS, FRAME1), F32)] * GROUP, [where, tilts], [measured, own_phase], 0, room
+        pack_measured, [struct((MESSAGE, TILE), F32)] * GROUP, [where, tilts], [measured, own_phase], 0, room
     )
     near, block1, block2, block3 = [blocks[0]] + [
         lax.ppermute(blocks[shift], "angle", swapped(shift)) for shift in range(1, GROUP)
@@ -388,7 +410,7 @@
         [struct((2, WIDEST, FRAME0), F32), struct((2, WIDE, FRAME1), F32)] + totals,
         [where],
         [across, beside, own, near, *matrices],
-        2_000_000_000,
+        800_000_000,
     )
     total0, total1 = call(
         next_angle, totals, [where], [block1, total0, total1, turn0, turn1, *matrices], 2_000_000_000

time: 67.5 us -> 63.3 us (0.938)
  the two profiles are of different devices: /device:TPU:57 before, /device:TPU:121 now
where the time goes in v8:
time: 63.3 us; the launch traced here: 62.9 us
  starting transfers between devices  26.5 us (42%)
  Pallas kernels  17.5 us (28%)
  blocking collectives  10 us (16%)
  waiting for transfers between devices  7.56 us (12%)
  local copies, waits for them, and re-layouts  1.06 us (2%)
    pallas_call x8, Pallas kernels, call(): pl.pallas_call(kernel, out_shape=shapes, in_specs=[pl.BlockSpec(memory_sp...  17.5 us
    all_to_all x1, blocking collectives, body(): tiles = lax.all_to_all(tiles, 'angle', 0, 0, axis_index_groups=beside_x)  10 us
    ppermute x1, starting transfers between devices, body(): across = lax.ppermute(to_border, ('space', 'angle'), over_border_nearest)  9.51 us
    ppermute x3, starting transfers between devices, body(): lax.ppermute(blocks[shift], 'angle', swapped(shift))  8.37 us
    ppermute x1, starting transfers between devices, body(): across = lax.ppermute(to_border, 'space', over_border)  4.82 us
    ppermute x1, waiting for transfers between devices, body(): across = lax.ppermute(to_border, 'space', over_border)  4.41 us
    ppermute x2, starting transfers between devices, body(): beside = lax.ppermute(to_core, 'space', in_chip)  3.84 us
    ppermute x3, waiting for transfers between devices, body(): lax.ppermute(blocks[shift], 'angle', swapped(shift))  3.14 us
  transfers between devices with their start and end apart: 7, of which 2 were waited for; matrix products, arithmetic and copies ran while one was open for 0% of the time, Pallas kernels for 15%

profile of v8, /device:TPU:121, one launch (start us, length us, event | category | flops | bytes accessed | tf_op | source)
XLA Modules:
  0.0 62.9 jit_solution(2446773795669013917)
XLA Ops:
  0.0 0.1 pad_add_fusion.where_ref
  0.1 1.0 %copy-done = f32[2,32,2048]{2,1,0:T(8,128)S(1)} copy-done((f32[2,32,2048]{2,1,0:T(8,128)S(1)}, f32[2,32,2048]{2,1,0:T(8,128)}, u32[]{:S(2)}) %copy-start) | copy-done | bytes 524312
  1.1 0.8 %shard_map.46 = (f32[48,640]{1,0:T(8,128)S(1)}, f32[48,640]{1,0:T(8,128)S(1)}, f32[2,32,640]{2,1,0:T(8,128)S(1)}) custom-call(s32[4]{0:T(128)S(1)} %pad_add_fusion.where_ref, f32[2,32,2048]{2,1,0:T(8,128)S(1)} %copy-done), custom_call_target="tpu_custom_call" | custom-call | bytes 933888 | tf_op jit(solution)/shard_map/pallas_call | solution.py:336
  1.9 9.5 %collective-permute-start.3 = (f32[48,640]{1,0:T(8,128)S(1)}, f32[48,640]{1,0:T(8,128)S(1)}, u32[]{:S(2)}, u32[]{:S(2)}) collective-permute-start(f32[48,640]{1,0:T(8,128)S(1)} %get-tuple-element.31), channel_id=1, source_target_pairs={{16,32},{17,33},{18,34},{19,35},{20,36},{21,37},{22,38},{23,39},{2... | collective-permute-start | bytes 368648 | tf_op jit(solution)/shard_map/ppermute | solution.py:386
  11.4 0.0 copy-start.3
  11.4 1.9 %collective-permute-start.4 = (f32[48,640]{1,0:T(8,128)S(1)}, f32[48,640]{1,0:T(8,128)S(1)}, u32[]{:S(2)}, u32[]{:S(2)}) collective-permute-start(f32[48,640]{1,0:T(8,128)S(1)} %get-tuple-element.32), channel_id=1, source_target_pairs={{0,16},{32,48},{64,80},{96,112},{128,144},{160,176},{192,208},{224... | collective-permute-start | bytes 368648 | tf_op jit(solution)/shard_map/ppermute | solution.py:385
  13.4 0.7 %shard_map.47 = (f32[296,128]{1,0:T(8,128)S(1)}, f32[296,128]{1,0:T(8,128)S(1)}, f32[296,128]{1,0:T(8,128)S(1)}, f32[296,128]{1,0:T(8,128)S(1)}) custom-call(s32[4]{0:T(128)S(1)} %pad_add_fusion.where_ref, f32[1,2]{1,0:T(1,128)S(1)} %copy-done.3, f32[1,2,32,2048]{3,2,1,0:T(8,128)S(1)} %copy-done.1, f32[2,32,640]{2,1,0:T(8,128)S(1)} %get-tuple-element.27.after_ref.own_ref), custom_call_target="tpu_custom_call" | custom-call | bytes 1294336 | tf_op jit(solution)/shard_map/pallas_call | solution.py:336
  14.1 0.0 copy-start.2
  14.1 2.2 %collective-permute-start.2 = (f32[296,128]{1,0:T(8,128)S(1)}, f32[296,128]{1,0:T(8,128)S(1)}, u32[]{:S(2)}, u32[]{:S(2)}) collective-permute-start(f32[296,128]{1,0:T(8,128)S(1)} %get-tuple-element.30), channel_id=1, source_target_pairs={{0,4},{1,5},{2,6},{3,7},{4,0},{5,1},{6,2},{7,3},{8,12},{9,13},{10,... | collective-permute-start | bytes 454664 | tf_op jit(solution)/shard_map/ppermute | solution.py:391
  16.3 3.1 %collective-permute-start = (f32[296,128]{1,0:T(8,128)S(1)}, f32[296,128]{1,0:T(8,128)S(1)}, u32[]{:S(2)}, u32[]{:S(2)}) collective-permute-start(f32[296,128]{1,0:T(8,128)S(1)} %get-tuple-element.28), channel_id=1, source_target_pairs={{0,8},{1,9},{2,10},{3,11},{4,12},{5,13},{6,14},{7,15},{8,0},{9,1},... | collective-permute-start | bytes 454664 | tf_op jit(solution)/shard_map/ppermute | solution.py:391
  19.4 3.1 %collective-permute-start.1 = (f32[296,128]{1,0:T(8,128)S(1)}, f32[296,128]{1,0:T(8,128)S(1)}, u32[]{:S(2)}, u32[]{:S(2)}) collective-permute-start(f32[296,128]{1,0:T(8,128)S(1)} %get-tuple-element.29), channel_id=1, source_target_pairs={{0,12},{1,13},{2,14},{3,15},{4,8},{5,9},{6,10},{7,11},{8,4},{9,5},... | collective-permute-start | bytes 454664 | tf_op jit(solution)/shard_map/ppermute | solution.py:391
  22.5 1.4 %shard_map.48 = (f32[2,2,32,640]{3,2,1,0:T(8,128)S(1)}, bf16[256,192]{1,0:T(8,128)(2,1)S(1)}, bf16[128,256]{1,0:T(8,128)(2,1)S(1)}, bf16[256,128]{1,0:T(8,128)(2...) custom-call(s32[4]{0:T(128)S(1)} %pad_add_fusion.where_ref, f32[2,2,33]{2,1,0:T(2,128)S(1)} %copy-done.2, ...), custom_call_target="tpu_custom_call" | custom-call | flops 10000000 | bytes 1966080 | tf_op jit(solution)/shard_map/pallas_call | solution.py:336
  24.0 0.0 collective-permute-done.3.across_ref
  24.0 3.8 %shard_map.49 = (f32[2,96,768]{2,1,0:T(8,128)S(1)}, f32[2,64,640]{2,1,0:T(8,128)S(1)}, f32[96,512]{1,0:T(8,128)S(1)}, f32[64,640]{1,0:T(8,128)S(1)}) custom-call(s32[4]{0:T(128)S(1)} %pad_add_fusion.where_ref, f32[48,640]{1,0:T(8,128)S(1)} %collective-permute-done.3.across_ref, f32[48,640]{1,0:T(8,128)S(1)} %collective-permute-done.4.beside_ref, ...), custom_call_target="tpu_custom_call" | custom-call | flops 800000000 | bytes 3477504 | tf_op jit(solution)/shard_map/pallas_call | solution.py:336
  27.8 3.6 %shard_map.50 = (f32[96,512]{1,0:T(8,128)S(1)}, f32[64,640]{1,0:T(8,128)S(1)}) custom-call(s32[4]{0:T(128)S(1)} %pad_add_fusion.where_ref, f32[296,128]{1,0:T(8,128)S(1)} %collective-permute-done.2.measured_ref, f32[96,512]{1,0:T(8,128)S(1)} %get-tuple-element.40.total0_ref, f32[64,640]{1,0:T(8,128)S(1)} %get-tuple-element.41.total1_ref, ...), custom_call_target="tpu_custom_call" | custom-call | flops 2000000000 | bytes 3264512 | tf_op jit(solution)/shard_map/pallas_call | solution.py:336
  31.4 0.0 collective-permute-done.near_ref
  31.4 3.1 %collective-permute-done.1.far_ref = f32[296,128]{1,0:T(8,128)S(1)} collective-permute-done((f32[296,128]{1,0:T(8,128)S(1)}, f32[296,128]{1,0:T(8,128)S(1)}, u32[]{:S(2)}, u32[]{:S(2)}) %collective-permute-start.1) | collective-permute-done | bytes 151584 | tf_op jit(solution)/shard_map/ppermute | solution.py:391
  34.6 5.4 %shard_map.51 = f32[4,160,128]{2,1,0:T(8,128)S(1)} custom-call(s32[4]{0:T(128)S(1)} %pad_add_fusion.where_ref, f32[296,128]{1,0:T(8,128)S(1)} %collective-permute-done.near_ref, f32[296,128]{1,0:T(8,128)S(1)} %collective-permute-done.1.far_ref, f32[96,512]{1,0:T(8,128)S(1)} %get-tuple-element.44.total0_ref, f32[64,640]{1,0:T(8,128)S(1)} %get-tuple-element.45.total1_ref, ...), custom_call_target="tpu_custom_call" | custom-call | flops 4000000000 | bytes 3383296 | tf_op jit(solution)/shard_map/pallas_call | solution.py:336
  40.0 10.0 %all_to_all.5.tiles_ref = f32[4,160,128]{2,1,0:T(8,128)S(1)} all-to-all(f32[4,160,128]{2,1,0:T(8,128)S(1)} %shard_map.51), channel_id=1, replica_groups={{0,1,2,3},{4,5,6,7},{8,9,10,11},{12,13,14,15},{16,17,18,19},{20,21,22,2..., dimensions={0} | all-to-all | bytes 655360 | tf_op jit(solution)/shard_map/all_to_all | solution.py:426
  50.0 0.6 shard_map.52
  50.6 4.8 %collective-permute-start.5 = (f32[48,128]{1,0:T(8,128)S(1)}, f32[48,128]{1,0:T(8,128)S(1)}, u32[]{:S(2)}, u32[]{:S(2)}) collective-permute-start(f32[48,128]{1,0:T(8,128)S(1)} %get-tuple-element.47), channel_id=1, source_target_pairs={{16,32},{48,64},{80,96},{112,128},{144,160},{176,192},{208,224},{2... | collective-permute-start | bytes 73736 | tf_op jit(solution)/shard_map/ppermute | solution.py:435
  55.4 1.9 %collective-permute-start.6 = (f32[48,128]{1,0:T(8,128)S(1)}, f32[48,128]{1,0:T(8,128)S(1)}, u32[]{:S(2)}, u32[]{:S(2)}) collective-permute-start(f32[48,128]{1,0:T(8,128)S(1)} %get-tuple-element.48), channel_id=1, source_target_pairs={{0,16},{32,48},{64,80},{96,112},{128,144},{160,176},{192,208},{224... | collective-permute-start | bytes 73736 | tf_op jit(solution)/shard_map/ppermute | solution.py:434
  57.4 4.4 %collective-permute-done.5.across_ref = f32[48,128]{1,0:T(8,128)S(1)} collective-permute-done((f32[48,128]{1,0:T(8,128)S(1)}, f32[48,128]{1,0:T(8,128)S(1)}, u32[]{:S(2)}, u32[]{:S(2)}) %collective-permute-start.5) | collective-permute-done | bytes 24608 | tf_op jit(solution)/shard_map/ppermute | solution.py:435
  61.8 1.2 %shard_map.53 = f32[2,32,128]{2,1,0:T(8,128)} custom-call(s32[4]{0:T(128)S(1)} %pad_add_fusion.where_ref, f32[2,32,128]{2,1,0:T(8,128)S(1)} %get-tuple-element.46.own_ref, f32[48,128]{1,0:T(8,128)S(1)} %collective-permute-done.5.across_ref, f32[48,128]{1,0:T(8,128)S(1)} %collective-permute-done.6.beside_ref), custom_call_target="tpu_custom_call" | custom-call | bytes 114688 | tf_op jit(solution)/shard_map/pallas_call | solution.py:336
  (8 shorter events, 0.0 us)
Async XLA Ops:
  0.1 1.0 %copy-start = (f32[2,32,2048]{2,1,0:T(8,128)S(1)}, f32[2,32,2048]{2,1,0:T(8,128)}, u32[]{:S(2)}) copy-start(f32[2,32,2048]{2,1,0:T(8,128)} %phase_ref.1) | copy-start | bytes 1572868
  1.1 12.2 %copy-start.1 = (f32[1,2,32,2048]{3,2,1,0:T(8,128)S(1)}, f32[1,2,32,2048]{3,2,1,0:T(8,128)}, u32[]{:S(2)}) copy-start(f32[1,2,32,2048]{3,2,1,0:T(8,128)} %measured_ref.1) | copy-start | bytes 1572868
  1.9 22.1 %collective-permute-start.3 = (f32[48,640]{1,0:T(8,128)S(1)}, f32[48,640]{1,0:T(8,128)S(1)}, u32[]{:S(2)}, u32[]{:S(2)}) collective-permute-start(f32[48,640]{1,0:T(8,128)S(1)} %get-tuple-element.31), channel_id=1, source_target_pairs={{16,32},{17,33},{18,34},{19,35},{20,36},{21,37},{22,38},{23,39},{2... | collective-permute-start | bytes 368648 | tf_op jit(solution)/shard_map/ppermute | solution.py:386
  11.4 2.0 %copy-start.3 = (f32[1,2]{1,0:T(1,128)S(1)}, f32[1,2]{1,0:T(1,128)}, u32[]{:S(2)}) copy-start(f32[1,2]{1,0:T(1,128)} %tilts_ref.1) | copy-start | bytes 28
  11.4 12.6 %collective-permute-start.4 = (f32[48,640]{1,0:T(8,128)S(1)}, f32[48,640]{1,0:T(8,128)S(1)}, u32[]{:S(2)}, u32[]{:S(2)}) collective-permute-start(f32[48,640]{1,0:T(8,128)S(1)} %get-tuple-element.32), channel_id=1, source_target_pairs={{0,16},{32,48},{64,80},{96,112},{128,144},{160,176},{192,208},{224... | collective-permute-start | bytes 368648 | tf_op jit(solution)/shard_map/ppermute | solution.py:385
  14.1 8.4 %copy-start.2 = (f32[2,2,33]{2,1,0:T(2,128)S(1)}, f32[2,2,33]{2,1,0:T(2,128)}, u32[]{:S(2)}) copy-start(f32[2,2,33]{2,1,0:T(2,128)} %taps_ref.1) | copy-start | bytes 1588
  14.1 13.7 %collective-permute-start.2 = (f32[296,128]{1,0:T(8,128)S(1)}, f32[296,128]{1,0:T(8,128)S(1)}, u32[]{:S(2)}, u32[]{:S(2)}) collective-permute-start(f32[296,128]{1,0:T(8,128)S(1)} %get-tuple-element.30), channel_id=1, source_target_pairs={{0,4},{1,5},{2,6},{3,7},{4,0},{5,1},{6,2},{7,3},{8,12},{9,13},{10,... | collective-permute-start | bytes 454664 | tf_op jit(solution)/shard_map/ppermute | solution.py:391
  16.3 15.1 %collective-permute-start = (f32[296,128]{1,0:T(8,128)S(1)}, f32[296,128]{1,0:T(8,128)S(1)}, u32[]{:S(2)}, u32[]{:S(2)}) collective-permute-start(f32[296,128]{1,0:T(8,128)S(1)} %get-tuple-element.28), channel_id=1, source_target_pairs={{0,8},{1,9},{2,10},{3,11},{4,12},{5,13},{6,14},{7,15},{8,0},{9,1},... | collective-permute-start | bytes 454664 | tf_op jit(solution)/shard_map/ppermute | solution.py:391
  19.4 15.2 %collective-permute-start.1 = (f32[296,128]{1,0:T(8,128)S(1)}, f32[296,128]{1,0:T(8,128)S(1)}, u32[]{:S(2)}, u32[]{:S(2)}) collective-permute-start(f32[296,128]{1,0:T(8,128)S(1)} %get-tuple-element.29), channel_id=1, source_target_pairs={{0,12},{1,13},{2,14},{3,15},{4,8},{5,9},{6,10},{7,11},{8,4},{9,5},... | collective-permute-start | bytes 454664 | tf_op jit(solution)/shard_map/ppermute | solution.py:391
  50.6 11.2 %collective-permute-start.5 = (f32[48,128]{1,0:T(8,128)S(1)}, f32[48,128]{1,0:T(8,128)S(1)}, u32[]{:S(2)}, u32[]{:S(2)}) collective-permute-start(f32[48,128]{1,0:T(8,128)S(1)} %get-tuple-element.47), channel_id=1, source_target_pairs={{16,32},{48,64},{80,96},{112,128},{144,160},{176,192},{208,224},{2... | collective-permute-start | bytes 73736 | tf_op jit(solution)/shard_map/ppermute | solution.py:435
  55.4 6.3 %collective-permute-start.6 = (f32[48,128]{1,0:T(8,128)S(1)}, f32[48,128]{1,0:T(8,128)S(1)}, u32[]{:S(2)}, u32[]{:S(2)}) collective-permute-start(f32[48,128]{1,0:T(8,128)S(1)} %get-tuple-element.48), channel_id=1, source_target_pairs={{0,16},{32,48},{64,80},{96,112},{128,144},{160,176},{192,208},{224... | collective-permute-start | bytes 73736 | tf_op jit(solution)/shard_map/ppermute | solution.py:434

commit v9 on v8

--- a/solution.py
+++ b/solution.py
@@ -57,11 +57,21 @@
 def tap_matrices(taps_ref, into1_ref, into2_ref, out1_ref, out2_ref, band_ref):
     lane = lax.broadcasted_iota(jnp.int32, (8, 256), 1)
 
-    def laid(direction, part, start, step):
+    def plain(direction, part, step):
         out = jnp.zeros((8, 256), F32)
         for tap in range(TAPS):
-            out = jnp.where(lane == (start + step * tap) % 256, taps_ref[direction, part, tap], out)
+            out = jnp.where(lane == step * tap % 256, taps_ref[direction, part, tap], out)
         return out
+
+    base = {
+        (direction, part, step): plain(direction, part, step)
+        for direction in range(2)
+        for part in range(2)
+        for step in (1, -1)
+    }
+
+    def laid(direction, part, start, step):
+        return pltpu.roll(base[direction, part, step], start % 256, 1)
 
     def toeplitz(vector, rows):
         full = jnp.broadcast_to(vector[:1], (rows, 256))
@@ -293,30 +303,21 @@
     )
 
 
-def next_angle(where_ref, measured_ref, total0_ref, total1_ref, *refs):
-    term0, term1 = sweep(where_ref, [measured_ref], *refs[:-2])
+def next_angles(where_ref, near_ref, far_ref, total0_ref, total1_ref, *refs):
+    term0, term1 = sweep(where_ref, [near_ref, far_ref], *refs[:-2])
     refs[-2][...] = total0_ref[...] + term0
     refs[-1][...] = total1_ref[...] + term1
 
 
-def last_angles(where_ref, near_ref, far_ref, total0_ref, total1_ref, *refs):
-    out_ref = refs[-1]
-    term0, term1 = sweep(where_ref, [near_ref, far_ref], *refs[:-1])
-    total0, total1 = total0_ref[...] + term0, total1_ref[...] + term1
-    total1 = total1[:, TILE // 2 : TILE // 2 + BLOCK]
+def last_angle(where_ref, measured_ref, total0_ref, total1_ref, *refs):
+    own_ref, border_ref, core_ref = refs[-3:]
+    term0, term1 = sweep(where_ref, [measured_ref], *refs[:-3])
+    slice0, slice1 = total0_ref[...] + term0, total1_ref[...] + term1
+    slice1 = slice1[:, TILE // 2 : TILE // 2 + BLOCK]
     for j in range(BLOCK // TILE):
-        out_ref[j, :WIDEST] = total0[:, j * TILE : (j + 1) * TILE]
-        out_ref[j, WIDEST:] = total1[:, j * TILE : (j + 1) * TILE]
-
-
-def add_angles(where_ref, tiles_ref, own_ref, border_ref, core_ref):
+        own_ref[j, :ROWS] = slice0[ROWS : 2 * ROWS, j * TILE : (j + 1) * TILE]
+        own_ref[j, ROWS:] = slice1[REACH : REACH + ROWS, j * TILE : (j + 1) * TILE]
     even = where_ref[1] == 0
-    total = tiles_ref[0]
-    for j in range(1, tiles_ref.shape[0]):
-        total = total + tiles_ref[j]
-    slice0, slice1 = total[:WIDEST], total[WIDEST:]
-    own_ref[0] = slice0[ROWS : 2 * ROWS]
-    own_ref[1] = slice1[REACH : REACH + ROWS]
     low = jnp.concatenate([slice0[:ROWS], slice1[:REACH]], axis=0)
     high = jnp.concatenate([slice0[2 * ROWS :], slice1[REACH + ROWS :]], axis=0)
     border_ref[...] = jnp.where(even, low, high)
@@ -325,9 +326,11 @@
 
 def add_strips(where_ref, own_ref, across_ref, beside_ref, out_ref):
     below, above = neighbours(where_ref[1] == 0, across_ref[...], beside_ref[...])
-    out_ref[0] = own_ref[0] + (below[:ROWS] + above[:ROWS])
-    out_ref[1, :REACH] = own_ref[1, :REACH] + below[ROWS:]
-    out_ref[1, REACH:] = own_ref[1, REACH:] + above[ROWS:]
+    for j in range(BLOCK // TILE):
+        tile = slice(j * TILE, (j + 1) * TILE)
+        out_ref[j, :ROWS] = own_ref[j, :ROWS] + (below[:ROWS, tile] + above[:ROWS, tile])
+        out_ref[j, ROWS : ROWS + REACH] = own_ref[j, ROWS : ROWS + REACH] + below[ROWS:, tile]
+        out_ref[j, ROWS + REACH :] = own_ref[j, ROWS + REACH :] + above[ROWS:, tile]
 
 
 def call(kernel, shapes, scalars, arrays, flops, scratch=()):
@@ -413,28 +416,22 @@
         800_000_000,
     )
     total0, total1 = call(
-        next_angle, totals, [where], [block1, total0, total1, turn0, turn1, *matrices], 2_000_000_000
-    )
-    (tiles,) = call(
-        last_angles,
-        [struct((BLOCK // TILE, WIDEST + WIDE, TILE), F32)],
+        next_angles, totals, [where], [block1, block2, total0, total1, turn0, turn1, *matrices], 4_000_000_000
+    )
+    tiles_struct = struct((BLOCK // TILE, 2 * ROWS, TILE), F32)
+    tiles, to_border, to_core = call(
+        last_angle,
+        [tiles_struct] + [struct((ROWS + REACH, BLOCK), F32)] * 2,
         [where],
-        [block2, block3, total0, total1, turn0, turn1, *matrices],
-        4_000_000_000,
-    )
+        [block3, total0, total1, turn0, turn1, *matrices],
+        2_000_000_000,
+    )
+    beside = lax.ppermute(to_core, "space", in_chip)
+    across = lax.ppermute(to_border, "space", over_border)
+    (tiles,) = call(add_strips, [tiles_struct], [where], [tiles, across, beside], 0)
     beside_x = [[g * along + i for i in range(along)] for g in range(GROUP)]
     tiles = lax.all_to_all(tiles, "angle", 0, 0, axis_index_groups=beside_x)
-    total, to_border, to_core = call(
-        add_angles,
-        [struct((2, ROWS, TILE), F32)] + [struct((ROWS + REACH, TILE), F32)] * 2,
-        [where],
-        [tiles],
-        0,
-    )
-    beside = lax.ppermute(to_core, "space", in_chip)
-    across = lax.ppermute(to_border, "space", over_border)
-    (gradient,) = call(add_strips, [struct((2, ROWS, TILE), F32)], [where], [total, across, beside], 0)
-    return gradient
+    return jnp.sum(tiles, axis=0).reshape(2, ROWS, TILE)
 
 
 def solution(mesh):

time: 63.3 us -> 64.4 us (1.017)
  the two profiles are of different devices: /device:TPU:121 before, /device:TPU:57 now
where the time goes in v9:
time: 64.4 us; the launch traced here: 64 us
  starting transfers between devices  28.4 us (44%)
  Pallas kernels  16.7 us (26%)
  blocking collectives  8.65 us (13%)
  waiting for transfers between devices  8.4 us (13%)
  local copies, waits for them, and re-layouts  1.06 us (2%)
  other arithmetic  0.7 us (1%)
    pallas_call x7, Pallas kernels, call(): pl.pallas_call(kernel, out_shape=shapes, in_specs=[pl.BlockSpec(memory_sp...  16.7 us
    ppermute x1, starting transfers between devices, body(): across = lax.ppermute(to_border, ('space', 'angle'), over_border_nearest)  10.4 us
    ppermute x3, starting transfers between devices, body(): lax.ppermute(blocks[shift], 'angle', swapped(shift))  9.27 us
    all_to_all x1, blocking collectives, body(): tiles = lax.all_to_all(tiles, 'angle', 0, 0, axis_index_groups=beside_x)  8.65 us
    ppermute x1, waiting for transfers between devices, body(): across = lax.ppermute(to_border, 'space', over_border)  5.2 us
    ppermute x1, starting transfers between devices, body(): across = lax.ppermute(to_border, 'space', over_border)  4.82 us
    ppermute x2, starting transfers between devices, body(): beside = lax.ppermute(to_core, 'space', in_chip)  3.84 us
    ppermute x3, waiting for transfers between devices, body(): lax.ppermute(blocks[shift], 'angle', swapped(shift))  3.19 us
  transfers between devices with their start and end apart: 7, of which 2 were waited for; matrix products, arithmetic and copies ran while one was open for 0% of the time, Pallas kernels for 18%

profile of v9, /device:TPU:57, one launch (start us, length us, event | category | flops | bytes accessed | tf_op | source)
XLA Modules:
  0.0 64.0 jit_solution(3393801877937232603)
XLA Ops:
  0.0 0.1 pad_add_fusion.where_ref
  0.1 1.0 %copy-done = f32[2,32,2048]{2,1,0:T(8,128)S(1)} copy-done((f32[2,32,2048]{2,1,0:T(8,128)S(1)}, f32[2,32,2048]{2,1,0:T(8,128)}, u32[]{:S(2)}) %copy-start) | copy-done | bytes 524312
  1.1 0.8 %shard_map.46 = (f32[48,640]{1,0:T(8,128)S(1)}, f32[48,640]{1,0:T(8,128)S(1)}, f32[2,32,640]{2,1,0:T(8,128)S(1)}) custom-call(s32[4]{0:T(128)S(1)} %pad_add_fusion.where_ref, f32[2,32,2048]{2,1,0:T(8,128)S(1)} %copy-done), custom_call_target="tpu_custom_call" | custom-call | bytes 933888 | tf_op jit(solution)/shard_map/pallas_call | solution.py:339
  1.9 10.4 %collective-permute-start.3 = (f32[48,640]{1,0:T(8,128)S(1)}, f32[48,640]{1,0:T(8,128)S(1)}, u32[]{:S(2)}, u32[]{:S(2)}) collective-permute-start(f32[48,640]{1,0:T(8,128)S(1)} %get-tuple-element.31), channel_id=1, source_target_pairs={{16,32},{17,33},{18,34},{19,35},{20,36},{21,37},{22,38},{23,39},{2... | collective-permute-start | bytes 368648 | tf_op jit(solution)/shard_map/ppermute | solution.py:389
  12.3 0.0 copy-start.3
  12.3 1.9 %collective-permute-start.4 = (f32[48,640]{1,0:T(8,128)S(1)}, f32[48,640]{1,0:T(8,128)S(1)}, u32[]{:S(2)}, u32[]{:S(2)}) collective-permute-start(f32[48,640]{1,0:T(8,128)S(1)} %get-tuple-element.32), channel_id=1, source_target_pairs={{0,16},{32,48},{64,80},{96,112},{128,144},{160,176},{192,208},{224... | collective-permute-start | bytes 368648 | tf_op jit(solution)/shard_map/ppermute | solution.py:388
  14.3 0.7 %shard_map.47 = (f32[296,128]{1,0:T(8,128)S(1)}, f32[296,128]{1,0:T(8,128)S(1)}, f32[296,128]{1,0:T(8,128)S(1)}, f32[296,128]{1,0:T(8,128)S(1)}) custom-call(s32[4]{0:T(128)S(1)} %pad_add_fusion.where_ref, f32[1,2]{1,0:T(1,128)S(1)} %copy-done.3, f32[1,2,32,2048]{3,2,1,0:T(8,128)S(1)} %copy-done.1, f32[2,32,640]{2,1,0:T(8,128)S(1)} %get-tuple-element.27.after_ref.own_ref), custom_call_target="tpu_custom_call" | custom-call | bytes 1294336 | tf_op jit(solution)/shard_map/pallas_call | solution.py:339
  15.0 0.0 copy-start.2
  15.1 3.1 %collective-permute-start.1 = (f32[296,128]{1,0:T(8,128)S(1)}, f32[296,128]{1,0:T(8,128)S(1)}, u32[]{:S(2)}, u32[]{:S(2)}) collective-permute-start(f32[296,128]{1,0:T(8,128)S(1)} %get-tuple-element.29), channel_id=1, source_target_pairs={{0,4},{1,5},{2,6},{3,7},{4,0},{5,1},{6,2},{7,3},{8,12},{9,13},{10,... | collective-permute-start | bytes 454664 | tf_op jit(solution)/shard_map/ppermute | solution.py:394
  18.1 1.9 %collective-permute-start.2 = (f32[296,128]{1,0:T(8,128)S(1)}, f32[296,128]{1,0:T(8,128)S(1)}, u32[]{:S(2)}, u32[]{:S(2)}) collective-permute-start(f32[296,128]{1,0:T(8,128)S(1)} %get-tuple-element.30), channel_id=1, source_target_pairs={{0,8},{1,9},{2,10},{3,11},{4,12},{5,13},{6,14},{7,15},{8,0},{9,1},... | collective-permute-start | bytes 454664 | tf_op jit(solution)/shard_map/ppermute | solution.py:394
  20.1 4.3 %collective-permute-start = (f32[296,128]{1,0:T(8,128)S(1)}, f32[296,128]{1,0:T(8,128)S(1)}, u32[]{:S(2)}, u32[]{:S(2)}) collective-permute-start(f32[296,128]{1,0:T(8,128)S(1)} %get-tuple-element.28), channel_id=1, source_target_pairs={{0,12},{1,13},{2,14},{3,15},{4,8},{5,9},{6,10},{7,11},{8,4},{9,5},... | collective-permute-start | bytes 454664 | tf_op jit(solution)/shard_map/ppermute | solution.py:394
  24.4 1.8 %shard_map.48 = (f32[2,2,32,640]{3,2,1,0:T(8,128)S(1)}, bf16[256,192]{1,0:T(8,128)(2,1)S(1)}, bf16[128,256]{1,0:T(8,128)(2,1)S(1)}, bf16[256,128]{1,0:T(8,128)(2...) custom-call(s32[4]{0:T(128)S(1)} %pad_add_fusion.where_ref, f32[2,2,33]{2,1,0:T(2,128)S(1)} %copy-done.2, ...), custom_call_target="tpu_custom_call" | custom-call | flops 10000000 | bytes 1966080 | tf_op jit(solution)/shard_map/pallas_call | solution.py:339
  26.1 0.0 collective-permute-done.3.across_ref
  26.1 0.0 collective-permute-done.4.beside_ref
  26.1 3.8 %shard_map.49 = (f32[2,96,768]{2,1,0:T(8,128)S(1)}, f32[2,64,640]{2,1,0:T(8,128)S(1)}, f32[96,512]{1,0:T(8,128)S(1)}, f32[64,640]{1,0:T(8,128)S(1)}) custom-call(s32[4]{0:T(128)S(1)} %pad_add_fusion.where_ref, f32[48,640]{1,0:T(8,128)S(1)} %collective-permute-done.3.across_ref, f32[48,640]{1,0:T(8,128)S(1)} %collective-permute-done.4.beside_ref, ...), custom_call_target="tpu_custom_call" | custom-call | flops 800000000 | bytes 3477504 | tf_op jit(solution)/shard_map/pallas_call | solution.py:339
  30.0 3.2 %collective-permute-done.2.far_ref = f32[296,128]{1,0:T(8,128)S(1)} collective-permute-done((f32[296,128]{1,0:T(8,128)S(1)}, f32[296,128]{1,0:T(8,128)S(1)}, u32[]{:S(2)}, u32[]{:S(2)}) %collective-permute-start.2) | collective-permute-done | bytes 151584 | tf_op jit(solution)/shard_map/ppermute | solution.py:394
  33.1 5.4 %shard_map.50 = (f32[96,512]{1,0:T(8,128)S(1)}, f32[64,640]{1,0:T(8,128)S(1)}) custom-call(s32[4]{0:T(128)S(1)} %pad_add_fusion.where_ref, f32[296,128]{1,0:T(8,128)S(1)} %collective-permute-done.1.near_ref, f32[296,128]{1,0:T(8,128)S(1)} %collective-permute-done.2.far_ref, f32[96,512]{1,0:T(8,128)S(1)} %get-tuple-element.40.total0_ref, ...), custom_call_target="tpu_custom_call" | custom-call | flops 4000000000 | bytes 3416064 | tf_op jit(solution)/shard_map/pallas_call | solution.py:339
  38.6 3.6 %shard_map.51 = (f32[4,64,128]{2,1,0:T(8,128)S(1)}, f32[48,512]{1,0:T(8,128)S(1)}, f32[48,512]{1,0:T(8,128)S(1)}) custom-call(s32[4]{0:T(128)S(1)} %pad_add_fusion.where_ref, f32[296,128]{1,0:T(8,128)S(1)} %collective-permute-done.measured_ref, f32[96,512]{1,0:T(8,128)S(1)} %get-tuple-element.44.total0_ref, f32[64,640]{1,0:T(8,128)S(1)} %get-tuple-element.45.total1_ref, ...), custom_call_target="tpu_custom_call" | custom-call | flops 2000000000 | bytes 3231744 | tf_op jit(solution)/shard_map/pallas_call | solution.py:339
  42.2 4.8 %collective-permute-start.5 = (f32[48,512]{1,0:T(8,128)S(1)}, f32[48,512]{1,0:T(8,128)S(1)}, u32[]{:S(2)}, u32[]{:S(2)}) collective-permute-start(f32[48,512]{1,0:T(8,128)S(1)} %get-tuple-element.47), channel_id=1, source_target_pairs={{16,32},{48,64},{80,96},{112,128},{144,160},{176,192},{208,224},{2... | collective-permute-start | bytes 294920 | tf_op jit(solution)/shard_map/ppermute | solution.py:430
  47.0 1.9 %collective-permute-start.6 = (f32[48,512]{1,0:T(8,128)S(1)}, f32[48,512]{1,0:T(8,128)S(1)}, u32[]{:S(2)}, u32[]{:S(2)}) collective-permute-start(f32[48,512]{1,0:T(8,128)S(1)} %get-tuple-element.48), channel_id=1, source_target_pairs={{0,16},{32,48},{64,80},{96,112},{128,144},{160,176},{192,208},{224... | collective-permute-start | bytes 294920 | tf_op jit(solution)/shard_map/ppermute | solution.py:429
  49.0 5.2 %collective-permute-done.5.across_ref = f32[48,512]{1,0:T(8,128)S(1)} collective-permute-done((f32[48,512]{1,0:T(8,128)S(1)}, f32[48,512]{1,0:T(8,128)S(1)}, u32[]{:S(2)}, u32[]{:S(2)}) %collective-permute-start.5) | collective-permute-done | bytes 98336 | tf_op jit(solution)/shard_map/ppermute | solution.py:430
  54.2 0.6 shard_map.52
  54.7 8.6 %all_to_all.5 = f32[4,64,128]{2,1,0:T(8,128)S(1)} all-to-all(f32[4,64,128]{2,1,0:T(8,128)S(1)} %shard_map.52), channel_id=1, replica_groups={{0,1,2,3},{4,5,6,7},{8,9,10,11},{12,13,14,15},{16,17,18,19},{20,21,22,2..., dimensions={0} | all-to-all | bytes 262144 | tf_op jit(solution)/shard_map/all_to_all | solution.py:433
  63.4 0.6 reduce_sum.9
  (8 shorter events, 0.0 us)
Async XLA Ops:
  0.1 1.0 %copy-start = (f32[2,32,2048]{2,1,0:T(8,128)S(1)}, f32[2,32,2048]{2,1,0:T(8,128)}, u32[]{:S(2)}) copy-start(f32[2,32,2048]{2,1,0:T(8,128)} %phase_ref.1) | copy-start | bytes 1572868
  1.1 13.1 %copy-start.1 = (f32[1,2,32,2048]{3,2,1,0:T(8,128)S(1)}, f32[1,2,32,2048]{3,2,1,0:T(8,128)}, u32[]{:S(2)}) copy-start(f32[1,2,32,2048]{3,2,1,0:T(8,128)} %measured_ref.1) | copy-start | bytes 1572868
  1.9 24.2 %collective-permute-start.3 = (f32[48,640]{1,0:T(8,128)S(1)}, f32[48,640]{1,0:T(8,128)S(1)}, u32[]{:S(2)}, u32[]{:S(2)}) collective-permute-start(f32[48,640]{1,0:T(8,128)S(1)} %get-tuple-element.31), channel_id=1, source_target_pairs={{16,32},{17,33},{18,34},{19,35},{20,36},{21,37},{22,38},{23,39},{2... | collective-permute-start | bytes 368648 | tf_op jit(solution)/shard_map/ppermute | solution.py:389
  12.3 2.0 %copy-start.3 = (f32[1,2]{1,0:T(1,128)S(1)}, f32[1,2]{1,0:T(1,128)}, u32[]{:S(2)}) copy-start(f32[1,2]{1,0:T(1,128)} %tilts_ref.1) | copy-start | bytes 28
  12.3 13.8 %collective-permute-start.4 = (f32[48,640]{1,0:T(8,128)S(1)}, f32[48,640]{1,0:T(8,128)S(1)}, u32[]{:S(2)}, u32[]{:S(2)}) collective-permute-start(f32[48,640]{1,0:T(8,128)S(1)} %get-tuple-element.32), channel_id=1, source_target_pairs={{0,16},{32,48},{64,80},{96,112},{128,144},{160,176},{192,208},{224... | collective-permute-start | bytes 368648 | tf_op jit(solution)/shard_map/ppermute | solution.py:388
  15.0 9.3 %copy-start.2 = (f32[2,2,33]{2,1,0:T(2,128)S(1)}, f32[2,2,33]{2,1,0:T(2,128)}, u32[]{:S(2)}) copy-start(f32[2,2,33]{2,1,0:T(2,128)} %taps_ref.1) | copy-start | bytes 1588
  15.1 14.9 %collective-permute-start.1 = (f32[296,128]{1,0:T(8,128)S(1)}, f32[296,128]{1,0:T(8,128)S(1)}, u32[]{:S(2)}, u32[]{:S(2)}) collective-permute-start(f32[296,128]{1,0:T(8,128)S(1)} %get-tuple-element.29), channel_id=1, source_target_pairs={{0,4},{1,5},{2,6},{3,7},{4,0},{5,1},{6,2},{7,3},{8,12},{9,13},{10,... | collective-permute-start | bytes 454664 | tf_op jit(solution)/shard_map/ppermute | solution.py:394
  18.1 15.0 %collective-permute-start.2 = (f32[296,128]{1,0:T(8,128)S(1)}, f32[296,128]{1,0:T(8,128)S(1)}, u32[]{:S(2)}, u32[]{:S(2)}) collective-permute-start(f32[296,128]{1,0:T(8,128)S(1)} %get-tuple-element.30), channel_id=1, source_target_pairs={{0,8},{1,9},{2,10},{3,11},{4,12},{5,13},{6,14},{7,15},{8,0},{9,1},... | collective-permute-start | bytes 454664 | tf_op jit(solution)/shard_map/ppermute | solution.py:394
  20.1 18.5 %collective-permute-start = (f32[296,128]{1,0:T(8,128)S(1)}, f32[296,128]{1,0:T(8,128)S(1)}, u32[]{:S(2)}, u32[]{:S(2)}) collective-permute-start(f32[296,128]{1,0:T(8,128)S(1)} %get-tuple-element.28), channel_id=1, source_target_pairs={{0,12},{1,13},{2,14},{3,15},{4,8},{5,9},{6,10},{7,11},{8,4},{9,5},... | collective-permute-start | bytes 454664 | tf_op jit(solution)/shard_map/ppermute | solution.py:394
  42.2 12.0 %collective-permute-start.5 = (f32[48,512]{1,0:T(8,128)S(1)}, f32[48,512]{1,0:T(8,128)S(1)}, u32[]{:S(2)}, u32[]{:S(2)}) collective-permute-start(f32[48,512]{1,0:T(8,128)S(1)} %get-tuple-element.47), channel_id=1, source_target_pairs={{16,32},{48,64},{80,96},{112,128},{144,160},{176,192},{208,224},{2... | collective-permute-start | bytes 294920 | tf_op jit(solution)/shard_map/ppermute | solution.py:430
  47.0 7.1 %collective-permute-start.6 = (f32[48,512]{1,0:T(8,128)S(1)}, f32[48,512]{1,0:T(8,128)S(1)}, u32[]{:S(2)}, u32[]{:S(2)}) collective-permute-start(f32[48,512]{1,0:T(8,128)S(1)} %get-tuple-element.48), channel_id=1, source_target_pairs={{0,16},{32,48},{64,80},{96,112},{128,144},{160,176},{192,208},{224... | collective-permute-start | bytes 294920 | tf_op jit(solution)/shard_map/ppermute | solution.py:429

commit v10 on v9

--- a/solution.py
+++ b/solution.py
@@ -57,21 +57,11 @@
 def tap_matrices(taps_ref, into1_ref, into2_ref, out1_ref, out2_ref, band_ref):
     lane = lax.broadcasted_iota(jnp.int32, (8, 256), 1)
 
-    def plain(direction, part, step):
+    def laid(direction, part, start, step):
         out = jnp.zeros((8, 256), F32)
         for tap in range(TAPS):
-            out = jnp.where(lane == step * tap % 256, taps_ref[direction, part, tap], out)
+            out = jnp.where(lane == (start + step * tap) % 256, taps_ref[direction, part, tap], out)
         return out
-
-    base = {
-        (direction, part, step): plain(direction, part, step)
-        for direction in range(2)
-        for part in range(2)
-        for step in (1, -1)
-    }
-
-    def laid(direction, part, start, step):
-        return pltpu.roll(base[direction, part, step], start % 256, 1)
 
     def toeplitz(vector, rows):
         full = jnp.broadcast_to(vector[:1], (rows, 256))
@@ -293,25 +283,19 @@
     return total0, total1
 
 
-def first_angle(
-    where_ref, across_ref, beside_ref, own_ref, measured_ref, into1_ref, into2_ref, out1_ref, out2_ref, band_ref,
+def first_angles(
+    where_ref, across_ref, beside_ref, own_ref, near_ref, far_ref, into1_ref, into2_ref, out1_ref, out2_ref, band_ref,
     turn0_ref, turn1_ref, total0_ref, total1_ref, *, total_rows,
 ):
     turns(where_ref, across_ref, beside_ref, own_ref, turn0_ref, turn1_ref, total_rows)
     total0_ref[...], total1_ref[...] = sweep(
-        where_ref, [measured_ref], turn0_ref, turn1_ref, into1_ref, into2_ref, out1_ref, out2_ref, band_ref
-    )
-
-
-def next_angles(where_ref, near_ref, far_ref, total0_ref, total1_ref, *refs):
-    term0, term1 = sweep(where_ref, [near_ref, far_ref], *refs[:-2])
-    refs[-2][...] = total0_ref[...] + term0
-    refs[-1][...] = total1_ref[...] + term1
-
-
-def last_angle(where_ref, measured_ref, total0_ref, total1_ref, *refs):
+        where_ref, [near_ref, far_ref], turn0_ref, turn1_ref, into1_ref, into2_ref, out1_ref, out2_ref, band_ref
+    )
+
+
+def last_angles(where_ref, near_ref, far_ref, total0_ref, total1_ref, *refs):
     own_ref, border_ref, core_ref = refs[-3:]
-    term0, term1 = sweep(where_ref, [measured_ref], *refs[:-3])
+    term0, term1 = sweep(where_ref, [near_ref, far_ref], *refs[:-3])
     slice0, slice1 = total0_ref[...] + term0, total1_ref[...] + term1
     slice1 = slice1[:, TILE // 2 : TILE // 2 + BLOCK]
     for j in range(BLOCK // TILE):
@@ -409,22 +393,19 @@
     )
     totals = [struct((WIDEST, BLOCK), F32), struct((WIDE, FRAME1), F32)]
     turn0, turn1, total0, total1 = call(
-        functools.partial(first_angle, total_rows=total_rows),
+        functools.partial(first_angles, total_rows=total_rows),
         [struct((2, WIDEST, FRAME0), F32), struct((2, WIDE, FRAME1), F32)] + totals,
         [where],
-        [across, beside, own, near, *matrices],
+        [across, beside, own, near, block2, *matrices],
         800_000_000,
-    )
-    total0, total1 = call(
-        next_angles, totals, [where], [block1, block2, total0, total1, turn0, turn1, *matrices], 4_000_000_000
     )
     tiles_struct = struct((BLOCK // TILE, 2 * ROWS, TILE), F32)
     tiles, to_border, to_core = call(
-        last_angle,
+        last_angles,
         [tiles_struct] + [struct((ROWS + REACH, BLOCK), F32)] * 2,
         [where],
-        [block3, total0, total1, turn0, turn1, *matrices],
-        2_000_000_000,
+        [block3, block1, total0, total1, turn0, turn1, *matrices],
+        4_000_000_000,
     )
     beside = lax.ppermute(to_core, "space", in_chip)
     across = lax.ppermute(to_border, "space", over_border)

time: 64.4 us -> 60 us (0.932)
  waiting for transfers between devices: 8.4 us -> 5.66 us
  Pallas kernels: 16.7 us -> 14.5 us
  local copies, waits for them, and re-layouts: 1.06 us -> 1.74 us
    ppermute x3, starting transfers between devices: 9.27 us -> 12.9 us  [body(): lax.ppermute(blocks[shift], 'angle', swapped(shift))]
    ppermute x1, starting transfers between devices: 10.4 us -> 7.07 us  [body(): across = lax.ppermute(to_border, ('space', 'angle'), over_border_nearest)]
    ppermute x3, waiting for transfers between devices: 3.19 us -> 0.01 us  [body(): lax.ppermute(blocks[shift], 'angle', swapped(shift))]
    pallas_call x7 -> x6, Pallas kernels: 16.7 us -> 14.5 us  [call(): pl.pallas_call(kernel, out_shape=shapes, in_specs=[pl.BlockSpec(memory_sp...]
    unnamed x8, local copies, waits for them, and re-layouts: 1.06 us -> 1.74 us
  transfers between devices with their start and end apart: 7 -> 7, of which waited for: 2 -> 1; matrix products, arithmetic and copies ran while one was open for 0% -> 0% of each run, Pallas kernels for 18% -> 12%
where the time goes in v10:
time: 60 us; the launch traced here: 59.6 us
  starting transfers between devices  28.2 us (47%)
  Pallas kernels  14.5 us (24%)
  blocking collectives  8.65 us (14%)
  waiting for transfers between devices  5.66 us (9%)
  local copies, waits for them, and re-layouts  1.74 us (3%)
  other arithmetic  0.7 us (1%)
    pallas_call x6, Pallas kernels, call(): pl.pallas_call(kernel, out_shape=shapes, in_specs=[pl.BlockSpec(memory_sp...  14.5 us
    ppermute x3, starting transfers between devices, body(): lax.ppermute(blocks[shift], 'angle', swapped(shift))  12.9 us
    all_to_all x1, blocking collectives, body(): tiles = lax.all_to_all(tiles, 'angle', 0, 0, axis_index_groups=beside_x)  8.65 us
    ppermute x1, starting transfers between devices, body(): across = lax.ppermute(to_border, ('space', 'angle'), over_border_nearest)  7.07 us
    ppermute x1, waiting for transfers between devices, body(): across = lax.ppermute(to_border, 'space', over_border)  5.64 us
    ppermute x1, starting transfers between devices, body(): across = lax.ppermute(to_border, 'space', over_border)  4.37 us
    ppermute x2, starting transfers between devices, body(): beside = lax.ppermute(to_core, 'space', in_chip)  3.84 us
    unnamed x8, local copies, waits for them, and re-layouts  1.74 us
  transfers between devices with their start and end apart: 7, of which 1 were waited for; matrix products, arithmetic and copies ran while one was open for 0% of the time, Pallas kernels for 12%

profile of v10, /device:TPU:57, one launch (start us, length us, event | category | flops | bytes accessed | tf_op | source)
XLA Modules:
  0.0 59.6 jit_solution(3263925978706357525)
XLA Ops:
  0.0 0.1 pad_add_fusion.where_ref
  0.1 1.0 %copy-done = f32[2,32,2048]{2,1,0:T(8,128)S(1)} copy-done((f32[2,32,2048]{2,1,0:T(8,128)S(1)}, f32[2,32,2048]{2,1,0:T(8,128)}, u32[]{:S(2)}) %copy-start) | copy-done | bytes 524312
  1.1 0.8 %shard_map.46 = (f32[48,640]{1,0:T(8,128)S(1)}, f32[48,640]{1,0:T(8,128)S(1)}, f32[2,32,640]{2,1,0:T(8,128)S(1)}) custom-call(s32[4]{0:T(128)S(1)} %pad_add_fusion.where_ref, f32[2,32,2048]{2,1,0:T(8,128)S(1)} %copy-done), custom_call_target="tpu_custom_call" | custom-call | bytes 933888 | tf_op jit(solution)/shard_map/pallas_call | solution.py:323
  1.9 0.0 copy-start.3
  1.9 0.3 copy-done.1
  2.2 0.4 copy-done.3
  2.6 0.7 %shard_map.47 = (f32[296,128]{1,0:T(8,128)S(1)}, f32[296,128]{1,0:T(8,128)S(1)}, f32[296,128]{1,0:T(8,128)S(1)}, f32[296,128]{1,0:T(8,128)S(1)}) custom-call(s32[4]{0:T(128)S(1)} %pad_add_fusion.where_ref, f32[1,2]{1,0:T(1,128)S(1)} %copy-done.3, f32[1,2,32,2048]{3,2,1,0:T(8,128)S(1)} %copy-done.1, f32[2,32,640]{2,1,0:T(8,128)S(1)} %get-tuple-element.25.after_ref.own_ref), custom_call_target="tpu_custom_call" | custom-call | bytes 1294336 | tf_op jit(solution)/shard_map/pallas_call | solution.py:323
  3.3 5.8 %collective-permute-start.4 = (f32[296,128]{1,0:T(8,128)S(1)}, f32[296,128]{1,0:T(8,128)S(1)}, u32[]{:S(2)}, u32[]{:S(2)}) collective-permute-start(f32[296,128]{1,0:T(8,128)S(1)} %get-tuple-element.32), channel_id=1, source_target_pairs={{0,8},{1,9},{2,10},{3,11},{4,12},{5,13},{6,14},{7,15},{8,0},{9,1},... | collective-permute-start | bytes 454664 | tf_op jit(solution)/shard_map/ppermute | solution.py:378
  9.2 7.1 %collective-permute-start.2 = (f32[48,640]{1,0:T(8,128)S(1)}, f32[48,640]{1,0:T(8,128)S(1)}, u32[]{:S(2)}, u32[]{:S(2)}) collective-permute-start(f32[48,640]{1,0:T(8,128)S(1)} %get-tuple-element.28), channel_id=1, source_target_pairs={{16,32},{17,33},{18,34},{19,35},{20,36},{21,37},{22,38},{23,39},{2... | collective-permute-start | bytes 368648 | tf_op jit(solution)/shard_map/ppermute | solution.py:373
  16.2 0.0 copy-start.2
  16.2 1.9 %collective-permute-start.3 = (f32[48,640]{1,0:T(8,128)S(1)}, f32[48,640]{1,0:T(8,128)S(1)}, u32[]{:S(2)}, u32[]{:S(2)}) collective-permute-start(f32[48,640]{1,0:T(8,128)S(1)} %get-tuple-element.29), channel_id=1, source_target_pairs={{0,16},{32,48},{64,80},{96,112},{128,144},{160,176},{192,208},{224... | collective-permute-start | bytes 368648 | tf_op jit(solution)/shard_map/ppermute | solution.py:372
  18.2 4.0 %collective-permute-start = (f32[296,128]{1,0:T(8,128)S(1)}, f32[296,128]{1,0:T(8,128)S(1)}, u32[]{:S(2)}, u32[]{:S(2)}) collective-permute-start(f32[296,128]{1,0:T(8,128)S(1)} %get-tuple-element.26), channel_id=1, source_target_pairs={{0,12},{1,13},{2,14},{3,15},{4,8},{5,9},{6,10},{7,11},{8,4},{9,5},... | collective-permute-start | bytes 454664 | tf_op jit(solution)/shard_map/ppermute | solution.py:378
  22.2 3.1 %collective-permute-start.1 = (f32[296,128]{1,0:T(8,128)S(1)}, f32[296,128]{1,0:T(8,128)S(1)}, u32[]{:S(2)}, u32[]{:S(2)}) collective-permute-start(f32[296,128]{1,0:T(8,128)S(1)} %get-tuple-element.27), channel_id=1, source_target_pairs={{0,4},{1,5},{2,6},{3,7},{4,0},{5,1},{6,2},{7,3},{8,12},{9,13},{10,... | collective-permute-start | bytes 454664 | tf_op jit(solution)/shard_map/ppermute | solution.py:378
  25.3 1.4 %shard_map.48 = (f32[2,2,32,640]{3,2,1,0:T(8,128)S(1)}, bf16[256,192]{1,0:T(8,128)(2,1)S(1)}, bf16[128,256]{1,0:T(8,128)(2,1)S(1)}, bf16[256,128]{1,0:T(8,128)(2...) custom-call(s32[4]{0:T(128)S(1)} %pad_add_fusion.where_ref, f32[2,2,33]{2,1,0:T(2,128)S(1)} %copy-done.2, ...), custom_call_target="tpu_custom_call" | custom-call | flops 10000000 | bytes 1966080 | tf_op jit(solution)/shard_map/pallas_call | solution.py:323
  26.7 0.0 collective-permute-done.2.across_ref
  26.8 0.0 collective-permute-done.4.far_ref
  26.8 5.6 %shard_map.49 = (f32[2,96,768]{2,1,0:T(8,128)S(1)}, f32[2,64,640]{2,1,0:T(8,128)S(1)}, f32[96,512]{1,0:T(8,128)S(1)}, f32[64,640]{1,0:T(8,128)S(1)}) custom-call(s32[4]{0:T(128)S(1)} %pad_add_fusion.where_ref, f32[48,640]{1,0:T(8,128)S(1)} %collective-permute-done.2.across_ref, f32[48,640]{1,0:T(8,128)S(1)} %collective-permute-done.3.beside_ref, ...), custom_call_target="tpu_custom_call" | custom-call | flops 800000000 | bytes 3629056 | tf_op jit(solution)/shard_map/pallas_call | solution.py:323
  32.4 5.4 %shard_map.50 = (f32[4,64,128]{2,1,0:T(8,128)S(1)}, f32[48,512]{1,0:T(8,128)S(1)}, f32[48,512]{1,0:T(8,128)S(1)}) custom-call(s32[4]{0:T(128)S(1)} %pad_add_fusion.where_ref, f32[296,128]{1,0:T(8,128)S(1)} %collective-permute-done.near_ref, f32[296,128]{1,0:T(8,128)S(1)} %collective-permute-done.1.far_ref, f32[96,512]{1,0:T(8,128)S(1)} %get-tuple-element.38.total0_ref, ...), custom_call_target="tpu_custom_call" | custom-call | flops 4000000000 | bytes 3383296 | tf_op jit(solution)/shard_map/pallas_call | solution.py:323
  37.8 4.4 %collective-permute-start.5 = (f32[48,512]{1,0:T(8,128)S(1)}, f32[48,512]{1,0:T(8,128)S(1)}, u32[]{:S(2)}, u32[]{:S(2)}) collective-permute-start(f32[48,512]{1,0:T(8,128)S(1)} %get-tuple-element.43), channel_id=1, source_target_pairs={{16,32},{48,64},{80,96},{112,128},{144,160},{176,192},{208,224},{2... | collective-permute-start | bytes 294920 | tf_op jit(solution)/shard_map/ppermute | solution.py:411
  42.2 1.9 %collective-permute-start.6 = (f32[48,512]{1,0:T(8,128)S(1)}, f32[48,512]{1,0:T(8,128)S(1)}, u32[]{:S(2)}, u32[]{:S(2)}) collective-permute-start(f32[48,512]{1,0:T(8,128)S(1)} %get-tuple-element.44), channel_id=1, source_target_pairs={{0,16},{32,48},{64,80},{96,112},{128,144},{160,176},{192,208},{224... | collective-permute-start | bytes 294920 | tf_op jit(solution)/shard_map/ppermute | solution.py:410
  44.1 5.6 %collective-permute-done.5.across_ref = f32[48,512]{1,0:T(8,128)S(1)} collective-permute-done((f32[48,512]{1,0:T(8,128)S(1)}, f32[48,512]{1,0:T(8,128)S(1)}, u32[]{:S(2)}, u32[]{:S(2)}) %collective-permute-start.5) | collective-permute-done | bytes 98336 | tf_op jit(solution)/shard_map/ppermute | solution.py:411
  49.8 0.6 shard_map.51
  50.3 8.6 %all_to_all.5 = f32[4,64,128]{2,1,0:T(8,128)S(1)} all-to-all(f32[4,64,128]{2,1,0:T(8,128)S(1)} %shard_map.51), channel_id=1, replica_groups={{0,1,2,3},{4,5,6,7},{8,9,10,11},{12,13,14,15},{16,17,18,19},{20,21,22,2..., dimensions={0} | all-to-all | bytes 262144 | tf_op jit(solution)/shard_map/all_to_all | solution.py:414
  59.0 0.6 %reduce_sum.9 = f32[64,128]{1,0:T(8,128)} reduce(f32[4,64,128]{2,1,0:T(8,128)S(1)} %all_to_all.5, f32[]{:T(128)} %constant.34.clone.1), dimensions={0}, to_apply=%region_0.1 | reduce | flops 24576 | bytes 163844 | tf_op jit(solution)/shard_map/reduce_sum | solution.py:415
  (7 shorter events, 0.0 us)
Async XLA Ops:
  0.1 1.0 %copy-start = (f32[2,32,2048]{2,1,0:T(8,128)S(1)}, f32[2,32,2048]{2,1,0:T(8,128)}, u32[]{:S(2)}) copy-start(f32[2,32,2048]{2,1,0:T(8,128)} %phase_ref.1) | copy-start | bytes 1572868
  1.1 1.0 %copy-start.1 = (f32[1,2,32,2048]{3,2,1,0:T(8,128)S(1)}, f32[1,2,32,2048]{3,2,1,0:T(8,128)}, u32[]{:S(2)}) copy-start(f32[1,2,32,2048]{3,2,1,0:T(8,128)} %measured_ref.1) | copy-start | bytes 1572868
  1.9 0.7 %copy-start.3 = (f32[1,2]{1,0:T(1,128)S(1)}, f32[1,2]{1,0:T(1,128)}, u32[]{:S(2)}) copy-start(f32[1,2]{1,0:T(1,128)} %tilts_ref.1) | copy-start | bytes 28
  3.3 23.4 %collective-permute-start.4 = (f32[296,128]{1,0:T(8,128)S(1)}, f32[296,128]{1,0:T(8,128)S(1)}, u32[]{:S(2)}, u32[]{:S(2)}) collective-permute-start(f32[296,128]{1,0:T(8,128)S(1)} %get-tuple-element.32), channel_id=1, source_target_pairs={{0,8},{1,9},{2,10},{3,11},{4,12},{5,13},{6,14},{7,15},{8,0},{9,1},... | collective-permute-start | bytes 454664 | tf_op jit(solution)/shard_map/ppermute | solution.py:378
  9.2 17.6 %collective-permute-start.2 = (f32[48,640]{1,0:T(8,128)S(1)}, f32[48,640]{1,0:T(8,128)S(1)}, u32[]{:S(2)}, u32[]{:S(2)}) collective-permute-start(f32[48,640]{1,0:T(8,128)S(1)} %get-tuple-element.28), channel_id=1, source_target_pairs={{16,32},{17,33},{18,34},{19,35},{20,36},{21,37},{22,38},{23,39},{2... | collective-permute-start | bytes 368648 | tf_op jit(solution)/shard_map/ppermute | solution.py:373
  16.2 9.1 %copy-start.2 = (f32[2,2,33]{2,1,0:T(2,128)S(1)}, f32[2,2,33]{2,1,0:T(2,128)}, u32[]{:S(2)}) copy-start(f32[2,2,33]{2,1,0:T(2,128)} %taps_ref.1) | copy-start | bytes 1588
  16.2 10.5 %collective-permute-start.3 = (f32[48,640]{1,0:T(8,128)S(1)}, f32[48,640]{1,0:T(8,128)S(1)}, u32[]{:S(2)}, u32[]{:S(2)}) collective-permute-start(f32[48,640]{1,0:T(8,128)S(1)} %get-tuple-element.29), channel_id=1, source_target_pairs={{0,16},{32,48},{64,80},{96,112},{128,144},{160,176},{192,208},{224... | collective-permute-start | bytes 368648 | tf_op jit(solution)/shard_map/ppermute | solution.py:372
  18.2 14.2 %collective-permute-start = (f32[296,128]{1,0:T(8,128)S(1)}, f32[296,128]{1,0:T(8,128)S(1)}, u32[]{:S(2)}, u32[]{:S(2)}) collective-permute-start(f32[296,128]{1,0:T(8,128)S(1)} %get-tuple-element.26), channel_id=1, source_target_pairs={{0,12},{1,13},{2,14},{3,15},{4,8},{5,9},{6,10},{7,11},{8,4},{9,5},... | collective-permute-start | bytes 454664 | tf_op jit(solution)/shard_map/ppermute | solution.py:378
  22.2 10.2 %collective-permute-start.1 = (f32[296,128]{1,0:T(8,128)S(1)}, f32[296,128]{1,0:T(8,128)S(1)}, u32[]{:S(2)}, u32[]{:S(2)}) collective-permute-start(f32[296,128]{1,0:T(8,128)S(1)} %get-tuple-element.27), channel_id=1, source_target_pairs={{0,4},{1,5},{2,6},{3,7},{4,0},{5,1},{6,2},{7,3},{8,12},{9,13},{10,... | collective-permute-start | bytes 454664 | tf_op jit(solution)/shard_map/ppermute | solution.py:378
  37.8 12.0 %collective-permute-start.5 = (f32[48,512]{1,0:T(8,128)S(1)}, f32[48,512]{1,0:T(8,128)S(1)}, u32[]{:S(2)}, u32[]{:S(2)}) collective-permute-start(f32[48,512]{1,0:T(8,128)S(1)} %get-tuple-element.43), channel_id=1, source_target_pairs={{16,32},{48,64},{80,96},{112,128},{144,160},{176,192},{208,224},{2... | collective-permute-start | bytes 294920 | tf_op jit(solution)/shard_map/ppermute | solution.py:411
  42.2 7.6 %collective-permute-start.6 = (f32[48,512]{1,0:T(8,128)S(1)}, f32[48,512]{1,0:T(8,128)S(1)}, u32[]{:S(2)}, u32[]{:S(2)}) collective-permute-start(f32[48,512]{1,0:T(8,128)S(1)} %get-tuple-element.44), channel_id=1, source_target_pairs={{0,16},{32,48},{64,80},{96,112},{128,144},{160,176},{192,208},{224... | collective-permute-start | bytes 294920 | tf_op jit(solution)/shard_map/ppermute | solution.py:410

commit v11 on v10

--- a/solution.py
+++ b/solution.py
@@ -24,6 +24,7 @@
 TILTS_AT = SIDES_AT + ROWS
 MESSAGE = TILTS_AT + 8
 VMEM_LIMIT = 32 * 1024 * 1024
+PACK_LIMIT = 55259136
 
 
 def split(x):
@@ -169,52 +170,53 @@
     return jnp.concatenate([blank, x, blank], axis=1)
 
 
-def padded_columns(source_ref, room_ref, semaphore):
-    columns = source_ref.shape[-1]
-    copy = pltpu.make_async_copy(source_ref, room_ref.at[:, :, TILE : TILE + columns], semaphore)
-    copy.start()
-    blank = jnp.zeros(room_ref.shape[:2] + (TILE,), F32)
-    room_ref[:, :, :TILE] = blank
-    room_ref[:, :, TILE + columns :] = blank
-    return copy
-
-
-def block_of(room_ref, part, block):
-    start = pl.multiple_of(block * BLOCK, TILE)
-    return room_ref[part, :, pl.ds(start, FRAME0)][:, TILE // 2 : TILE // 2 + FRAME1]
-
-
-def pack_phase(where_ref, phase_ref, border_ref, core_ref, own_ref, room_ref, semaphore):
+def block_tile(ref, part, block, index):
+    columns = ref.shape[-1]
+    start = jnp.clip(block * BLOCK + index * TILE, 0, columns - TILE)
+    tile = ref[part, :, pl.ds(pl.multiple_of(start, TILE), TILE)]
+    if index < 0:
+        return jnp.where(block == 0, 0.0, tile)
+    if index * TILE >= BLOCK:
+        return jnp.where(block == GROUP - 1, 0.0, tile)
+    return tile
+
+
+def phase_block(ref, part, block):
+    tiles = [block_tile(ref, part, block, index) for index in range(-1, BLOCK // TILE + 1)]
+    return jnp.concatenate(tiles, axis=1)[:, TILE // 2 : TILE // 2 + FRAME1]
+
+
+def pack(where_ref, tilts_ref, phase_hbm, measured_hbm, border_ref, core_ref, own_ref, *refs):
+    block_refs, (phase_ref, plane_ref, semaphores) = refs[:GROUP], refs[GROUP:]
+    copies = []
+    for source, room in ((phase_hbm, phase_ref), (measured_hbm.at[0], plane_ref)):
+        for part in range(2):
+            copies.append(pltpu.make_async_copy(source.at[part], room.at[part], semaphores.at[len(copies)]))
+            copies[-1].start()
+    copies[0].wait()
+    copies[1].wait()
     even = where_ref[1] == 0
-    padded_columns(phase_ref, room_ref, semaphore).wait()
     low, high = slice(0, REACH), slice(ROWS - REACH, ROWS)
-    border_ref[:ROWS] = block_of(room_ref, 0, where_ref[3])
-    slice1 = block_of(room_ref, 1, where_ref[3])
+    border_ref[:ROWS] = phase_block(phase_ref, 0, where_ref[3])
+    slice1 = phase_block(phase_ref, 1, where_ref[3])
     border_ref[ROWS:] = jnp.where(even, slice1[low], slice1[high])
-    own_ref[0] = block_of(room_ref, 0, where_ref[2])
-    own_ref[1] = block_of(room_ref, 1, where_ref[2])
+    own_ref[0] = phase_block(phase_ref, 0, where_ref[2])
+    own_ref[1] = phase_block(phase_ref, 1, where_ref[2])
     core_ref[:ROWS] = own_ref[0]
     core_ref[ROWS:] = jnp.where(even, own_ref[1, high], own_ref[1, low])
-
-
-def pack_measured(where_ref, tilts_ref, measured_ref, after_ref, *refs):
-    block_refs, room_ref, semaphore = refs[:GROUP], refs[GROUP], refs[GROUP + 1]
-    padded_columns(measured_ref.at[0], room_ref, semaphore).wait()
     lane = lax.broadcasted_iota(jnp.int32, (ROWS, TILE), 1)
     tilts = jnp.where(lane[:8] == 0, tilts_ref[0, 0], tilts_ref[0, 1])
+    copies[2].wait()
+    copies[3].wait()
     for shift, ref in enumerate(block_refs):
-        start = (where_ref[2] ^ shift) * BLOCK
-
-        def tile(part, index):
-            return room_ref[part, :, pl.ds(pl.multiple_of(start + index * TILE, TILE), TILE)]
-
+        block = where_ref[2] ^ shift
         for part in range(2):
             for j in range(BLOCK // TILE):
-                ref[pl.ds((part * (BLOCK // TILE) + j) * ROWS, ROWS)] = tile(part, 1 + j)
+                ref[pl.ds((part * (BLOCK // TILE) + j) * ROWS, ROWS)] = block_tile(plane_ref, part, block, j)
         sides = [
-            pltpu.roll(tile(part, index), SIDE + 2 * SIDE * part, 1)
+            pltpu.roll(block_tile(plane_ref, part, block, index), SIDE + 2 * SIDE * part, 1)
             for part in range(2)
-            for index in (0, 1 + BLOCK // TILE)
+            for index in (-1, BLOCK // TILE)
         ]
         left, right = jnp.where(lane < SIDE, sides[0], sides[1]), jnp.where(lane < 3 * SIDE, sides[2], sides[3])
         ref[pl.ds(SIDES_AT, ROWS)] = jnp.where(lane < 2 * SIDE, left, right)
@@ -317,17 +319,17 @@
         out_ref[j, ROWS + REACH :] = own_ref[j, ROWS + REACH :] + above[ROWS:, tile]
 
 
-def call(kernel, shapes, scalars, arrays, flops, scratch=()):
+def call(kernel, shapes, scalars, arrays, flops, scratch=(), space=pltpu.VMEM, limit=VMEM_LIMIT):
     moved = sum(a.size * a.dtype.itemsize for a in arrays)
     moved += sum(int(s.size) * s.dtype.itemsize for s in shapes)
     return pl.pallas_call(
         kernel,
         out_shape=shapes,
         in_specs=[pl.BlockSpec(memory_space=pltpu.SMEM)] * len(scalars)
-        + [pl.BlockSpec(memory_space=pltpu.VMEM)] * len(arrays),
+        + [pl.BlockSpec(memory_space=space)] * len(arrays),
         out_specs=[pl.BlockSpec(memory_space=pltpu.VMEM)] * len(shapes),
         scratch_shapes=list(scratch),
-        compiler_params=pltpu.CompilerParams(vmem_limit_bytes=VMEM_LIMIT),
+        compiler_params=pltpu.CompilerParams(vmem_limit_bytes=limit),
         cost_estimate=pl.CostEstimate(flops=flops, bytes_accessed=moved, transcendentals=0),
     )(*scalars, *arrays)
 
@@ -360,20 +362,20 @@
         return [(g * along + i, (g ^ shift) * along + i) for g in range(GROUP) for i in range(along)]
 
     struct = jax.ShapeDtypeStruct
-    room = [pltpu.VMEM((2, ROWS, columns + 2 * TILE), F32), pltpu.SemaphoreType.DMA]
-    to_border, to_core, own_phase = call(
-        pack_phase,
-        [struct((ROWS + REACH, FRAME1), F32)] * 2 + [struct((2, ROWS, FRAME1), F32)],
-        [where],
-        [phase_delay],
+    to_border, to_core, own_phase, *blocks = call(
+        pack,
+        [struct((ROWS + REACH, FRAME1), F32)] * 2
+        + [struct((2, ROWS, FRAME1), F32)]
+        + [struct((MESSAGE, TILE), F32)] * GROUP,
+        [where, tilts],
+        [phase_delay, measured],
         0,
-        room,
+        [pltpu.VMEM((2, ROWS, columns), F32)] * 2 + [pltpu.SemaphoreType.DMA((4,))],
+        pltpu.HBM,
+        PACK_LIMIT,
     )
     beside = lax.ppermute(to_core, "space", in_chip)
     across = lax.ppermute(to_border, ("space", "angle"), over_border_nearest)
-    blocks = call(
-        pack_measured, [struct((MESSAGE, TILE), F32)] * GROUP, [where, tilts], [measured, own_phase], 0, room
-    )
     near, block1, block2, block3 = [blocks[0]] + [
         lax.ppermute(blocks[shift], "angle", swapped(shift)) for shift in range(1, GROUP)
     ]

time: 60 us -> 59.3 us (0.988)
  local copies, waits for them, and re-layouts: 1.74 us -> 0.58 us
    unnamed x8 -> x4, local copies, waits for them, and re-layouts: 1.74 us -> 0.58 us
    pallas_call x6 -> x5, Pallas kernels: 14.5 us -> 15 us  [call(): pl.pallas_call(kernel, out_shape=shapes, in_specs=[pl.BlockSpec(memory_sp...]
where the time goes in v11:
time: 59.3 us; the launch traced here: 58.9 us
  starting transfers between devices  28.2 us (48%)
  Pallas kernels  15 us (25%)
  blocking collectives  8.64 us (15%)
  waiting for transfers between devices  5.69 us (10%)
  other arithmetic  0.7 us (1%)
    pallas_call x5, Pallas kernels, call(): pl.pallas_call(kernel, out_shape=shapes, in_specs=[pl.BlockSpec(memory_sp...  15 us
    ppermute x3, starting transfers between devices, body(): lax.ppermute(blocks[shift], 'angle', swapped(shift))  12.9 us
    all_to_all x1, blocking collectives, body(): tiles = lax.all_to_all(tiles, 'angle', 0, 0, axis_index_groups=beside_x)  8.64 us
    ppermute x1, starting transfers between devices, body(): across = lax.ppermute(to_border, ('space', 'angle'), over_border_nearest)  7.07 us
    ppermute x1, waiting for transfers between devices, body(): across = lax.ppermute(to_border, 'space', over_border)  5.67 us
    ppermute x1, starting transfers between devices, body(): across = lax.ppermute(to_border, 'space', over_border)  4.35 us
    ppermute x2, starting transfers between devices, body(): beside = lax.ppermute(to_core, 'space', in_chip)  3.84 us
  transfers between devices with their start and end apart: 7, of which 1 were waited for; matrix products, arithmetic and copies ran while one was open for 0% of the time, Pallas kernels for 12%

profile of v11, /device:TPU:57, one launch (start us, length us, event | category | flops | bytes accessed | tf_op | source)
XLA Modules:
  0.0 58.9 jit_solution(18388550628882844312)
XLA Ops:
  0.0 0.1 pad_add_fusion.where_ref
  0.1 0.6 copy-done.1
  0.7 2.0 %shard_map.46 = (f32[48,640]{1,0:T(8,128)S(1)}, f32[48,640]{1,0:T(8,128)S(1)}, f32[2,32,640]{2,1,0:T(8,128)S(1)}, f32[296,128]{1,0:T(8,128)S(1)}, f32[296,128]{1...) custom-call(s32[4]{0:T(128)S(1)} %pad_add_fusion.where_ref, f32[1,2]{1,0:T(1,128)S(1)} %copy-done.1, ...), custom_call_target="tpu_custom_call" | custom-call | bytes 2064384 | tf_op jit(solution)/shard_map/pallas_call | solution.py:325
  2.6 5.8 %collective-permute-start.4 = (f32[296,128]{1,0:T(8,128)S(1)}, f32[296,128]{1,0:T(8,128)S(1)}, u32[]{:S(2)}, u32[]{:S(2)}) collective-permute-start(f32[296,128]{1,0:T(8,128)S(1)} %get-tuple-element.32), channel_id=1, source_target_pairs={{0,8},{1,9},{2,10},{3,11},{4,12},{5,13},{6,14},{7,15},{8,0},{9,1},... | collective-permute-start | bytes 454664 | tf_op jit(solution)/shard_map/ppermute | solution.py:380
  8.4 7.1 %collective-permute-start.2 = (f32[48,640]{1,0:T(8,128)S(1)}, f32[48,640]{1,0:T(8,128)S(1)}, u32[]{:S(2)}, u32[]{:S(2)}) collective-permute-start(f32[48,640]{1,0:T(8,128)S(1)} %get-tuple-element.27), channel_id=1, source_target_pairs={{16,32},{17,33},{18,34},{19,35},{20,36},{21,37},{22,38},{23,39},{2... | collective-permute-start | bytes 368648 | tf_op jit(solution)/shard_map/ppermute | solution.py:378
  15.5 1.9 %collective-permute-start.3 = (f32[48,640]{1,0:T(8,128)S(1)}, f32[48,640]{1,0:T(8,128)S(1)}, u32[]{:S(2)}, u32[]{:S(2)}) collective-permute-start(f32[48,640]{1,0:T(8,128)S(1)} %get-tuple-element.28), channel_id=1, source_target_pairs={{0,16},{32,48},{64,80},{96,112},{128,144},{160,176},{192,208},{224... | collective-permute-start | bytes 368648 | tf_op jit(solution)/shard_map/ppermute | solution.py:377
  17.4 0.0 copy-start
  17.5 4.0 %collective-permute-start = (f32[296,128]{1,0:T(8,128)S(1)}, f32[296,128]{1,0:T(8,128)S(1)}, u32[]{:S(2)}, u32[]{:S(2)}) collective-permute-start(f32[296,128]{1,0:T(8,128)S(1)} %get-tuple-element.25), channel_id=1, source_target_pairs={{0,12},{1,13},{2,14},{3,15},{4,8},{5,9},{6,10},{7,11},{8,4},{9,5},... | collective-permute-start | bytes 454664 | tf_op jit(solution)/shard_map/ppermute | solution.py:380
  21.5 3.1 %collective-permute-start.1 = (f32[296,128]{1,0:T(8,128)S(1)}, f32[296,128]{1,0:T(8,128)S(1)}, u32[]{:S(2)}, u32[]{:S(2)}) collective-permute-start(f32[296,128]{1,0:T(8,128)S(1)} %get-tuple-element.26), channel_id=1, source_target_pairs={{0,4},{1,5},{2,6},{3,7},{4,0},{5,1},{6,2},{7,3},{8,12},{9,13},{10,... | collective-permute-start | bytes 454664 | tf_op jit(solution)/shard_map/ppermute | solution.py:380
  24.6 1.4 %shard_map.47 = (f32[2,2,32,640]{3,2,1,0:T(8,128)S(1)}, bf16[256,192]{1,0:T(8,128)(2,1)S(1)}, bf16[128,256]{1,0:T(8,128)(2,1)S(1)}, bf16[256,128]{1,0:T(8,128)(2...) custom-call(s32[4]{0:T(128)S(1)} %pad_add_fusion.where_ref, f32[2,2,33]{2,1,0:T(2,128)S(1)} %copy-done, ...), custom_call_target="tpu_custom_call" | custom-call | flops 10000000 | bytes 1966080 | tf_op jit(solution)/shard_map/pallas_call | solution.py:325
  26.0 0.0 collective-permute-done.2.across_ref
  26.0 0.0 collective-permute-done.3.beside_ref
  26.0 0.0 collective-permute-done.4.far_ref
  26.0 5.6 %shard_map.48 = (f32[2,96,768]{2,1,0:T(8,128)S(1)}, f32[2,64,640]{2,1,0:T(8,128)S(1)}, f32[96,512]{1,0:T(8,128)S(1)}, f32[64,640]{1,0:T(8,128)S(1)}) custom-call(s32[4]{0:T(128)S(1)} %pad_add_fusion.where_ref, f32[48,640]{1,0:T(8,128)S(1)} %collective-permute-done.2.across_ref, f32[48,640]{1,0:T(8,128)S(1)} %collective-permute-done.3.beside_ref, ...), custom_call_target="tpu_custom_call" | custom-call | flops 800000000 | bytes 3629056 | tf_op jit(solution)/shard_map/pallas_call | solution.py:325
  31.7 0.0 collective-permute-done.near_ref
  31.7 0.0 collective-permute-done.1.far_ref
  31.7 5.4 %shard_map.49 = (f32[4,64,128]{2,1,0:T(8,128)S(1)}, f32[48,512]{1,0:T(8,128)S(1)}, f32[48,512]{1,0:T(8,128)S(1)}) custom-call(s32[4]{0:T(128)S(1)} %pad_add_fusion.where_ref, f32[296,128]{1,0:T(8,128)S(1)} %collective-permute-done.near_ref, f32[296,128]{1,0:T(8,128)S(1)} %collective-permute-done.1.far_ref, f32[96,512]{1,0:T(8,128)S(1)} %get-tuple-element.38.total0_ref, ...), custom_call_target="tpu_custom_call" | custom-call | flops 4000000000 | bytes 3383296 | tf_op jit(solution)/shard_map/pallas_call | solution.py:325
  37.1 4.3 %collective-permute-start.5 = (f32[48,512]{1,0:T(8,128)S(1)}, f32[48,512]{1,0:T(8,128)S(1)}, u32[]{:S(2)}, u32[]{:S(2)}) collective-permute-start(f32[48,512]{1,0:T(8,128)S(1)} %get-tuple-element.43), channel_id=1, source_target_pairs={{16,32},{48,64},{80,96},{112,128},{144,160},{176,192},{208,224},{2... | collective-permute-start | bytes 294920 | tf_op jit(solution)/shard_map/ppermute | solution.py:413
  41.5 1.9 %collective-permute-start.6 = (f32[48,512]{1,0:T(8,128)S(1)}, f32[48,512]{1,0:T(8,128)S(1)}, u32[]{:S(2)}, u32[]{:S(2)}) collective-permute-start(f32[48,512]{1,0:T(8,128)S(1)} %get-tuple-element.44), channel_id=1, source_target_pairs={{0,16},{32,48},{64,80},{96,112},{128,144},{160,176},{192,208},{224... | collective-permute-start | bytes 294920 | tf_op jit(solution)/shard_map/ppermute | solution.py:412
  43.4 5.7 %collective-permute-done.5.across_ref = f32[48,512]{1,0:T(8,128)S(1)} collective-permute-done((f32[48,512]{1,0:T(8,128)S(1)}, f32[48,512]{1,0:T(8,128)S(1)}, u32[]{:S(2)}, u32[]{:S(2)}) %collective-permute-start.5) | collective-permute-done | bytes 98336 | tf_op jit(solution)/shard_map/ppermute | solution.py:413
  49.1 0.0 collective-permute-done.6.beside_ref
  49.1 0.6 shard_map.50
  49.7 8.6 %all_to_all.5 = f32[4,64,128]{2,1,0:T(8,128)S(1)} all-to-all(f32[4,64,128]{2,1,0:T(8,128)S(1)} %shard_map.50), channel_id=1, replica_groups={{0,1,2,3},{4,5,6,7},{8,9,10,11},{12,13,14,15},{16,17,18,19},{20,21,22,2..., dimensions={0} | all-to-all | bytes 262144 | tf_op jit(solution)/shard_map/all_to_all | solution.py:416
  58.3 0.6 %reduce_sum.9 = f32[64,128]{1,0:T(8,128)} reduce(f32[4,64,128]{2,1,0:T(8,128)S(1)} %all_to_all.5, f32[]{:T(128)} %constant.34.clone.1), dimensions={0}, to_apply=%region_0.1 | reduce | flops 24576 | bytes 163844 | tf_op jit(solution)/shard_map/reduce_sum | solution.py:417
  (2 shorter events, 0.0 us)
Async XLA Ops:
  0.0 0.7 %copy-start.1 = (f32[1,2]{1,0:T(1,128)S(1)}, f32[1,2]{1,0:T(1,128)}, u32[]{:S(2)}) copy-start(f32[1,2]{1,0:T(1,128)} %tilts_ref.1) | copy-start | bytes 28
  2.6 23.4 %collective-permute-start.4 = (f32[296,128]{1,0:T(8,128)S(1)}, f32[296,128]{1,0:T(8,128)S(1)}, u32[]{:S(2)}, u32[]{:S(2)}) collective-permute-start(f32[296,128]{1,0:T(8,128)S(1)} %get-tuple-element.32), channel_id=1, source_target_pairs={{0,8},{1,9},{2,10},{3,11},{4,12},{5,13},{6,14},{7,15},{8,0},{9,1},... | collective-permute-start | bytes 454664 | tf_op jit(solution)/shard_map/ppermute | solution.py:380
  8.4 17.6 %collective-permute-start.2 = (f32[48,640]{1,0:T(8,128)S(1)}, f32[48,640]{1,0:T(8,128)S(1)}, u32[]{:S(2)}, u32[]{:S(2)}) collective-permute-start(f32[48,640]{1,0:T(8,128)S(1)} %get-tuple-element.27), channel_id=1, source_target_pairs={{16,32},{17,33},{18,34},{19,35},{20,36},{21,37},{22,38},{23,39},{2... | collective-permute-start | bytes 368648 | tf_op jit(solution)/shard_map/ppermute | solution.py:378
  15.5 10.5 %collective-permute-start.3 = (f32[48,640]{1,0:T(8,128)S(1)}, f32[48,640]{1,0:T(8,128)S(1)}, u32[]{:S(2)}, u32[]{:S(2)}) collective-permute-start(f32[48,640]{1,0:T(8,128)S(1)} %get-tuple-element.28), channel_id=1, source_target_pairs={{0,16},{32,48},{64,80},{96,112},{128,144},{160,176},{192,208},{224... | collective-permute-start | bytes 368648 | tf_op jit(solution)/shard_map/ppermute | solution.py:377
  17.4 7.1 %copy-start = (f32[2,2,33]{2,1,0:T(2,128)S(1)}, f32[2,2,33]{2,1,0:T(2,128)}, u32[]{:S(2)}) copy-start(f32[2,2,33]{2,1,0:T(2,128)} %taps_ref.1) | copy-start | bytes 1588
  17.5 14.2 %collective-permute-start = (f32[296,128]{1,0:T(8,128)S(1)}, f32[296,128]{1,0:T(8,128)S(1)}, u32[]{:S(2)}, u32[]{:S(2)}) collective-permute-start(f32[296,128]{1,0:T(8,128)S(1)} %get-tuple-element.25), channel_id=1, source_target_pairs={{0,12},{1,13},{2,14},{3,15},{4,8},{5,9},{6,10},{7,11},{8,4},{9,5},... | collective-permute-start | bytes 454664 | tf_op jit(solution)/shard_map/ppermute | solution.py:380
  21.5 10.2 %collective-permute-start.1 = (f32[296,128]{1,0:T(8,128)S(1)}, f32[296,128]{1,0:T(8,128)S(1)}, u32[]{:S(2)}, u32[]{:S(2)}) collective-permute-start(f32[296,128]{1,0:T(8,128)S(1)} %get-tuple-element.26), channel_id=1, source_target_pairs={{0,4},{1,5},{2,6},{3,7},{4,0},{5,1},{6,2},{7,3},{8,12},{9,13},{10,... | collective-permute-start | bytes 454664 | tf_op jit(solution)/shard_map/ppermute | solution.py:380
  37.1 12.0 %collective-permute-start.5 = (f32[48,512]{1,0:T(8,128)S(1)}, f32[48,512]{1,0:T(8,128)S(1)}, u32[]{:S(2)}, u32[]{:S(2)}) collective-permute-start(f32[48,512]{1,0:T(8,128)S(1)} %get-tuple-element.43), channel_id=1, source_target_pairs={{16,32},{48,64},{80,96},{112,128},{144,160},{176,192},{208,224},{2... | collective-permute-start | bytes 294920 | tf_op jit(solution)/shard_map/ppermute | solution.py:413
  41.5 7.6 %collective-permute-start.6 = (f32[48,512]{1,0:T(8,128)S(1)}, f32[48,512]{1,0:T(8,128)S(1)}, u32[]{:S(2)}, u32[]{:S(2)}) collective-permute-start(f32[48,512]{1,0:T(8,128)S(1)} %get-tuple-element.44), channel_id=1, source_target_pairs={{0,16},{32,48},{64,80},{96,112},{128,144},{160,176},{192,208},{224... | collective-permute-start | bytes 294920 | tf_op jit(solution)/shard_map/ppermute | solution.py:412

commit v12 on v11

--- a/solution.py
+++ b/solution.py
@@ -127,8 +127,12 @@
 
 
 def column_pass(fields, band_ref, index, tiles, first):
-    rows = fields[0][0].shape[0]
-    have = fields[0][0].shape[1] // TILE
+    return [column_pass_of(field, band_ref, index, tiles, first) for field in fields]
+
+
+def column_pass_of(field, band_ref, index, tiles, first):
+    rows = field[0].shape[0]
+    have = field[0].shape[1] // TILE
     blank = jnp.zeros((rows, TILE), BF16)
 
     def stacked(parts):
@@ -137,28 +141,22 @@
 
         return jnp.concatenate(
             [
-                jnp.concatenate([tile(part, first + j + i) for part in field for i in range(2)], axis=1)
-                for field in parts
+                jnp.concatenate([tile(part, first + j + i) for part in parts for i in range(2)], axis=1)
                 for j in range(tiles)
             ],
             axis=0,
         )
 
-    levels = [[split(part) for part in field] for field in fields]
-    high = stacked([[part[0] for part in field] for field in levels])
-    low = stacked([[part[1] for part in field] for field in levels])
+    levels = [split(part) for part in field]
+    high = stacked([level[0] for level in levels])
+    low = stacked([level[1] for level in levels])
     band_high = band_ref[index, 0]
     out = matmul(high, band_high) + (matmul(low, band_high) + matmul(high, band_ref[index, 1]))
-    results = []
-    for i in range(len(fields)):
-        pieces = [out[(i * tiles + j) * rows : (i * tiles + j + 1) * rows] for j in range(tiles)]
-        results.append(
-            (
-                jnp.concatenate([p[:, :TILE] for p in pieces], axis=1),
-                jnp.concatenate([p[:, TILE:] for p in pieces], axis=1),
-            )
-        )
-    return results
+    pieces = [out[j * rows : (j + 1) * rows] for j in range(tiles)]
+    return (
+        jnp.concatenate([piece[:, :TILE] for piece in pieces], axis=1),
+        jnp.concatenate([piece[:, TILE:] for piece in pieces], axis=1),
+    )
 
 
 def neighbours(even, across, beside):

time: 59.3 us -> 56.6 us (0.954)
  Pallas kernels: 15 us -> 12.3 us
  starting transfers between devices: 28.2 us -> 29.5 us
  waiting for transfers between devices: 5.69 us -> 4.4 us
    pallas_call x5, Pallas kernels: 15 us -> 12.3 us  [call(): pl.pallas_call(kernel, out_shape=shapes, in_specs=[pl.BlockSpec(memory_sp...]
    ppermute x1, starting transfers between devices: 4.35 us -> 5.66 us  [body(): across = lax.ppermute(to_border, 'space', over_border)]
    ppermute x1, waiting for transfers between devices: 5.67 us -> 4.38 us  [body(): across = lax.ppermute(to_border, 'space', over_border)]
  transfers between devices with their start and end apart: 7 -> 7, of which waited for: 1 -> 1; matrix products, arithmetic and copies ran while one was open for 0% -> 0% of each run, Pallas kernels for 12% -> 10%
where the time goes in v12:
time: 56.6 us; the launch traced here: 56.3 us
  starting transfers between devices  29.5 us (52%)
  Pallas kernels  12.3 us (22%)
  blocking collectives  8.63 us (15%)
  waiting for transfers between devices  4.4 us (8%)
  other arithmetic  0.7 us (1%)
  local copies, waits for them, and re-layouts  0.58 us (1%)
    ppermute x3, starting transfers between devices, body(): lax.ppermute(blocks[shift], 'angle', swapped(shift))  12.9 us
    pallas_call x5, Pallas kernels, call(): pl.pallas_call(kernel, out_shape=shapes, in_specs=[pl.BlockSpec(memory_sp...  12.3 us
    all_to_all x1, blocking collectives, body(): tiles = lax.all_to_all(tiles, 'angle', 0, 0, axis_index_groups=beside_x)  8.63 us
    ppermute x1, starting transfers between devices, body(): across = lax.ppermute(to_border, ('space', 'angle'), over_border_nearest)  7.07 us
    ppermute x1, starting transfers between devices, body(): across = lax.ppermute(to_border, 'space', over_border)  5.66 us
    ppermute x1, waiting for transfers between devices, body(): across = lax.ppermute(to_border, 'space', over_border)  4.38 us
    ppermute x2, starting transfers between devices, body(): beside = lax.ppermute(to_core, 'space', in_chip)  3.84 us
  transfers between devices with their start and end apart: 7, of which 1 were waited for; matrix products, arithmetic and copies ran while one was open for 0% of the time, Pallas kernels for 10%

profile of v12, /device:TPU:57, one launch (start us, length us, event | category | flops | bytes accessed | tf_op | source)
XLA Modules:
  0.0 56.3 jit_solution(13150634486694990442)
XLA Ops:
  0.0 0.1 pad_add_fusion.where_ref
  0.1 0.6 %copy-done.1 = f32[1,2]{1,0:T(1,128)S(1)} copy-done((f32[1,2]{1,0:T(1,128)S(1)}, f32[1,2]{1,0:T(1,128)}, u32[]{:S(2)}) %copy-start.1) | copy-done | bytes 32
  0.7 2.0 %shard_map.46 = (f32[48,640]{1,0:T(8,128)S(1)}, f32[48,640]{1,0:T(8,128)S(1)}, f32[2,32,640]{2,1,0:T(8,128)S(1)}, f32[296,128]{1,0:T(8,128)S(1)}, f32[296,128]{1...) custom-call(s32[4]{0:T(128)S(1)} %pad_add_fusion.where_ref, f32[1,2]{1,0:T(1,128)S(1)} %copy-done.1, ...), custom_call_target="tpu_custom_call" | custom-call | bytes 2064384 | tf_op jit(solution)/shard_map/pallas_call | solution.py:323
  2.6 5.8 %collective-permute-start.4 = (f32[296,128]{1,0:T(8,128)S(1)}, f32[296,128]{1,0:T(8,128)S(1)}, u32[]{:S(2)}, u32[]{:S(2)}) collective-permute-start(f32[296,128]{1,0:T(8,128)S(1)} %get-tuple-element.32), channel_id=1, source_target_pairs={{0,8},{1,9},{2,10},{3,11},{4,12},{5,13},{6,14},{7,15},{8,0},{9,1},... | collective-permute-start | bytes 454664 | tf_op jit(solution)/shard_map/ppermute | solution.py:378
  8.4 7.1 %collective-permute-start.2 = (f32[48,640]{1,0:T(8,128)S(1)}, f32[48,640]{1,0:T(8,128)S(1)}, u32[]{:S(2)}, u32[]{:S(2)}) collective-permute-start(f32[48,640]{1,0:T(8,128)S(1)} %get-tuple-element.27), channel_id=1, source_target_pairs={{16,32},{17,33},{18,34},{19,35},{20,36},{21,37},{22,38},{23,39},{2... | collective-permute-start | bytes 368648 | tf_op jit(solution)/shard_map/ppermute | solution.py:376
  15.5 1.9 %collective-permute-start.3 = (f32[48,640]{1,0:T(8,128)S(1)}, f32[48,640]{1,0:T(8,128)S(1)}, u32[]{:S(2)}, u32[]{:S(2)}) collective-permute-start(f32[48,640]{1,0:T(8,128)S(1)} %get-tuple-element.28), channel_id=1, source_target_pairs={{0,16},{32,48},{64,80},{96,112},{128,144},{160,176},{192,208},{224... | collective-permute-start | bytes 368648 | tf_op jit(solution)/shard_map/ppermute | solution.py:375
  17.4 0.0 copy-start
  17.5 4.0 %collective-permute-start = (f32[296,128]{1,0:T(8,128)S(1)}, f32[296,128]{1,0:T(8,128)S(1)}, u32[]{:S(2)}, u32[]{:S(2)}) collective-permute-start(f32[296,128]{1,0:T(8,128)S(1)} %get-tuple-element.25), channel_id=1, source_target_pairs={{0,12},{1,13},{2,14},{3,15},{4,8},{5,9},{6,10},{7,11},{8,4},{9,5},... | collective-permute-start | bytes 454664 | tf_op jit(solution)/shard_map/ppermute | solution.py:378
  21.5 3.1 %collective-permute-start.1 = (f32[296,128]{1,0:T(8,128)S(1)}, f32[296,128]{1,0:T(8,128)S(1)}, u32[]{:S(2)}, u32[]{:S(2)}) collective-permute-start(f32[296,128]{1,0:T(8,128)S(1)} %get-tuple-element.26), channel_id=1, source_target_pairs={{0,4},{1,5},{2,6},{3,7},{4,0},{5,1},{6,2},{7,3},{8,12},{9,13},{10,... | collective-permute-start | bytes 454664 | tf_op jit(solution)/shard_map/ppermute | solution.py:378
  24.6 1.4 %shard_map.47 = (f32[2,2,32,640]{3,2,1,0:T(8,128)S(1)}, bf16[256,192]{1,0:T(8,128)(2,1)S(1)}, bf16[128,256]{1,0:T(8,128)(2,1)S(1)}, bf16[256,128]{1,0:T(8,128)(2...) custom-call(s32[4]{0:T(128)S(1)} %pad_add_fusion.where_ref, f32[2,2,33]{2,1,0:T(2,128)S(1)} %copy-done, ...), custom_call_target="tpu_custom_call" | custom-call | flops 10000000 | bytes 1966080 | tf_op jit(solution)/shard_map/pallas_call | solution.py:323
  26.0 0.0 collective-permute-done.2.across_ref
  26.0 0.0 collective-permute-done.3.beside_ref
  26.0 0.0 collective-permute-done.4.far_ref
  26.0 4.3 %shard_map.48 = (f32[2,96,768]{2,1,0:T(8,128)S(1)}, f32[2,64,640]{2,1,0:T(8,128)S(1)}, f32[96,512]{1,0:T(8,128)S(1)}, f32[64,640]{1,0:T(8,128)S(1)}) custom-call(s32[4]{0:T(128)S(1)} %pad_add_fusion.where_ref, f32[48,640]{1,0:T(8,128)S(1)} %collective-permute-done.2.across_ref, f32[48,640]{1,0:T(8,128)S(1)} %collective-permute-done.3.beside_ref, ...), custom_call_target="tpu_custom_call" | custom-call | flops 800000000 | bytes 3629056 | tf_op jit(solution)/shard_map/pallas_call | solution.py:323
  30.4 0.0 collective-permute-done.near_ref
  30.4 0.0 collective-permute-done.1.far_ref
  30.4 4.1 %shard_map.49 = (f32[4,64,128]{2,1,0:T(8,128)S(1)}, f32[48,512]{1,0:T(8,128)S(1)}, f32[48,512]{1,0:T(8,128)S(1)}) custom-call(s32[4]{0:T(128)S(1)} %pad_add_fusion.where_ref, f32[296,128]{1,0:T(8,128)S(1)} %collective-permute-done.near_ref, f32[296,128]{1,0:T(8,128)S(1)} %collective-permute-done.1.far_ref, f32[96,512]{1,0:T(8,128)S(1)} %get-tuple-element.38.total0_ref, ...), custom_call_target="tpu_custom_call" | custom-call | flops 4000000000 | bytes 3383296 | tf_op jit(solution)/shard_map/pallas_call | solution.py:323
  34.5 5.7 %collective-permute-start.5 = (f32[48,512]{1,0:T(8,128)S(1)}, f32[48,512]{1,0:T(8,128)S(1)}, u32[]{:S(2)}, u32[]{:S(2)}) collective-permute-start(f32[48,512]{1,0:T(8,128)S(1)} %get-tuple-element.43), channel_id=1, source_target_pairs={{16,32},{48,64},{80,96},{112,128},{144,160},{176,192},{208,224},{2... | collective-permute-start | bytes 294920 | tf_op jit(solution)/shard_map/ppermute | solution.py:411
  40.1 1.9 %collective-permute-start.6 = (f32[48,512]{1,0:T(8,128)S(1)}, f32[48,512]{1,0:T(8,128)S(1)}, u32[]{:S(2)}, u32[]{:S(2)}) collective-permute-start(f32[48,512]{1,0:T(8,128)S(1)} %get-tuple-element.44), channel_id=1, source_target_pairs={{0,16},{32,48},{64,80},{96,112},{128,144},{160,176},{192,208},{224... | collective-permute-start | bytes 294920 | tf_op jit(solution)/shard_map/ppermute | solution.py:410
  42.1 4.4 %collective-permute-done.5.across_ref = f32[48,512]{1,0:T(8,128)S(1)} collective-permute-done((f32[48,512]{1,0:T(8,128)S(1)}, f32[48,512]{1,0:T(8,128)S(1)}, u32[]{:S(2)}, u32[]{:S(2)}) %collective-permute-start.5) | collective-permute-done | bytes 98336 | tf_op jit(solution)/shard_map/ppermute | solution.py:411
  46.4 0.0 collective-permute-done.6.beside_ref
  46.4 0.6 %shard_map.50 = f32[4,64,128]{2,1,0:T(8,128)S(1)} custom-call(s32[4]{0:T(128)S(1)} %pad_add_fusion.where_ref, f32[4,64,128]{2,1,0:T(8,128)S(1)} %get-tuple-element.42.own_ref, f32[48,512]{1,0:T(8,128)S(1)} %collective-permute-done.5.across_ref, f32[48,512]{1,0:T(8,128)S(1)} %collective-permute-done.6.beside_ref), custom_call_target="tpu_custom_call" | custom-call | bytes 458752 | tf_op jit(solution)/shard_map/pallas_call | solution.py:323
  47.0 8.6 %all_to_all.5 = f32[4,64,128]{2,1,0:T(8,128)S(1)} all-to-all(f32[4,64,128]{2,1,0:T(8,128)S(1)} %shard_map.50), channel_id=1, replica_groups={{0,1,2,3},{4,5,6,7},{8,9,10,11},{12,13,14,15},{16,17,18,19},{20,21,22,2..., dimensions={0} | all-to-all | bytes 262144 | tf_op jit(solution)/shard_map/all_to_all | solution.py:414
  55.7 0.6 %reduce_sum.9 = f32[64,128]{1,0:T(8,128)} reduce(f32[4,64,128]{2,1,0:T(8,128)S(1)} %all_to_all.5, f32[]{:T(128)} %constant.34.clone.1), dimensions={0}, to_apply=%region_0.1 | reduce | flops 24576 | bytes 163844 | tf_op jit(solution)/shard_map/reduce_sum | solution.py:415
  (2 shorter events, 0.0 us)
Async XLA Ops:
  0.0 0.7 %copy-start.1 = (f32[1,2]{1,0:T(1,128)S(1)}, f32[1,2]{1,0:T(1,128)}, u32[]{:S(2)}) copy-start(f32[1,2]{1,0:T(1,128)} %tilts_ref.1) | copy-start | bytes 28
  2.6 23.4 %collective-permute-start.4 = (f32[296,128]{1,0:T(8,128)S(1)}, f32[296,128]{1,0:T(8,128)S(1)}, u32[]{:S(2)}, u32[]{:S(2)}) collective-permute-start(f32[296,128]{1,0:T(8,128)S(1)} %get-tuple-element.32), channel_id=1, source_target_pairs={{0,8},{1,9},{2,10},{3,11},{4,12},{5,13},{6,14},{7,15},{8,0},{9,1},... | collective-permute-start | bytes 454664 | tf_op jit(solution)/shard_map/ppermute | solution.py:378
  8.4 17.6 %collective-permute-start.2 = (f32[48,640]{1,0:T(8,128)S(1)}, f32[48,640]{1,0:T(8,128)S(1)}, u32[]{:S(2)}, u32[]{:S(2)}) collective-permute-start(f32[48,640]{1,0:T(8,128)S(1)} %get-tuple-element.27), channel_id=1, source_target_pairs={{16,32},{17,33},{18,34},{19,35},{20,36},{21,37},{22,38},{23,39},{2... | collective-permute-start | bytes 368648 | tf_op jit(solution)/shard_map/ppermute | solution.py:376
  15.5 10.5 %collective-permute-start.3 = (f32[48,640]{1,0:T(8,128)S(1)}, f32[48,640]{1,0:T(8,128)S(1)}, u32[]{:S(2)}, u32[]{:S(2)}) collective-permute-start(f32[48,640]{1,0:T(8,128)S(1)} %get-tuple-element.28), channel_id=1, source_target_pairs={{0,16},{32,48},{64,80},{96,112},{128,144},{160,176},{192,208},{224... | collective-permute-start | bytes 368648 | tf_op jit(solution)/shard_map/ppermute | solution.py:375
  17.4 7.1 %copy-start = (f32[2,2,33]{2,1,0:T(2,128)S(1)}, f32[2,2,33]{2,1,0:T(2,128)}, u32[]{:S(2)}) copy-start(f32[2,2,33]{2,1,0:T(2,128)} %taps_ref.1) | copy-start | bytes 1588
  17.5 12.9 %collective-permute-start = (f32[296,128]{1,0:T(8,128)S(1)}, f32[296,128]{1,0:T(8,128)S(1)}, u32[]{:S(2)}, u32[]{:S(2)}) collective-permute-start(f32[296,128]{1,0:T(8,128)S(1)} %get-tuple-element.25), channel_id=1, source_target_pairs={{0,12},{1,13},{2,14},{3,15},{4,8},{5,9},{6,10},{7,11},{8,4},{9,5},... | collective-permute-start | bytes 454664 | tf_op jit(solution)/shard_map/ppermute | solution.py:378
  21.5 8.9 %collective-permute-start.1 = (f32[296,128]{1,0:T(8,128)S(1)}, f32[296,128]{1,0:T(8,128)S(1)}, u32[]{:S(2)}, u32[]{:S(2)}) collective-permute-start(f32[296,128]{1,0:T(8,128)S(1)} %get-tuple-element.26), channel_id=1, source_target_pairs={{0,4},{1,5},{2,6},{3,7},{4,0},{5,1},{6,2},{7,3},{8,12},{9,13},{10,... | collective-permute-start | bytes 454664 | tf_op jit(solution)/shard_map/ppermute | solution.py:378
  34.5 12.0 %collective-permute-start.5 = (f32[48,512]{1,0:T(8,128)S(1)}, f32[48,512]{1,0:T(8,128)S(1)}, u32[]{:S(2)}, u32[]{:S(2)}) collective-permute-start(f32[48,512]{1,0:T(8,128)S(1)} %get-tuple-element.43), channel_id=1, source_target_pairs={{16,32},{48,64},{80,96},{112,128},{144,160},{176,192},{208,224},{2... | collective-permute-start | bytes 294920 | tf_op jit(solution)/shard_map/ppermute | solution.py:411
  40.1 6.3 %collective-permute-start.6 = (f32[48,512]{1,0:T(8,128)S(1)}, f32[48,512]{1,0:T(8,128)S(1)}, u32[]{:S(2)}, u32[]{:S(2)}) collective-permute-start(f32[48,512]{1,0:T(8,128)S(1)} %get-tuple-element.44), channel_id=1, source_target_pairs={{0,16},{32,48},{64,80},{96,112},{128,144},{160,176},{192,208},{224... | collective-permute-start | bytes 294920 | tf_op jit(solution)/shard_map/ppermute | solution.py:410

commit v13 on v12

--- a/solution.py
+++ b/solution.py
@@ -396,7 +396,7 @@
         functools.partial(first_angles, total_rows=total_rows),
         [struct((2, WIDEST, FRAME0), F32), struct((2, WIDE, FRAME1), F32)] + totals,
         [where],
-        [across, beside, own, near, block2, *matrices],
+        [across, beside, own, near, block3, *matrices],
         800_000_000,
     )
     tiles_struct = struct((BLOCK // TILE, 2 * ROWS, TILE), F32)
@@ -404,7 +404,7 @@
         last_angles,
         [tiles_struct] + [struct((ROWS + REACH, BLOCK), F32)] * 2,
         [where],
-        [block3, block1, total0, total1, turn0, turn1, *matrices],
+        [block2, block1, total0, total1, turn0, turn1, *matrices],
         4_000_000_000,
     )
     beside = lax.ppermute(to_core, "space", in_chip)

time: 56.6 us -> 57 us (level)
    ppermute x1, starting transfers between devices: 7.07 us -> 5.26 us  [body(): across = lax.ppermute(to_border, ('space', 'angle'), over_border_nearest)]
    ppermute x3, starting transfers between devices: 12.9 us -> 14.7 us  [body(): lax.ppermute(blocks[shift], 'angle', swapped(shift))]
  transfers between devices with their start and end apart: 7 -> 7, of which waited for: 1 -> 2; matrix products, arithmetic and copies ran while one was open for 0% -> 0% of each run, Pallas kernels for 10% -> 10%
where the time goes in v13:
time: 57 us; the launch traced here: 56.6 us
  starting transfers between devices  29.6 us (52%)
  Pallas kernels  12.3 us (22%)
  blocking collectives  8.64 us (15%)
  waiting for transfers between devices  4.63 us (8%)
  other arithmetic  0.7 us (1%)
  local copies, waits for them, and re-layouts  0.58 us (1%)
    ppermute x3, starting transfers between devices, body(): lax.ppermute(blocks[shift], 'angle', swapped(shift))  14.7 us
    pallas_call x5, Pallas kernels, call(): pl.pallas_call(kernel, out_shape=shapes, in_specs=[pl.BlockSpec(memory_sp...  12.3 us
    all_to_all x1, blocking collectives, body(): tiles = lax.all_to_all(tiles, 'angle', 0, 0, axis_index_groups=beside_x)  8.64 us
    ppermute x1, starting transfers between devices, body(): across = lax.ppermute(to_border, 'space', over_border)  5.79 us
    ppermute x1, starting transfers between devices, body(): across = lax.ppermute(to_border, ('space', 'angle'), over_border_nearest)  5.26 us
    ppermute x1, waiting for transfers between devices, body(): across = lax.ppermute(to_border, 'space', over_border)  4.22 us
    ppermute x2, starting transfers between devices, body(): beside = lax.ppermute(to_core, 'space', in_chip)  3.84 us
  transfers between devices with their start and end apart: 7, of which 2 were waited for; matrix products, arithmetic and copies ran while one was open for 0% of the time, Pallas kernels for 10%

profile of v13, /device:TPU:57, one launch (start us, length us, event | category | flops | bytes accessed | tf_op | source)
XLA Modules:
  0.0 56.6 jit_solution(14152347330020678264)
XLA Ops:
  0.0 0.1 pad_add_fusion.where_ref
  0.1 0.6 %copy-done.1 = f32[1,2]{1,0:T(1,128)S(1)} copy-done((f32[1,2]{1,0:T(1,128)S(1)}, f32[1,2]{1,0:T(1,128)}, u32[]{:S(2)}) %copy-start.1) | copy-done | bytes 32
  0.7 2.0 %shard_map.46 = (f32[48,640]{1,0:T(8,128)S(1)}, f32[48,640]{1,0:T(8,128)S(1)}, f32[2,32,640]{2,1,0:T(8,128)S(1)}, f32[296,128]{1,0:T(8,128)S(1)}, f32[296,128]{1...) custom-call(s32[4]{0:T(128)S(1)} %pad_add_fusion.where_ref, f32[1,2]{1,0:T(1,128)S(1)} %copy-done.1, ...), custom_call_target="tpu_custom_call" | custom-call | bytes 2064384 | tf_op jit(solution)/shard_map/pallas_call | solution.py:323
  2.6 7.6 %collective-permute-start.4 = (f32[296,128]{1,0:T(8,128)S(1)}, f32[296,128]{1,0:T(8,128)S(1)}, u32[]{:S(2)}, u32[]{:S(2)}) collective-permute-start(f32[296,128]{1,0:T(8,128)S(1)} %get-tuple-element.32), channel_id=1, source_target_pairs={{0,12},{1,13},{2,14},{3,15},{4,8},{5,9},{6,10},{7,11},{8,4},{9,5},... | collective-permute-start | bytes 454664 | tf_op jit(solution)/shard_map/ppermute | solution.py:378
  10.2 5.3 %collective-permute-start.2 = (f32[48,640]{1,0:T(8,128)S(1)}, f32[48,640]{1,0:T(8,128)S(1)}, u32[]{:S(2)}, u32[]{:S(2)}) collective-permute-start(f32[48,640]{1,0:T(8,128)S(1)} %get-tuple-element.27), channel_id=1, source_target_pairs={{16,32},{17,33},{18,34},{19,35},{20,36},{21,37},{22,38},{23,39},{2... | collective-permute-start | bytes 368648 | tf_op jit(solution)/shard_map/ppermute | solution.py:376
  15.5 1.9 %collective-permute-start.3 = (f32[48,640]{1,0:T(8,128)S(1)}, f32[48,640]{1,0:T(8,128)S(1)}, u32[]{:S(2)}, u32[]{:S(2)}) collective-permute-start(f32[48,640]{1,0:T(8,128)S(1)} %get-tuple-element.28), channel_id=1, source_target_pairs={{0,16},{32,48},{64,80},{96,112},{128,144},{160,176},{192,208},{224... | collective-permute-start | bytes 368648 | tf_op jit(solution)/shard_map/ppermute | solution.py:375
  17.4 0.0 copy-start
  17.4 4.0 %collective-permute-start = (f32[296,128]{1,0:T(8,128)S(1)}, f32[296,128]{1,0:T(8,128)S(1)}, u32[]{:S(2)}, u32[]{:S(2)}) collective-permute-start(f32[296,128]{1,0:T(8,128)S(1)} %get-tuple-element.25), channel_id=1, source_target_pairs={{0,8},{1,9},{2,10},{3,11},{4,12},{5,13},{6,14},{7,15},{8,0},{9,1},... | collective-permute-start | bytes 454664 | tf_op jit(solution)/shard_map/ppermute | solution.py:378
  21.5 3.1 %collective-permute-start.1 = (f32[296,128]{1,0:T(8,128)S(1)}, f32[296,128]{1,0:T(8,128)S(1)}, u32[]{:S(2)}, u32[]{:S(2)}) collective-permute-start(f32[296,128]{1,0:T(8,128)S(1)} %get-tuple-element.26), channel_id=1, source_target_pairs={{0,4},{1,5},{2,6},{3,7},{4,0},{5,1},{6,2},{7,3},{8,12},{9,13},{10,... | collective-permute-start | bytes 454664 | tf_op jit(solution)/shard_map/ppermute | solution.py:378
  24.6 1.4 %shard_map.47 = (f32[2,2,32,640]{3,2,1,0:T(8,128)S(1)}, bf16[256,192]{1,0:T(8,128)(2,1)S(1)}, bf16[128,256]{1,0:T(8,128)(2,1)S(1)}, bf16[256,128]{1,0:T(8,128)(2...) custom-call(s32[4]{0:T(128)S(1)} %pad_add_fusion.where_ref, f32[2,2,33]{2,1,0:T(2,128)S(1)} %copy-done, ...), custom_call_target="tpu_custom_call" | custom-call | flops 10000000 | bytes 1966080 | tf_op jit(solution)/shard_map/pallas_call | solution.py:323
  26.0 0.0 collective-permute-done.2.across_ref
  26.0 0.0 collective-permute-done.3.beside_ref
  26.0 0.0 collective-permute-done.4.far_ref
  26.0 4.3 %shard_map.48 = (f32[2,96,768]{2,1,0:T(8,128)S(1)}, f32[2,64,640]{2,1,0:T(8,128)S(1)}, f32[96,512]{1,0:T(8,128)S(1)}, f32[64,640]{1,0:T(8,128)S(1)}) custom-call(s32[4]{0:T(128)S(1)} %pad_add_fusion.where_ref, f32[48,640]{1,0:T(8,128)S(1)} %collective-permute-done.2.across_ref, f32[48,640]{1,0:T(8,128)S(1)} %collective-permute-done.3.beside_ref, ...), custom_call_target="tpu_custom_call" | custom-call | flops 800000000 | bytes 3629056 | tf_op jit(solution)/shard_map/pallas_call | solution.py:323
  30.4 0.0 collective-permute-done.near_ref
  30.4 0.4 collective-permute-done.1.far_ref
  30.8 4.1 %shard_map.49 = (f32[4,64,128]{2,1,0:T(8,128)S(1)}, f32[48,512]{1,0:T(8,128)S(1)}, f32[48,512]{1,0:T(8,128)S(1)}) custom-call(s32[4]{0:T(128)S(1)} %pad_add_fusion.where_ref, f32[296,128]{1,0:T(8,128)S(1)} %collective-permute-done.near_ref, f32[296,128]{1,0:T(8,128)S(1)} %collective-permute-done.1.far_ref, f32[96,512]{1,0:T(8,128)S(1)} %get-tuple-element.38.total0_ref, ...), custom_call_target="tpu_custom_call" | custom-call | flops 4000000000 | bytes 3383296 | tf_op jit(solution)/shard_map/pallas_call | solution.py:323
  34.8 5.8 %collective-permute-start.5 = (f32[48,512]{1,0:T(8,128)S(1)}, f32[48,512]{1,0:T(8,128)S(1)}, u32[]{:S(2)}, u32[]{:S(2)}) collective-permute-start(f32[48,512]{1,0:T(8,128)S(1)} %get-tuple-element.43), channel_id=1, source_target_pairs={{16,32},{48,64},{80,96},{112,128},{144,160},{176,192},{208,224},{2... | collective-permute-start | bytes 294920 | tf_op jit(solution)/shard_map/ppermute | solution.py:411
  40.6 1.9 %collective-permute-start.6 = (f32[48,512]{1,0:T(8,128)S(1)}, f32[48,512]{1,0:T(8,128)S(1)}, u32[]{:S(2)}, u32[]{:S(2)}) collective-permute-start(f32[48,512]{1,0:T(8,128)S(1)} %get-tuple-element.44), channel_id=1, source_target_pairs={{0,16},{32,48},{64,80},{96,112},{128,144},{160,176},{192,208},{224... | collective-permute-start | bytes 294920 | tf_op jit(solution)/shard_map/ppermute | solution.py:410
  42.6 4.2 %collective-permute-done.5.across_ref = f32[48,512]{1,0:T(8,128)S(1)} collective-permute-done((f32[48,512]{1,0:T(8,128)S(1)}, f32[48,512]{1,0:T(8,128)S(1)}, u32[]{:S(2)}, u32[]{:S(2)}) %collective-permute-start.5) | collective-permute-done | bytes 98336 | tf_op jit(solution)/shard_map/ppermute | solution.py:411
  46.8 0.0 collective-permute-done.6.beside_ref
  46.8 0.6 %shard_map.50 = f32[4,64,128]{2,1,0:T(8,128)S(1)} custom-call(s32[4]{0:T(128)S(1)} %pad_add_fusion.where_ref, f32[4,64,128]{2,1,0:T(8,128)S(1)} %get-tuple-element.42.own_ref, f32[48,512]{1,0:T(8,128)S(1)} %collective-permute-done.5.across_ref, f32[48,512]{1,0:T(8,128)S(1)} %collective-permute-done.6.beside_ref), custom_call_target="tpu_custom_call" | custom-call | bytes 458752 | tf_op jit(solution)/shard_map/pallas_call | solution.py:323
  47.4 8.6 %all_to_all.5 = f32[4,64,128]{2,1,0:T(8,128)S(1)} all-to-all(f32[4,64,128]{2,1,0:T(8,128)S(1)} %shard_map.50), channel_id=1, replica_groups={{0,1,2,3},{4,5,6,7},{8,9,10,11},{12,13,14,15},{16,17,18,19},{20,21,22,2..., dimensions={0} | all-to-all | bytes 262144 | tf_op jit(solution)/shard_map/all_to_all | solution.py:414
  56.0 0.6 %reduce_sum.9 = f32[64,128]{1,0:T(8,128)} reduce(f32[4,64,128]{2,1,0:T(8,128)S(1)} %all_to_all.5, f32[]{:T(128)} %constant.34.clone.1), dimensions={0}, to_apply=%region_0.1 | reduce | flops 24576 | bytes 163844 | tf_op jit(solution)/shard_map/reduce_sum | solution.py:415
  (2 shorter events, 0.0 us)
Async XLA Ops:
  0.0 0.7 %copy-start.1 = (f32[1,2]{1,0:T(1,128)S(1)}, f32[1,2]{1,0:T(1,128)}, u32[]{:S(2)}) copy-start(f32[1,2]{1,0:T(1,128)} %tilts_ref.1) | copy-start | bytes 28
  2.6 23.4 %collective-permute-start.4 = (f32[296,128]{1,0:T(8,128)S(1)}, f32[296,128]{1,0:T(8,128)S(1)}, u32[]{:S(2)}, u32[]{:S(2)}) collective-permute-start(f32[296,128]{1,0:T(8,128)S(1)} %get-tuple-element.32), channel_id=1, source_target_pairs={{0,12},{1,13},{2,14},{3,15},{4,8},{5,9},{6,10},{7,11},{8,4},{9,5},... | collective-permute-start | bytes 454664 | tf_op jit(solution)/shard_map/ppermute | solution.py:378
  10.2 15.8 %collective-permute-start.2 = (f32[48,640]{1,0:T(8,128)S(1)}, f32[48,640]{1,0:T(8,128)S(1)}, u32[]{:S(2)}, u32[]{:S(2)}) collective-permute-start(f32[48,640]{1,0:T(8,128)S(1)} %get-tuple-element.27), channel_id=1, source_target_pairs={{16,32},{17,33},{18,34},{19,35},{20,36},{21,37},{22,38},{23,39},{2... | collective-permute-start | bytes 368648 | tf_op jit(solution)/shard_map/ppermute | solution.py:376
  15.5 10.5 %collective-permute-start.3 = (f32[48,640]{1,0:T(8,128)S(1)}, f32[48,640]{1,0:T(8,128)S(1)}, u32[]{:S(2)}, u32[]{:S(2)}) collective-permute-start(f32[48,640]{1,0:T(8,128)S(1)} %get-tuple-element.28), channel_id=1, source_target_pairs={{0,16},{32,48},{64,80},{96,112},{128,144},{160,176},{192,208},{224... | collective-permute-start | bytes 368648 | tf_op jit(solution)/shard_map/ppermute | solution.py:375
  17.4 7.1 %copy-start = (f32[2,2,33]{2,1,0:T(2,128)S(1)}, f32[2,2,33]{2,1,0:T(2,128)}, u32[]{:S(2)}) copy-start(f32[2,2,33]{2,1,0:T(2,128)} %taps_ref.1) | copy-start | bytes 1588
  17.4 12.9 %collective-permute-start = (f32[296,128]{1,0:T(8,128)S(1)}, f32[296,128]{1,0:T(8,128)S(1)}, u32[]{:S(2)}, u32[]{:S(2)}) collective-permute-start(f32[296,128]{1,0:T(8,128)S(1)} %get-tuple-element.25), channel_id=1, source_target_pairs={{0,8},{1,9},{2,10},{3,11},{4,12},{5,13},{6,14},{7,15},{8,0},{9,1},... | collective-permute-start | bytes 454664 | tf_op jit(solution)/shard_map/ppermute | solution.py:378
  21.5 9.3 %collective-permute-start.1 = (f32[296,128]{1,0:T(8,128)S(1)}, f32[296,128]{1,0:T(8,128)S(1)}, u32[]{:S(2)}, u32[]{:S(2)}) collective-permute-start(f32[296,128]{1,0:T(8,128)S(1)} %get-tuple-element.26), channel_id=1, source_target_pairs={{0,4},{1,5},{2,6},{3,7},{4,0},{5,1},{6,2},{7,3},{8,12},{9,13},{10,... | collective-permute-start | bytes 454664 | tf_op jit(solution)/shard_map/ppermute | solution.py:378
  34.8 12.0 %collective-permute-start.5 = (f32[48,512]{1,0:T(8,128)S(1)}, f32[48,512]{1,0:T(8,128)S(1)}, u32[]{:S(2)}, u32[]{:S(2)}) collective-permute-start(f32[48,512]{1,0:T(8,128)S(1)} %get-tuple-element.43), channel_id=1, source_target_pairs={{16,32},{48,64},{80,96},{112,128},{144,160},{176,192},{208,224},{2... | collective-permute-start | bytes 294920 | tf_op jit(solution)/shard_map/ppermute | solution.py:411
  40.6 6.2 %collective-permute-start.6 = (f32[48,512]{1,0:T(8,128)S(1)}, f32[48,512]{1,0:T(8,128)S(1)}, u32[]{:S(2)}, u32[]{:S(2)}) collective-permute-start(f32[48,512]{1,0:T(8,128)S(1)} %get-tuple-element.44), channel_id=1, source_target_pairs={{0,16},{32,48},{64,80},{96,112},{128,144},{160,176},{192,208},{224... | collective-permute-start | bytes 294920 | tf_op jit(solution)/shard_map/ppermute | solution.py:410
